TPU v7x, 128 devices: a whole 4x4x4 slice. The times are simulated.
128 devices in a mesh: rep: 8 (over y, z_lo), tp: 16 (over x, z_hi, core).
Axes of the slice: x: 4, y: 4, z: 4 (z_hi: 2, z_lo: 2; z = z_hi * 2 + z_lo), core: 2. Of those that a mesh axis runs over, the one named last changes fastest.
Arguments:
- token_hidden_rows: bfloat16 [4, 512, 8192], P(None, 'rep', 'tp'), may hold values from -5400 to 5400
- input_norm_gain: float32 [8192], replicated, may hold values from 0.1 to 1.9
- frozen_query: bfloat16 [8192, 8192], P(('rep', 'tp')), may hold values from -20 to 20
- frozen_key_value: bfloat16 [8192, 2048], P(('rep', 'tp')), may hold values from -20 to 20
- frozen_output: bfloat16 [8192, 8192], P(('rep', 'tp')), may hold values from -20 to 20
- query_down_factor: bfloat16 [8192, 32], P(('rep', 'tp')), may hold values from -0.0625 to 0.0625
- query_up_factor: bfloat16 [32, 8192], replicated, may hold values from -12 to 12
- key_value_down_factor: bfloat16 [8192, 32], P(('rep', 'tp')), may hold values from -0.0625 to 0.0625
- key_value_up_factor: bfloat16 [32, 2048], replicated, may hold values from -12 to 12
- output_down_factor: bfloat16 [8192, 32], P(('rep', 'tp')), may hold values from -0.0625 to 0.0625
- output_up_factor: bfloat16 [32, 8192], replicated, may hold values from -12 to 12
- query_column_scale: float32 [8192], replicated, may hold values from 1 to 4
- key_value_column_scale: float32 [2048], replicated, may hold values from 2 to 8
- output_column_scale: float32 [8192], replicated, may hold values from 2 to 8
- cached_key_rows: bfloat16 [512, 8, 1024, 128], P(('rep', 'tp')), may hold values from -1900 to 1900
- cached_value_rows: bfloat16 [512, 8, 1024, 128], P(('rep', 'tp')), may hold values from -6 to 6
- lengths: int32 [512], P(('rep', 'tp')), may hold values from 1 to 1024, as said below
Outputs:
- output: bfloat16 [4, 512, 8192], P(None, 'rep', 'tp')
Inputs may be any that keep to these rules, and one draw needn't show every extreme that they name: The first lengths[b] cache positions of sequence b are valid; in every draw some sequence holds all 1024.
All inputs are finite; a program needn't handle non-finite values.
Results may differ from a plain program's by a relative error of at most 0.0055.
The roundings to bfloat16 on the way count: a program that leaves them out, or rounds other values in their place, can miss the bound.
Values may be sent and summed in bfloat16 or wider, within the bound.
No kernel may reach another device: no remote copies, remote signals or barrier semaphores. Data moves between devices by JAX's collectives and lax.ppermute only.
A program may use at most 128 MiB of HBM per device.

v0:
```python
import math

import jax
import jax.numpy as jnp
from jax import lax
from jax.sharding import PartitionSpec as P

EPSILON = 1e-06
NEG_LARGE = -1e30


def merge_local_columns(base_weight, adapter_down_factor, adapter_up_factor):
    return base_weight.astype(jnp.float32) + jnp.dot(
        adapter_down_factor, adapter_up_factor, preferred_element_type=jnp.float32
    )


def per_device(
    token_hidden_rows,
    input_norm_gain,
    frozen_query,
    frozen_key_value,
    frozen_output,
    query_down_factor,
    query_up_factor,
    key_value_down_factor,
    key_value_up_factor,
    output_down_factor,
    output_up_factor,
    query_column_scale,
    key_value_column_scale,
    output_column_scale,
    cached_key_rows,
    cached_value_rows,
    lengths,
):
    merged_query_weight = merge_local_columns(frozen_query, query_down_factor, query_up_factor)
    merged_key_value = merge_local_columns(
        frozen_key_value, key_value_down_factor, key_value_up_factor
    )
    merged_output_weight = merge_local_columns(frozen_output, output_down_factor, output_up_factor)
    norm_sums = lax.psum(
        (
            jnp.sum(merged_query_weight * merged_query_weight, axis=0),
            jnp.sum(merged_key_value * merged_key_value, axis=0),
            jnp.sum(merged_output_weight * merged_output_weight, axis=0),
        ),
        ("rep", "tp"),
    )
    scaled_q = (merged_query_weight * (query_column_scale / jnp.sqrt(norm_sums[0]))).astype(
        jnp.bfloat16
    )
    scaled_kv = (merged_key_value * (key_value_column_scale / jnp.sqrt(norm_sums[1]))).astype(
        jnp.bfloat16
    )
    scaled_o = (merged_output_weight * (output_column_scale / jnp.sqrt(norm_sums[2]))).astype(
        jnp.bfloat16
    )
    step_count, seq_count, feat_width = token_hidden_rows.shape
    row_count = step_count * seq_count
    features = lax.all_gather(token_hidden_rows, "tp", axis=2, tiled=True).astype(jnp.float32)
    mean_sq = jnp.mean(features * features, axis=-1, keepdims=True)
    normed = (features * lax.rsqrt(mean_sq + EPSILON) * input_norm_gain).astype(jnp.bfloat16)
    normed = normed.reshape(row_count, -1)
    blocks = (
        lax.all_to_all(scaled_q, "tp", split_axis=1, concat_axis=0, tiled=True),
        lax.all_to_all(scaled_kv, "tp", split_axis=1, concat_axis=0, tiled=True),
        lax.all_to_all(scaled_o, "tp", split_axis=1, concat_axis=0, tiled=True),
    )
    query_sum = jnp.dot(
        normed,
        lax.all_gather(blocks[0], "rep", axis=0, tiled=True),
        preferred_element_type=jnp.float32,
    )
    fresh_sum = jnp.dot(
        normed,
        lax.all_gather(blocks[1], "rep", axis=0, tiled=True),
        preferred_element_type=jnp.float32,
    )
    output_weight = lax.all_gather(blocks[2], "rep", axis=0, tiled=True)
    query_loc = query_sum.astype(jnp.bfloat16).reshape(step_count, seq_count, -1)
    fresh_loc = fresh_sum.astype(jnp.bfloat16).reshape(step_count, seq_count, -1)
    heads_all, fresh_token_rows = (
        lax.all_to_all(query_loc, "tp", split_axis=1, concat_axis=2, tiled=True),
        lax.all_to_all(fresh_loc, "tp", split_axis=1, concat_axis=2, tiled=True),
    )
    local_seqs = heads_all.shape[1]
    heads_kv = cached_key_rows.shape[1]
    cache_len = cached_key_rows.shape[2]
    head_dim = cached_key_rows.shape[3]
    tensor_group_width = heads_all.shape[2] // (heads_kv * head_dim)
    query_heads = heads_all.reshape(step_count, local_seqs, heads_kv, tensor_group_width, head_dim)
    fresh_heads = fresh_token_rows.reshape(step_count, local_seqs, heads_kv, 2, head_dim)
    inv_root = 1.0 / math.sqrt(head_dim)
    live_mask = jnp.arange(cache_len, dtype=jnp.int32)[None, :] < lengths[:, None]
    live_mask = live_mask[None, :, None, None, :]
    order_ok = (
        jnp.arange(step_count, dtype=jnp.int32)[None, :]
        <= jnp.arange(step_count, dtype=jnp.int32)[:, None]
    )
    order_ok = order_ok[:, None, None, None, :]
    cache_scores = (
        jnp.einsum(
            "tbghd,bgjd->tbghj", query_heads, cached_key_rows, preferred_element_type=jnp.float32
        )
        * inv_root
    )
    cache_scores = jnp.where(live_mask, cache_scores, NEG_LARGE)
    fresh_scores = (
        jnp.einsum(
            "tbghd,ubgd->tbghu",
            query_heads,
            fresh_heads[:, :, :, 0],
            preferred_element_type=jnp.float32,
        )
        * inv_root
    )
    fresh_scores = jnp.where(order_ok, fresh_scores, NEG_LARGE)
    peak_score = jnp.maximum(jnp.max(cache_scores, axis=-1), jnp.max(fresh_scores, axis=-1))
    cache_probs = jnp.where(live_mask, jnp.exp(cache_scores - peak_score[..., None]), 0.0)
    fresh_probs = jnp.where(order_ok, jnp.exp(fresh_scores - peak_score[..., None]), 0.0)
    weight_total = jnp.sum(cache_probs, axis=-1) + jnp.sum(fresh_probs, axis=-1)
    context = jnp.einsum(
        "tbghj,bgjd->tbghd",
        cache_probs.astype(jnp.bfloat16),
        cached_value_rows,
        preferred_element_type=jnp.float32,
    )
    context = context + jnp.einsum(
        "tbghu,ubgd->tbghd",
        fresh_probs.astype(jnp.bfloat16),
        fresh_heads[:, :, :, 1],
        preferred_element_type=jnp.float32,
    )
    attended = (
        (context / weight_total[..., None]).astype(jnp.bfloat16).reshape(step_count, local_seqs, -1)
    )
    gathered = lax.all_gather(attended, "tp", axis=1, tiled=True)
    output = jnp.dot(
        gathered.reshape(row_count, -1), output_weight, preferred_element_type=jnp.float32
    ).astype(jnp.bfloat16)
    return output.reshape(step_count, seq_count, -1)


def solution(mesh):
    return jax.shard_map(
        per_device,
        mesh=mesh,
        in_specs=(
            P(None, "rep", "tp"),
            P(),
            P(("rep", "tp"), None),
            P(("rep", "tp"), None),
            P(("rep", "tp"), None),
            P(("rep", "tp"), None),
            P(),
            P(("rep", "tp"), None),
            P(),
            P(("rep", "tp"), None),
            P(),
            P(),
            P(),
            P(),
            P(("rep", "tp"), None, None, None),
            P(("rep", "tp"), None, None, None),
            P(("rep", "tp")),
        ),
        out_specs=P(None, "rep", "tp"),
        check_vma=False,
    )
```

profile of v0, /device:TPU:1, one launch (start us, length us, event | category | flops | bytes accessed | tf_op | source)
XLA Modules:
  0.0 700.8 jit_solution(18070017078653210167)
XLA Ops:
  8.4 3.8 multiply_reduce_fusion.1
  12.2 1.9 multiply_reduce_fusion.2
  15.9 152.7 %all-reduce.3.cloned.1.call-done = (f32[8192]{0:T(1024)}, f32[2048]{0:T(1024)}, f32[8192]{0:T(1024)}) async-done(((f32[8192]{0:T(1024)}, f32[2048]{0:T(1024)}, f32[8192]{0:T(1024)}), (f32[8192]{0:T(1024)}, f32[2048]{0:T(1024)}, f32[8192]{0:T(1024)})) %all-reduce.3.cloned.1.call-update) | async-done | bytes 73744 | tf_op jit(solution)/shard_map/psum | solution.py:42
  169.4 13.1 %all_to_all.87 = bf16[64,16,128]{2,0,1:T(8,128)(2,1)} all-to-all(bf16[64,16,128]{2,0,1:T(8,128)(2,1)S(1)} %copy_bitcast_fusion.2), channel_id=1, replica_groups=mesh['rep'=8,'tp'=16] {'tp'}, dimensions={1} | all-to-all | bytes 524288 | tf_op jit(solution)/shard_map/all_to_all | solution.py:67
  183.4 1.7 multiply_convert_fusion.1
  185.3 24.3 %all_to_all.88 = bf16[64,16,512]{2,0,1:T(8,128)(2,1)} all-to-all(bf16[64,16,512]{2,0,1:T(8,128)(2,1)S(1)} %bitcast.115), channel_id=1, replica_groups=mesh['rep'=8,'tp'=16] {'tp'}, dimensions={1} | all-to-all | bytes 2097152 | tf_op jit(solution)/shard_map/all_to_all | solution.py:66
  209.7 3.3 fusion
  213.2 3.1 fusion.2
  216.3 23.8 %all-gather.10.cloned.1.call-done = bf16[8192,128]{1,0:T(8,128)(2,1)} async-done(((bf16[1024,128]{1,0:T(8,128)(2,1)}), bf16[8192,128]{1,0:T(8,128)(2,1)}) %all-gather.10.cloned.1.call-update) | async-done | bytes 2097168 | tf_op jit(solution)/shard_map/all_gather | solution.py:77
  240.1 4.1 convolution_convert_fusion.2
  244.9 8.9 %all-to-all-start.3 = ((bf16[4,64,128]{2,0,1:T(4,128)(2,1)}), bf16[4,64,128]{2,0,1:T(4,128)(2,1)S(1)}, u32[]{:S(2)}, u32[]{:S(2)}) async-start(bf16[4,64,128]{2,0,1:T(4,128)(2,1)} %copy.56), calls=%async_computation.3 | async-start | bytes 131072 | tf_op jit(solution)/shard_map/all_to_all | solution.py:85
  253.8 158.5 %all-gather.8.cloned.1.call-done = bf16[8192,512]{1,0:T(8,128)(2,1)} async-done(((bf16[1024,512]{1,0:T(8,128)(2,1)}), bf16[8192,512]{1,0:T(8,128)(2,1)}) %all-gather.8.cloned.1.call-update) | async-done | bytes 8388624 | tf_op jit(solution)/shard_map/all_gather | solution.py:72
  412.3 7.0 convolution_convert_fusion.1
  420.2 7.3 %all-to-all-start.1 = ((bf16[4,64,512]{2,0,1:T(4,128)(2,1)}), bf16[4,64,512]{2,0,1:T(4,128)(2,1)S(1)}, u32[]{:S(2)}, u32[]{:S(2)}) async-start(bf16[4,64,512]{2,0,1:T(4,128)(2,1)} %copy.52), calls=%async_computation.1 | async-start | bytes 524288 | tf_op jit(solution)/shard_map/all_to_all | solution.py:84
  427.9 8.5 %all-to-all-done.1 = bf16[4,64,512]{2,0,1:T(4,128)(2,1)S(1)} async-done(((bf16[4,64,512]{2,0,1:T(4,128)(2,1)}), bf16[4,64,512]{2,0,1:T(4,128)(2,1)S(1)}, u32[]{:S(2)}, u32[]{:S(2)}) %all-to-all-start.1) | async-done | bytes 262176 | tf_op jit(solution)/shard_map/all_to_all | solution.py:84
  436.8 6.3 bitcast_reduce_fusion
  443.0 1.3 fusion.42
  444.4 1.2 fusion.9
  445.6 5.3 fusion.18
  452.8 22.2 %all_to_all.89 = bf16[64,16,512]{2,0,1:T(8,128)(2,1)} all-to-all(bf16[64,16,512]{2,0,1:T(8,128)(2,1)S(1)} %bitcast.116), channel_id=1, replica_groups=mesh['rep'=8,'tp'=16] {'tp'}, dimensions={1} | all-to-all | bytes 2097152 | tf_op jit(solution)/shard_map/all_to_all | solution.py:68
  475.0 42.3 %all-gather.12.cloned.1.call-done = bf16[4,64,8192]{2,0,1:T(4,128)(2,1)} async-done(((bf16[4,4,8192]{2,0,1:T(4,128)(2,1)}), bf16[4,64,8192]{2,0,1:T(4,128)(2,1)}) %all-gather.12.cloned.1.call-update) | async-done | bytes 4194320 | tf_op jit(solution)/shard_map/all_gather | solution.py:138
  517.3 6.4 copy.64
  523.7 161.8 %all-gather.14.cloned.1.call-done = bf16[8192,512]{1,0:T(8,128)(2,1)} async-done(((bf16[1024,512]{1,0:T(8,128)(2,1)}), bf16[8192,512]{1,0:T(8,128)(2,1)}) %all-gather.14.cloned.1.call-update) | async-done | bytes 8388624 | tf_op jit(solution)/shard_map/all_gather | solution.py:80
  685.5 7.7 %convolution_convert_fusion = bf16[256,512]{1,0:T(8,128)(2,1)} fusion(bf16[256,8192]{1,0:T(8,128)(2,1)} %bitcast.112, bf16[8192,512]{1,0:T(8,128)(2,1)} %all-gather.14.cloned.1.call-done), kind=kOutput, calls=%fused_computation.34 | convolution fusion | flops 2147614720 | bytes 12845056 | tf_op jit(solution)/shard_map/dot_general | solution.py:139
  (59 shorter events, 8.9 us)
Async XLA Ops:
  7.4 1.0 copy-start
  7.4 6.8 copy-start.8
  7.4 6.8 copy-start.4
  7.4 161.2 %copy-start.9 = (f32[2048]{0:T(1024)S(1)}, f32[2048]{0:T(1024)}, u32[]{:S(2)}) copy-start(f32[2048]{0:T(1024)} %param.29) | copy-start | bytes 24580
  7.4 161.2 %all-reduce.3.cloned.1.call-start = ((), (), s32[]{:S(2)}) async-start(), calls=%async_computation.10 | async-start | bytes 147456 | tf_op jit(solution)/shard_map/psum | solution.py:42
  8.4 5.7 copy-start.3
  12.2 170.4 %copy-start.6 = (f32[8192]{0:T(1024)S(1)}, f32[8192]{0:T(1024)}, u32[]{:S(2)}) copy-start(f32[8192]{0:T(1024)} %param.30) | copy-start | bytes 98308
  12.2 170.4 %copy-start.7 = (f32[8192]{0:T(1024)S(1)}, f32[8192]{0:T(1024)}, u32[]{:S(2)}) copy-start(f32[8192]{0:T(1024)} %param.28) | copy-start | bytes 98308
  15.3 194.4 %all-gather.6.cloned.1.call-start = ((), (), s32[]{:S(2)}) async-start(), calls=%async_computation.5 | async-start | bytes 4456448 | tf_op jit(solution)/shard_map/all_gather | solution.py:61
  15.9 224.2 %all-gather.10.cloned.1.call-start = ((), (), s32[]{:S(2)}) async-start(), calls=%async_computation.7 | async-start | bytes 2359296 | tf_op jit(solution)/shard_map/all_gather | solution.py:77
  182.5 229.8 %all-gather.8.cloned.1.call-start = ((), (), s32[]{:S(2)}) async-start(), calls=%async_computation.6 | async-start | bytes 9437184 | tf_op jit(solution)/shard_map/all_gather | solution.py:72
  183.4 26.2 %copy-start.10 = (s32[4]{0:T(128)S(1)}, s32[4]{0:T(128)}, u32[]{:S(2)}) copy-start(s32[4]{0:T(128)} %param.33) | copy-start | bytes 52
  185.2 27.8 %copy-start.5 = (f32[8192]{0:T(1024)S(1)}, f32[8192]{0:T(1024)}, u32[]{:S(2)}) copy-start(f32[8192]{0:T(1024)} %param.18) | copy-start | bytes 98308
  209.7 3.5 copy-start.2
  244.9 175.3 %all-to-all-start.3 = ((bf16[4,64,128]{2,0,1:T(4,128)(2,1)}), bf16[4,64,128]{2,0,1:T(4,128)(2,1)S(1)}, u32[]{:S(2)}, u32[]{:S(2)}) async-start(bf16[4,64,128]{2,0,1:T(4,128)(2,1)} %copy.56), calls=%async_computation.3 | async-start | bytes 131072 | tf_op jit(solution)/shard_map/all_to_all | solution.py:85
  420.2 16.2 %all-to-all-start.1 = ((bf16[4,64,512]{2,0,1:T(4,128)(2,1)}), bf16[4,64,512]{2,0,1:T(4,128)(2,1)S(1)}, u32[]{:S(2)}, u32[]{:S(2)}) async-start(bf16[4,64,512]{2,0,1:T(4,128)(2,1)} %copy.52), calls=%async_computation.1 | async-start | bytes 524288 | tf_op jit(solution)/shard_map/all_to_all | solution.py:84
  427.5 89.8 %all-gather.12.cloned.1.call-start = ((), (), s32[]{:S(2)}) async-start(), calls=%async_computation.8 | async-start | bytes 4456448 | tf_op jit(solution)/shard_map/all_gather | solution.py:138
  452.5 233.0 %all-gather.14.cloned.1.call-start = ((), (), s32[]{:S(2)}) async-start(), calls=%async_computation.9 | async-start | bytes 9437184 | tf_op jit(solution)/shard_map/all_gather | solution.py:80
  685.5 7.7 %copy-start.1 = (bf16[32,8192]{1,0:T(8,128)(2,1)S(1)}, bf16[32,8192]{1,0:T(8,128)(2,1)}, u32[]{:S(2)}) copy-start(bf16[32,8192]{1,0:T(8,128)(2,1)} %param.23) | copy-start | bytes 1572868
Sparse Core Ops, SparseCore 0:
  15.4 153.1 all-reduce.2
Sparse Core Ops, SparseCore 1:
  18.1 62.4 all-gather.5
  182.6 57.4 all-gather.9
  241.7 170.5 all-gather.7
  452.5 64.7 all-gather.11
  519.0 166.4 all-gather.13
where the time goes:
time: 705 us; the launch traced here: 701 us
  waiting for transfers between devices  548 us (78%)
  blocking collectives  59.7 us (8%)
  matrix products  38.9 us (6%)
  starting transfers between devices  16.7 us (2%)
  between operations  15.3 us (2%)
  other arithmetic  11.5 us (2%)
  local copies, waits for them, and re-layouts  10.7 us (2%)
    all_gather x1, waiting for transfers between devices, per_device(): output_weight = lax.all_gather(blocks[2], 'rep', axis=0, tiled=True)  162 us
    all_gather x1, waiting for transfers between devices, per_device(): lax.all_gather(blocks[0], 'rep', axis=0, tiled=True)  158 us
    psum x1, waiting for transfers between devices, per_device(): lax.psum((jnp.sum(merged_query_weight * merged_query_weight, axis=0), jnp...  153 us
    all_gather x1, waiting for transfers between devices, per_device(): gathered = lax.all_gather(attended, 'tp', axis=1, tiled=True)  42.3 us
    all_to_all x1, blocking collectives, per_device(): lax.all_to_all(scaled_q, 'tp', split_axis=1, concat_axis=0, tiled=True)  24.3 us
    all_gather x1, waiting for transfers between devices, per_device(): lax.all_gather(blocks[1], 'rep', axis=0, tiled=True)  23.8 us
    all_to_all x1, blocking collectives, per_device(): lax.all_to_all(scaled_o, 'tp', split_axis=1, concat_axis=0, tiled=True)  22.2 us
  transfers between devices with their start and end apart: 8, of which 6 were waited for; matrix products, arithmetic and copies ran while one was open for 4% of the time, Pallas kernels for 0%

commit v1 on v0

v1 whole, which is shorter than its diff:
```python
import math

import jax
import jax.numpy as jnp
from jax import lax
from jax.experimental import pallas as pl
from jax.experimental.pallas import tpu as pltpu
from jax.sharding import PartitionSpec as P

EPSILON = 1e-06
NEG_LARGE = -1e30
AXES = ("rep", "tp")


def device_index(y, zl, x, zh, c):
    return (y * 2 + zl) * 16 + x * 4 + zh * 2 + c


def permute(value, target):
    pairs = []
    for y in range(4):
        for zl in range(2):
            for x in range(4):
                for zh in range(2):
                    for c in range(2):
                        pairs.append(
                            (device_index(y, zl, x, zh, c), device_index(*target(y, zl, x, zh, c)))
                        )
    return lax.ppermute(value, AXES, pairs)


def swap_low(value):
    return permute(value, lambda y, zl, x, zh, c: (y, 1 - zl, x, zh, c))


def swap_core(value):
    return permute(value, lambda y, zl, x, zh, c: (y, zl, x, zh, 1 - c))


def from_y(value, step):
    return permute(value, lambda y, zl, x, zh, c: ((y - step) % 4, zl, x, zh, c))


def from_x(value, step):
    return permute(value, lambda y, zl, x, zh, c: (y, zl, (x - step) % 4, zh, c))


def after(value, earlier):
    return lax.optimization_barrier((value, earlier))[0]


def pick(value, index, axis=0):
    return lax.dynamic_index_in_dim(value, index, axis, keepdims=False)


def share_sums(sums):
    spread = jnp.broadcast_to(sums[None, :], (8, sums.shape[0]))
    return jnp.sum(lax.all_to_all(spread, "rep", 0, 0, tiled=True), axis=0)


def pack_columns_kernel(place, query, key_value, down_q, down_kv, down_o, out):
    f32 = jnp.float32
    down_q, down_kv, down_o = (d[...].astype(f32) for d in (down_q, down_kv, down_o))
    blank = jnp.zeros_like(down_o)
    down = jnp.where(
        place[0] < 8,
        jnp.concatenate([down_q, down_kv, down_o, blank], axis=0),
        jnp.concatenate([down_o, blank, down_q, down_kv], axis=0),
    )
    down = down.T.astype(jnp.bfloat16)
    for i in range(4):
        for k in range(4):
            out[i, k] = query[:, (i * 4 + k) * 128 : (i * 4 + k + 1) * 128]
        out[i, 4] = key_value[:, i * 128 : (i + 1) * 128]
        out[i, 5] = down


def pack_columns(place, query, key_value, *downs):
    down = pl.BlockSpec((32, 64), lambda i, place: (0, 0))
    return pl.pallas_call(
        pack_columns_kernel,
        grid_spec=pltpu.PrefetchScalarGridSpec(
            num_scalar_prefetch=1,
            grid=(4,),
            in_specs=[
                pl.BlockSpec((64, 2048), lambda i, place: (0, i)),
                pl.BlockSpec((64, 512), lambda i, place: (0, i)),
                down,
                down,
                down,
            ],
            out_specs=pl.BlockSpec((4, 6, 64, 128), lambda i, place: (i, 0, 0, 0)),
        ),
        out_shape=jax.ShapeDtypeStruct((16, 6, 64, 128), jnp.bfloat16),
        cost_estimate=pl.CostEstimate(flops=0, bytes_accessed=2**22, transcendentals=0),
    )(place, query, key_value, *downs)


def unpack_columns_kernel(received, ups, block_a, block_b, down, out):
    lanes = lax.broadcasted_iota(jnp.int32, (64, 128), 1)
    for i in range(8):
        rows = slice(i * 64, (i + 1) * 64)
        first, second = received[i, 5], received[8 + i, 5]
        down[rows] = first
        down[512 + i * 64 : 512 + (i + 1) * 64] = second
        block_a[0, rows] = jnp.where(
            lanes < 64, first.astype(jnp.float32), second.astype(jnp.float32)
        ).astype(jnp.bfloat16)
        for k in range(5):
            block_a[1 + k, rows] = received[i, k]
            block_b[k, rows] = received[8 + i, k]
    for half in range(2):
        merged = jnp.dot(block_a[0], ups[half], preferred_element_type=jnp.float32)
        sums = []
        for k in range(5):
            rows = block_a[1 + k] if half == 0 else block_b[k]
            tile = merged[:, k * 128 : (k + 1) * 128] + rows.astype(jnp.float32)
            sums.append(jnp.sum(tile * tile, axis=0, keepdims=True))
        sums = jnp.concatenate(sums, axis=1)
        if half == 0:
            out[...] = sums
        else:
            out[...] += sums


def unpack_columns(received, ups):
    return pl.pallas_call(
        unpack_columns_kernel,
        out_shape=[
            jax.ShapeDtypeStruct((6, 512, 128), jnp.bfloat16),
            jax.ShapeDtypeStruct((5, 512, 128), jnp.bfloat16),
            jax.ShapeDtypeStruct((1024, 128), jnp.bfloat16),
            jax.ShapeDtypeStruct((1, 640), jnp.float32),
        ],
        compiler_params=pltpu.CompilerParams(vmem_limit_bytes=24 * 2**20),
        cost_estimate=pl.CostEstimate(flops=2**28, bytes_accessed=2**22, transcendentals=0),
    )(received, ups)


def multiply_slab_kernel(place, near, far, inverse, gain, ups, factor, block_a, block_b, *rest):
    out = rest[-1]
    value = None
    for half in range(2):
        tokens = jnp.where(place[2] == half, near[0], far[0]).astype(jnp.float32)
        normed = (tokens * inverse[...] * gain[0, half]).astype(jnp.bfloat16)
        merged = jnp.dot(block_a[0], ups[half], preferred_element_type=jnp.float32)
        tiles = []
        for k in range(5):
            rows = block_a[1 + k] if half == 0 else block_b[k]
            tiles.append(merged[:, k * 128 : (k + 1) * 128] + rows.astype(jnp.float32))
        weight = (jnp.concatenate(tiles, axis=1) * factor[...]).astype(jnp.bfloat16)
        part = jnp.dot(normed, weight, preferred_element_type=jnp.float32)
        value = part if value is None else value + part
    if len(rest) == 2:
        value = value + rest[0][...]
    out[...] = value


def multiply_slab(place, near, far, inverse, gains, blocks, ups, factor, total):
    def whole(shape):
        return pl.BlockSpec(shape, lambda i, place: (0,) * len(shape))

    operands = [near, far, inverse, gains, ups, factor, *blocks]
    specs = [
        pl.BlockSpec((1, 512, 512), lambda i, place: (place[0], 0, 0)),
        pl.BlockSpec((1, 512, 512), lambda i, place: (place[0], 0, 0)),
        whole((512, 1)),
        pl.BlockSpec((1, 2, 1, 512), lambda i, place: (place[1], 0, 0, 0)),
        whole((2, 128, 640)),
        whole((1, 640)),
    ]
    specs += [whole(block.shape) for block in blocks]
    if total is not None:
        operands.append(total)
        specs.append(whole((512, 640)))
    return pl.pallas_call(
        multiply_slab_kernel,
        grid_spec=pltpu.PrefetchScalarGridSpec(
            num_scalar_prefetch=1,
            grid=(1,),
            in_specs=specs,
            out_specs=whole((512, 640)),
        ),
        out_shape=jax.ShapeDtypeStruct((512, 640), jnp.float32),
        compiler_params=pltpu.CompilerParams(vmem_limit_bytes=40 * 2**20),
        cost_estimate=pl.CostEstimate(flops=2**30, bytes_accessed=2**22, transcendentals=0),
    )(place, *operands)


def attend_kernel(place, lengths, every, keys, values, out):
    f32, bf16 = jnp.float32, jnp.bfloat16
    inv_root = 1.0 / math.sqrt(128)
    both = every[...].astype(f32)
    fresh_keys = every[0, :, 512:]
    fresh_values = every[1, :, 512:]
    contract_last = (((1,), (1,)), ((), ()))
    fresh_column = lax.broadcasted_iota(jnp.int32, (32, 16), 1)
    fresh_row = lax.broadcasted_iota(jnp.int32, (32, 16), 0)
    slots = lax.broadcasted_iota(jnp.int32, (32, 1024), 1)
    pieces = []
    for b in range(4):
        rows = slice(b * 4, b * 4 + 4)
        query = jnp.concatenate(
            [both[h // 4, rows, (h % 4) * 128 : (h % 4 + 1) * 128] for h in range(8)], axis=0
        ).astype(bf16)
        live = slots < lengths[b]
        scores = lax.dot_general(query, keys[b, 0], contract_last, preferred_element_type=f32)
        scores = jnp.where(live, scores * inv_root, NEG_LARGE)
        order = (fresh_column >= b * 4) & (fresh_column - b * 4 <= fresh_row % 4)
        fresh = lax.dot_general(query, fresh_keys, contract_last, preferred_element_type=f32)
        fresh = jnp.where(order, fresh * inv_root, NEG_LARGE)
        peak = jnp.maximum(
            jnp.max(scores, axis=1, keepdims=True), jnp.max(fresh, axis=1, keepdims=True)
        )
        probs = jnp.where(live, jnp.exp(scores - peak), 0.0)
        fresh_probs = jnp.where(order, jnp.exp(fresh - peak), 0.0)
        total = jnp.sum(probs, axis=1, keepdims=True) + jnp.sum(fresh_probs, axis=1, keepdims=True)
        context = jnp.dot(probs.astype(bf16), values[b, 0], preferred_element_type=f32)
        context += jnp.dot(fresh_probs.astype(bf16), fresh_values, preferred_element_type=f32)
        context = context / total
        pieces.append(jnp.concatenate([context[h * 4 : h * 4 + 4] for h in range(8)], axis=1))
    out[0] = jnp.concatenate(pieces, axis=0).astype(bf16)


def attend(place, lengths, every, cached_key_rows, cached_value_rows):
    def slab(g, place, lengths):
        return (((g + place[1]) % 2) * 4 + (g // 2 + 4 - place[0]) % 4, 0, 0)

    cache = pl.BlockSpec((4, 1, 1024, 128), lambda g, place, lengths: (0, g, 0, 0))
    return pl.pallas_call(
        attend_kernel,
        grid_spec=pltpu.PrefetchScalarGridSpec(
            num_scalar_prefetch=2,
            grid=(8,),
            in_specs=[
                pl.BlockSpec((2, 16, 640), lambda g, place, lengths: (g, 0, 0)),
                cache,
                cache,
            ],
            out_specs=pl.BlockSpec((1, 16, 1024), slab),
        ),
        out_shape=jax.ShapeDtypeStruct((8, 16, 1024), jnp.bfloat16),
        compiler_params=pltpu.CompilerParams(vmem_limit_bytes=56 * 2**20),
        cost_estimate=pl.CostEstimate(flops=2**29, bytes_accessed=2**24, transcendentals=2**20),
    )(place, lengths, every, cached_key_rows, cached_value_rows)


def output_kernel(place, near_a, near_b, far_a, far_b, rows_0, rows_1, rows_2, rows_3, mine, other):
    weights = (rows_0, rows_1, rows_2, rows_3)
    total = None
    for j in range(4):
        parts = []
        for first, second in ((near_a, near_b), (far_a, far_b)):
            if j < 2:
                parts.append(first[:, :, j].reshape(256, 1024))
            else:
                parts.extend(second[:, e, j - 2].reshape(64, 1024) for e in range(4))
        part = jnp.dot(
            jnp.concatenate(parts, axis=0), weights[j][...], preferred_element_type=jnp.float32
        )
        total = part if total is None else total + part
    for cr in range(2):
        for e in range(4):
            for dl in range(2):
                for dh in range(2):
                    start = cr * 256 + e * 64 + dl * 32 + dh * 16
                    target = ((place[0] + e) % 4) * 4 + (place[1] ^ dh) * 2 + (place[2] ^ cr)
                    rows = total[start : start + 16]
                    if dl == 0:
                        mine[target] = rows
                    else:
                        other[target] = rows.astype(jnp.bfloat16)


def multiply_output(place, pieces, rows_o):
    def whole(shape):
        return pl.BlockSpec(shape, lambda i, place: (0,) * len(shape))

    operands = [*pieces, *rows_o]
    return pl.pallas_call(
        output_kernel,
        grid_spec=pltpu.PrefetchScalarGridSpec(
            num_scalar_prefetch=1,
            grid=(1,),
            in_specs=[whole(operand.shape) for operand in operands],
            out_specs=[whole((16, 16, 512)), whole((16, 16, 512))],
        ),
        out_shape=[
            jax.ShapeDtypeStruct((16, 16, 512), jnp.float32),
            jax.ShapeDtypeStruct((16, 16, 512), jnp.bfloat16),
        ],
        compiler_params=pltpu.CompilerParams(vmem_limit_bytes=40 * 2**20),
        cost_estimate=pl.CostEstimate(flops=2**31, bytes_accessed=2**23, transcendentals=0),
    )(place, *operands)


def per_device(
    token_hidden_rows,
    input_norm_gain,
    frozen_query,
    frozen_key_value,
    frozen_output,
    query_down_factor,
    query_up_factor,
    key_value_down_factor,
    key_value_up_factor,
    output_down_factor,
    output_up_factor,
    query_column_scale,
    key_value_column_scale,
    output_column_scale,
    cached_key_rows,
    cached_value_rows,
    lengths,
):
    f32, bf16 = jnp.float32, jnp.bfloat16
    r, t = lax.axis_index("rep"), lax.axis_index("tp")
    y, zl = r // 2, r % 2
    x, zh, c = t // 4, (t // 2) % 2, t % 2

    local = token_hidden_rows.reshape(256, 512)
    pair = jnp.concatenate(
        [
            permute(local, lambda y, zl, x, zh, c, s=s: (y, zh, x, zl ^ s, c))
            for s in range(2)
        ]
    )

    frozen = pack_columns(
        t.astype(jnp.int32).reshape(1),
        frozen_query,
        frozen_key_value,
        query_down_factor.T,
        key_value_down_factor.T,
        output_down_factor.T,
    )
    received = lax.all_to_all(frozen, "tp", 0, 0, tiled=True)

    up_q = lax.dynamic_slice_in_dim(query_up_factor, t * 512, 512, 1)
    up_kv = lax.dynamic_slice_in_dim(key_value_up_factor, t * 128, 128, 1)
    up_o = lax.dynamic_slice_in_dim(output_up_factor, t * 512, 512, 1)
    up_qkv = jnp.concatenate(
        [
            jnp.concatenate([up_q, jnp.zeros((32, 128), bf16)], axis=1),
            jnp.concatenate([jnp.zeros((32, 512), bf16), up_kv], axis=1),
        ],
        axis=0,
    )
    blank = jnp.zeros((64, 640), bf16)
    ups = jnp.stack(
        [jnp.concatenate([up_qkv, blank], axis=0), jnp.concatenate([blank, up_qkv], axis=0)]
    )
    up_out_a = jnp.concatenate(
        [jnp.zeros((64, 512), bf16), up_o, jnp.zeros((32, 512), bf16)], axis=0
    )
    up_out_b = jnp.concatenate([up_o, jnp.zeros((96, 512), bf16)], axis=0)
    scale_qkv = jnp.concatenate(
        [
            lax.dynamic_slice_in_dim(query_column_scale, t * 512, 512, 0),
            lax.dynamic_slice_in_dim(key_value_column_scale, t * 128, 128, 0),
        ]
    )
    scale_out = lax.dynamic_slice_in_dim(output_column_scale, t * 512, 512, 0)

    received, ups, up_out_a, up_out_b, scale_qkv, scale_out = lax.optimization_barrier(
        (received, ups, up_out_a, up_out_b, scale_qkv, scale_out)
    )
    own_a, own_b, down_own, sums = unpack_columns(received, ups)
    sums = share_sums(sums.reshape(640))
    factor_qkv = (scale_qkv / jnp.sqrt(sums)).reshape(1, 640)

    own_a, own_b, pair = lax.optimization_barrier((own_a, own_b, pair, sums))[:3]
    next_a, next_b = from_y(own_a, 1), from_y(own_b, 1)
    last_b, last_a = from_y(own_b, 3), from_y(own_a, 3)
    tokens = [pair] + [from_x(pair, step) for step in (1, 2, 3)]
    tokens, next_a, next_b, last_a, last_b = lax.optimization_barrier(
        (tokens, next_a, next_b, last_a, last_b)
    )
    far_a, far_b = from_y(next_a, 1), from_y(last_b, 3)

    frozen_o = after(frozen_output, next_a)
    own_o = lax.all_to_all(
        frozen_o.reshape(64, 16, 512).transpose(1, 0, 2), "tp", 0, 0, tiled=True
    ).reshape(1024, 512)
    merged_o = own_o.astype(f32) + jnp.concatenate(
        [
            jnp.dot(down_own[:512], up_out_a, preferred_element_type=f32),
            jnp.dot(down_own[512:], up_out_b, preferred_element_type=f32),
        ]
    )
    sums_o = jnp.sum(merged_o * merged_o, axis=0)

    near = jnp.stack(tokens)
    far = swap_core(near)
    near_wide, far_wide = near.astype(f32), far.astype(f32)
    square_sum = jnp.sum(near_wide * near_wide + far_wide * far_wide, axis=(0, 2))
    square_sum = square_sum + swap_low(square_sum)
    inverse = lax.rsqrt(square_sum / 8192.0 + EPSILON).reshape(512, 1)
    gains = pick(input_norm_gain.reshape(4, 2, 2, 1, 512), zl, 1)

    def project(step, blocks, total):
        place = jnp.stack([(y + step - x) % 4, (y + step) % 4, c]).astype(jnp.int32)
        return multiply_slab(
            place, near, far, inverse, gains, blocks, ups, factor_qkv, total
        )

    total = project(0, (own_a, own_b), None)
    total = project(1, (next_a, next_b), total)
    total = project(3, (last_a, last_b), total)
    total, far_a, far_b = lax.optimization_barrier((total, far_a, far_b))
    total = project(2, (far_a, far_b), total)

    sums_o = share_sums(after(sums_o, total))
    weight_o = (merged_o * (scale_out / jnp.sqrt(sums_o))).astype(bf16)
    rows_o = [weight_o] + [from_y(weight_o, step) for step in (1, 2, 3)]

    total = total.reshape(2, 256, 640)
    mine = zh ^ zl
    projected = (pick(total, mine) + swap_low(pick(total, 1 - mine))).astype(bf16)

    projected = projected.reshape(4, 16, 4, 640).transpose(1, 2, 0, 3).reshape(16, 16, 640)
    every = lax.all_to_all(projected, "tp", 0, 0, tiled=True)
    place = jnp.stack([y, zl]).astype(jnp.int32)
    attended = attend(place, lengths, every, cached_key_rows, cached_value_rows)

    attended, rows_o = lax.optimization_barrier((attended, rows_o))
    slabs = attended.reshape(2, 4, 16, 1024)

    def along_z(own, other):
        def flip(value, dl, dh):
            return permute(value, lambda y, zl, x, zh, c: (y, zl ^ dl, x, zh ^ dh, c))

        return jnp.stack([own, flip(own, 0, 1), flip(other, 1, 0), flip(other, 1, 1)])

    def along_x(value):
        return jnp.stack([value] + [from_x(value, step) for step in (1, 2, 3)])

    first = along_z(slabs[0, :2], slabs[1, :2])
    second = along_x(slabs[:, 2:])
    first = along_x(first)
    second = along_z(second[:, 0], second[:, 1])
    place = jnp.stack([x, zh, c]).astype(jnp.int32)
    mine, other = multiply_output(
        place, (first, second, swap_core(first), swap_core(second)), rows_o
    )
    result = (mine + swap_low(other).astype(f32)).astype(bf16)
    return result.reshape(16, 4, 4, 512).transpose(2, 0, 1, 3).reshape(4, 64, 512)


def solution(mesh):
    return jax.shard_map(
        per_device,
        mesh=mesh,
        in_specs=(
            P(None, "rep", "tp"),
            P(),
            P(("rep", "tp"), None),
            P(("rep", "tp"), None),
            P(("rep", "tp"), None),
            P(("rep", "tp"), None),
            P(),
            P(("rep", "tp"), None),
            P(),
            P(("rep", "tp"), None),
            P(),
            P(),
            P(),
            P(),
            P(("rep", "tp"), None, None, None),
            P(("rep", "tp"), None, None, None),
            P(("rep", "tp")),
        ),
        out_specs=P(None, "rep", "tp"),
        check_vma=False,
    )
```

time: 705 us -> 250 us (0.35)
  waiting for transfers between devices: 548 us -> 89.9 us
  starting transfers between devices: 16.7 us -> 84.2 us
  blocking collectives: 59.7 us -> 0 us
  Pallas kernels: 0 us -> 36.6 us
  matrix products: 38.9 us -> 3.51 us
  between operations: 15.3 us -> 0.44 us
  local copies, waits for them, and re-layouts: 10.7 us -> 20.3 us
    all_gather x5 -> x0, waiting for transfers between devices: 386 us -> none  [the longest x1 162 us: per_device(): output_weight = lax.all_gather(blocks[2], 'rep', axis=0, tiled=True)]
    psum x1 -> x0, waiting for transfers between devices: 153 us -> none  [per_device(): lax.psum((jnp.sum(merged_query_weight * merged_query_weight, axis=0), jnp...]
    all_to_all x3 -> x0, blocking collectives: 59.7 us -> none  [the longest x1 24.3 us: per_device(): lax.all_to_all(scaled_q, 'tp', split_axis=1, concat_axis=0, tiled=True)]
    ppermute x0 -> x32, waiting for transfers between devices: none -> 54.9 us  [permute(): return lax.ppermute(value, AXES, pairs)]
    ppermute x0 -> x32, starting transfers between devices: none -> 51.1 us  [permute(): return lax.ppermute(value, AXES, pairs)]
    pallas_call x0 -> x8, Pallas kernels: none -> 36.6 us  [the longest x1 14.8 us: attend(): pl.pallas_call(attend_kernel, grid_spec=pltpu.PrefetchScalarGridSpec(num_...]
    dot_general x10 -> x2, matrix products: 38.9 us -> 3.51 us  [the longest x1 2.24 us: per_device(): jnp.dot(down_own[512:], up_out_b, preferred_element_type=f32)]
    all_to_all x2 -> x5, waiting for transfers between devices: 8.53 us -> 35 us  [the longest x1 12.4 us: per_device(): received = lax.all_to_all(frozen, 'tp', 0, 0, tiled=True)]
  transfers between devices with their start and end apart: 8 -> 37, of which waited for: 6 -> 16; matrix products, arithmetic and copies ran while one was open for 4% -> 11% of each run, Pallas kernels for 0% -> 10%
where the time goes in v1:
time: 250 us; the launch traced here: 249 us
  waiting for transfers between devices  89.9 us (36%)
  starting transfers between devices  84.2 us (34%)
  Pallas kernels  36.6 us (15%)
  local copies, waits for them, and re-layouts  20.3 us (8%)
  other arithmetic  13.8 us (6%)
  matrix products  3.51 us (1%)
    ppermute x32, waiting for transfers between devices, permute(): return lax.ppermute(value, AXES, pairs)  54.9 us
    ppermute x32, starting transfers between devices, permute(): return lax.ppermute(value, AXES, pairs)  51.1 us
    pallas_call x1, Pallas kernels, attend(): pl.pallas_call(attend_kernel, grid_spec=pltpu.PrefetchScalarGridSpec(num_...  14.8 us
    pallas_call x4, Pallas kernels, multiply_slab(): pl.pallas_call(multiply_slab_kernel, grid_spec=pltpu.PrefetchScalarGridSp...  13.1 us
    all_to_all x1, waiting for transfers between devices, per_device(): received = lax.all_to_all(frozen, 'tp', 0, 0, tiled=True)  12.4 us
    all_to_all x1, starting transfers between devices, per_device(): lax.all_to_all(frozen_o.reshape(64, 16, 512).transpose(1, 0, 2), 'tp', 0,...  9.65 us
    all_to_all x1, starting transfers between devices, per_device(): received = lax.all_to_all(frozen, 'tp', 0, 0, tiled=True)  9.13 us
    all_to_all x1, waiting for transfers between devices, per_device(): lax.all_to_all(frozen_o.reshape(64, 16, 512).transpose(1, 0, 2), 'tp', 0,...  9.03 us
  transfers between devices with their start and end apart: 37, of which 16 were waited for; matrix products, arithmetic and copies ran while one was open for 11% of the time, Pallas kernels for 10%

profile of v1, /device:TPU:1, one launch (start us, length us, event | category | flops | bytes accessed | tf_op | source)
XLA Modules:
  0.0 248.7 jit_solution(7974882259919848902)
XLA Ops:
  0.0 3.7 %shard_map.163 = bf16[16,6,64,128]{3,2,1,0:T(8,128)(2,1)} custom-call(s32[1]{0:T(128)} %bitcast.7.place, bf16[64,8192]{1,0:T(8,128)(2,1)} %query.1, bf16[64,2048]{1,0:T(8,128)(2,1)} %key_value.1, bf16[32,64]{1,0:T(8,128)(2,1)} %bitcast.117, bf16[32,64]{1,0:T(8,128)(2,1)} %bitcast.118, bf16[32,64]{1,0:T(8,128)(2,1)} %bitcast.119), custom_call_target="tpu_custom_call" | custom-call | bytes 4194304 | tf_op jit(solution)/shard_map/pallas_call | solution.py:80
  3.7 9.1 %all-to-all-start = ((bf16[16,6,64,128]{3,2,1,0:T(8,128)(2,1)}), bf16[16,6,64,128]{3,2,1,0:T(8,128)(2,1)S(1)}, u32[]{:S(2)}, u32[]{:S(2)}) async-start(bf16[16,6,64,128]{3,2,1,0:T(8,128)(2,1)} %shard_map.163), calls=%async_computation | async-start | bytes 3145728 | tf_op jit(solution)/shard_map/all_to_all | solution.py:337
  15.7 3.6 %collective-permute-start = (bf16[256,512]{1,0:T(8,128)(2,1)}, bf16[256,512]{1,0:T(8,128)(2,1)}, u32[]{:S(2)}, u32[]{:S(2)}) collective-permute-start(bf16[256,512]{1,0:T(8,128)(2,1)} %bitcast.13), channel_id=1, source_target_pairs={{0,0},{1,1},{2,16},{3,17},{4,4},{5,5},{6,20},{7,21},{8,8},{9,9},{1... | collective-permute-start | bytes 786440 | tf_op jit(solution)/shard_map/ppermute | solution.py:29
  23.3 12.4 %all-to-all-done.received = bf16[16,6,64,128]{3,2,1,0:T(8,128)(2,1)S(1)} async-done(((bf16[16,6,64,128]{3,2,1,0:T(8,128)(2,1)}), bf16[16,6,64,128]{3,2,1,0:T(8,128)(2,1)S(1)}, u32[]{:S(2)}, u32[]{:S(2)}) %all-to-all-start) | async-done | bytes 1572896 | tf_op jit(solution)/shard_map/all_to_all | solution.py:337
  37.8 4.6 %all-to-all-start.1 = ((f32[8,1,640]{2,1,0:T(1,128)}), f32[8,1,640]{2,1,0:T(1,128)S(1)}, u32[]{:S(2)}, u32[]{:S(2)}) async-start(f32[8,1,640]{2,1,0:T(1,128)} %broadcast_in_dim.10), calls=%async_computation.1 | async-start | bytes 40960 | tf_op jit(solution)/shard_map/all_to_all | solution.py:58
  52.6 6.3 %collective-permute-done.2 = bf16[512,512]{1,0:T(8,128)(2,1)S(1)} collective-permute-done((bf16[512,512]{1,0:T(8,128)(2,1)}, bf16[512,512]{1,0:T(8,128)(2,1)S(1)}, u32[]{:S(2)}, u32[]{:S(2)}) %collective-permute-start.2) | collective-permute-done | bytes 524320 | tf_op jit(solution)/shard_map/ppermute | solution.py:29
  60.7 10.5 %collective-permute-start.4 = (bf16[512,512]{1,0:T(8,128)(2,1)}, bf16[512,512]{1,0:T(8,128)(2,1)S(1)}, u32[]{:S(2)}, u32[]{:S(2)}) collective-permute-start(bf16[512,512]{1,0:T(8,128)(2,1)} %pad_maximum_fusion.4), channel_id=1, source_target_pairs={{0,4},{1,5},{2,6},{3,7},{4,8},{5,9},{6,10},{7,11},{8,12},{9,13},{1... | collective-permute-start | bytes 1572872 | tf_op jit(solution)/shard_map/ppermute | solution.py:29
  71.2 10.5 %collective-permute-done.4 = bf16[512,512]{1,0:T(8,128)(2,1)S(1)} collective-permute-done((bf16[512,512]{1,0:T(8,128)(2,1)}, bf16[512,512]{1,0:T(8,128)(2,1)S(1)}, u32[]{:S(2)}, u32[]{:S(2)}) %collective-permute-start.4) | collective-permute-done | bytes 524320 | tf_op jit(solution)/shard_map/ppermute | solution.py:29
  84.9 3.9 %collective-permute-start.9 = (bf16[4,512,512]{2,1,0:T(8,128)(2,1)S(1)}, bf16[4,512,512]{2,1,0:T(8,128)(2,1)}, u32[]{:S(2)}, u32[]{:S(2)}) collective-permute-start(bf16[4,512,512]{2,1,0:T(8,128)(2,1)S(1)} %pad_maximum_fusion.near), channel_id=1, source_target_pairs={{0,1},{1,0},{2,3},{3,2},{4,5},{5,4},{6,7},{7,6},{8,9},{9,8},{10,11... | collective-permute-start | bytes 6291464 | tf_op jit(solution)/shard_map/ppermute | solution.py:29
  92.1 9.7 %all-to-all-start.3 = ((bf16[16,64,512]{2,1,0:T(8,128)(2,1)}), bf16[16,64,512]{2,1,0:T(8,128)(2,1)}, u32[]{:S(2)}, u32[]{:S(2)}) async-start(bf16[16,64,512]{2,1,0:T(8,128)(2,1)} %bitcast.93), calls=%async_computation.3 | async-start | bytes 2097152 | tf_op jit(solution)/shard_map/all_to_all | solution.py:382
  110.1 9.0 %all-to-all-done.3 = bf16[16,64,512]{2,1,0:T(8,128)(2,1)} async-done(((bf16[16,64,512]{2,1,0:T(8,128)(2,1)}), bf16[16,64,512]{2,1,0:T(8,128)(2,1)}, u32[]{:S(2)}, u32[]{:S(2)}) %all-to-all-start.3) | async-done | bytes 1048608 | tf_op jit(solution)/shard_map/all_to_all | solution.py:382
  122.6 3.3 %shard_map.165.rest_0_ = f32[512,640]{1,0:T(8,128)S(1)} custom-call(s32[3]{0:T(128)S(1)} %get-tuple-element.86.place, bf16[4,512,512]{2,1,0:T(8,128)(2,1)S(1)} %pad_maximum_fusion.near, bf16[4,512,512]{2,1,0:T(8,128)(2,1)} %collective-permute-done.9.far, f32[512,1]{1,0:T(8,128)S(1)} %copy.47.inverse, f32[4,2,1,512]{3,2,1,0:T(1,128)S(1)} %dynamic-slice_bitcast_fusion.1.gain, ...), custom_call_target="tpu_custom_call" | custom-call | flops 1073741824 | bytes 4194304 | tf_op jit(solution)/shard_map/pallas_call | solution.py:176
  132.4 3.4 %shard_map.168 = f32[512,640]{1,0:T(8,128)S(1)} custom-call(s32[3]{0:T(128)S(1)} %add_add_fusion.1.place, bf16[4,512,512]{2,1,0:T(8,128)(2,1)S(1)} %pad_maximum_fusion.near, bf16[4,512,512]{2,1,0:T(8,128)(2,1)} %collective-permute-done.9.far, f32[512,1]{1,0:T(8,128)S(1)} %copy.47.inverse, f32[4,2,1,512]{3,2,1,0:T(1,128)S(1)} %dynamic-slice_bitcast_fusion.1.gain, ...), custom_call_target="tpu_custom_call" | custom-call | flops 1073741824 | bytes 4194304 | tf_op jit(solution)/shard_map/pallas_call | solution.py:176
  137.5 3.4 %all-to-all-start.4 = ((f32[8,1,512]{2,1,0:T(1,128)}), f32[8,1,512]{2,1,0:T(1,128)S(1)}, u32[]{:S(2)}, u32[]{:S(2)}) async-start(f32[8,1,512]{2,1,0:T(1,128)} %broadcast_in_dim.11), calls=%async_computation.4 | async-start | bytes 32768 | tf_op jit(solution)/shard_map/all_to_all | solution.py:58
  150.2 8.3 %collective-permute-done.13 = f32[256,640]{1,0:T(8,128)} collective-permute-done((f32[256,640]{1,0:T(8,128)}, f32[256,640]{1,0:T(8,128)}, u32[]{:S(2)}, u32[]{:S(2)}) %collective-permute-start.13) | collective-permute-done | bytes 655392 | tf_op jit(solution)/shard_map/ppermute | solution.py:29
  162.5 6.2 %all-to-all-start.2 = ((bf16[16,16,640]{2,1,0:T(8,128)(2,1)}), bf16[16,16,640]{2,1,0:T(8,128)(2,1)S(1)}, u32[]{:S(2)}, u32[]{:S(2)}) async-start(bf16[16,16,640]{2,1,0:T(8,128)(2,1)} %reshape.60), calls=%async_computation.2 | async-start | bytes 655360 | tf_op jit(solution)/shard_map/all_to_all | solution.py:422
  169.4 8.9 %all-to-all-done.2.every = bf16[16,16,640]{2,1,0:T(8,128)(2,1)S(1)} async-done(((bf16[16,16,640]{2,1,0:T(8,128)(2,1)}), bf16[16,16,640]{2,1,0:T(8,128)(2,1)S(1)}, u32[]{:S(2)}, u32[]{:S(2)}) %all-to-all-start.2) | async-done | bytes 327712 | tf_op jit(solution)/shard_map/all_to_all | solution.py:422
  179.0 14.8 %shard_map.169 = bf16[8,16,1024]{2,1,0:T(8,128)(2,1)} custom-call(s32[2]{0:T(128)} %pad_add_fusion.place, s32[4]{0:T(128)} %lengths.1, bf16[16,16,640]{2,1,0:T(8,128)(2,1)} %copy-done.20, bf16[4,8,1024,128]{3,2,1,0:T(8,128)(2,1)} %keys.1, bf16[4,8,1024,128]{3,2,1,0:T(8,128)(2,1)} %values.1), custom_call_target="tpu_custom_call" | custom-call | flops 536870912 | bytes 16777216 | tf_op jit(solution)/shard_map/pallas_call | solution.py:230
  193.9 4.3 %collective-permute-done.16.rows_3 = bf16[1024,512]{1,0:T(8,128)(2,1)} collective-permute-done((bf16[1024,512]{1,0:T(8,128)(2,1)S(1)}, bf16[1024,512]{1,0:T(8,128)(2,1)}, u32[]{:S(2)}, u32[]{:S(2)}) %collective-permute-start.16) | collective-permute-done | bytes 1048608 | tf_op jit(solution)/shard_map/ppermute | solution.py:29
  213.2 6.6 %collective-permute-done.22 = bf16[4,2,16,1024]{3,2,1,0:T(8,128)(2,1)S(1)} collective-permute-done((bf16[4,2,16,1024]{3,2,1,0:T(8,128)(2,1)S(1)}, bf16[4,2,16,1024]{3,2,1,0:T(8,128)(2,1)S(1)}, u32[]{:S(2)}, u32[]{:S(2)}) %collective-permute-start.22) | collective-permute-done | bytes 262176 | tf_op jit(solution)/shard_map/ppermute | solution.py:29
  219.9 4.2 %collective-permute-start.26 = (bf16[4,2,16,1024]{3,2,1,0:T(8,128)(2,1)S(1)}, bf16[4,2,16,1024]{3,2,1,0:T(8,128)(2,1)S(1)}, u32[]{:S(2)}, u32[]{:S(2)}) collective-permute-start(bf16[4,2,16,1024]{3,2,1,0:T(8,128)(2,1)S(1)} %get-tuple-element.72), channel_id=1, source_target_pairs={{0,2},{1,3},{2,0},{3,1},{4,6},{5,7},{6,4},{7,5},{8,10},{9,11},{10,... | collective-permute-start | bytes 786440 | tf_op jit(solution)/shard_map/ppermute | solution.py:29
  226.0 4.1 %collective-permute-done.26 = bf16[4,2,16,1024]{3,2,1,0:T(8,128)(2,1)S(1)} collective-permute-done((bf16[4,2,16,1024]{3,2,1,0:T(8,128)(2,1)S(1)}, bf16[4,2,16,1024]{3,2,1,0:T(8,128)(2,1)S(1)}, u32[]{:S(2)}, u32[]{:S(2)}) %collective-permute-start.26) | collective-permute-done | bytes 262176 | tf_op jit(solution)/shard_map/ppermute | solution.py:29
  235.7 4.4 %shard_map.170 = (f32[16,16,512]{2,1,0:T(8,128)S(1)}, bf16[16,16,512]{2,1,0:T(8,128)(2,1)S(1)}) custom-call(s32[3]{0:T(128)S(1)} %add_add_fusion.place, bf16[4,4,2,16,1024]{4,3,2,1,0:T(8,128)(2,1)S(1)} %pad_maximum_fusion.2.near_a, bf16[4,4,2,16,1024]{4,3,2,1,0:T(8,128)(2,1)S(1)} %pad_maximum_fusion.3.near_b, ...), custom_call_target="tpu_custom_call" | custom-call | flops 2147483648 | bytes 8388608 | tf_op jit(solution)/shard_map/pallas_call | solution.py:280
  240.3 7.5 %collective-permute-done.31 = bf16[16,16,512]{2,1,0:T(8,128)(2,1)S(1)} collective-permute-done((bf16[16,16,512]{2,1,0:T(8,128)(2,1)S(1)}, bf16[16,16,512]{2,1,0:T(8,128)(2,1)S(1)}, u32[]{:S(2)}, u32[]{:S(2)}) %collective-permute-start.31) | collective-permute-done | bytes 262176 | tf_op jit(solution)/shard_map/ppermute | solution.py:29
  (155 shorter events, 85.5 us)
Async XLA Ops:
  3.7 32.0 %all-to-all-start = ((bf16[16,6,64,128]{3,2,1,0:T(8,128)(2,1)}), bf16[16,6,64,128]{3,2,1,0:T(8,128)(2,1)S(1)}, u32[]{:S(2)}, u32[]{:S(2)}) async-start(bf16[16,6,64,128]{3,2,1,0:T(8,128)(2,1)} %shard_map.163), calls=%async_computation | async-start | bytes 3145728 | tf_op jit(solution)/shard_map/all_to_all | solution.py:337
  12.8 29.6 %collective-permute-start.1 = (bf16[256,512]{1,0:T(8,128)(2,1)}, bf16[256,512]{1,0:T(8,128)(2,1)}, u32[]{:S(2)}, u32[]{:S(2)}) collective-permute-start(bf16[256,512]{1,0:T(8,128)(2,1)} %bitcast.13), channel_id=1, source_target_pairs={{0,2},{1,3},{2,18},{3,19},{4,6},{5,7},{6,22},{7,23},{8,10},{9,11},... | collective-permute-start | bytes 786440 | tf_op jit(solution)/shard_map/ppermute | solution.py:29
  15.7 26.7 %collective-permute-start = (bf16[256,512]{1,0:T(8,128)(2,1)}, bf16[256,512]{1,0:T(8,128)(2,1)}, u32[]{:S(2)}, u32[]{:S(2)}) collective-permute-start(bf16[256,512]{1,0:T(8,128)(2,1)} %bitcast.13), channel_id=1, source_target_pairs={{0,0},{1,1},{2,16},{3,17},{4,4},{5,5},{6,20},{7,21},{8,8},{9,9},{1... | collective-permute-start | bytes 786440 | tf_op jit(solution)/shard_map/ppermute | solution.py:29
  48.2 12.5 %collective-permute-start.3 = (bf16[512,512]{1,0:T(8,128)(2,1)}, bf16[512,512]{1,0:T(8,128)(2,1)S(1)}, u32[]{:S(2)}, u32[]{:S(2)}) collective-permute-start(bf16[512,512]{1,0:T(8,128)(2,1)} %pad_maximum_fusion.4), channel_id=1, source_target_pairs={{0,8},{1,9},{2,10},{3,11},{4,12},{5,13},{6,14},{7,15},{8,0},{9,1},... | collective-permute-start | bytes 1572872 | tf_op jit(solution)/shard_map/ppermute | solution.py:29
  49.2 33.4 %collective-permute-start.5 = (bf16[6,512,128]{2,1,0:T(8,128)(2,1)S(1)}, bf16[6,512,128]{2,1,0:T(8,128)(2,1)}, u32[]{:S(2)}, u32[]{:S(2)}) collective-permute-start(bf16[6,512,128]{2,1,0:T(8,128)(2,1)S(1)} %get-tuple-element.44.block_a), channel_id=1, source_target_pairs={{0,96},{1,97},{2,98},{3,99},{4,100},{5,101},{6,102},{7,103},{8,104... | collective-permute-start | bytes 2359304 | tf_op jit(solution)/shard_map/ppermute | solution.py:29
  50.0 32.6 %collective-permute-start.7 = (bf16[6,512,128]{2,1,0:T(8,128)(2,1)S(1)}, bf16[6,512,128]{2,1,0:T(8,128)(2,1)S(1)}, u32[]{:S(2)}, u32[]{:S(2)}) collective-permute-start(bf16[6,512,128]{2,1,0:T(8,128)(2,1)S(1)} %get-tuple-element.44.block_a), channel_id=1, source_target_pairs={{0,32},{1,33},{2,34},{3,35},{4,36},{5,37},{6,38},{7,39},{8,40},{9,... | collective-permute-start | bytes 2359304 | tf_op jit(solution)/shard_map/ppermute | solution.py:29
  50.7 31.0 %collective-permute-start.6 = (bf16[5,512,128]{2,1,0:T(8,128)(2,1)}, bf16[5,512,128]{2,1,0:T(8,128)(2,1)S(1)}, u32[]{:S(2)}, u32[]{:S(2)}) collective-permute-start(bf16[5,512,128]{2,1,0:T(8,128)(2,1)} %copy-done.7), channel_id=1, source_target_pairs={{0,96},{1,97},{2,98},{3,99},{4,100},{5,101},{6,102},{7,103},{8,104... | collective-permute-start | bytes 1966088 | tf_op jit(solution)/shard_map/ppermute | solution.py:29
  58.9 23.7 %collective-permute-start.8 = (bf16[5,512,128]{2,1,0:T(8,128)(2,1)}, bf16[5,512,128]{2,1,0:T(8,128)(2,1)}, u32[]{:S(2)}, u32[]{:S(2)}) collective-permute-start(bf16[5,512,128]{2,1,0:T(8,128)(2,1)} %copy-done.7), channel_id=1, source_target_pairs={{0,32},{1,33},{2,34},{3,35},{4,36},{5,37},{6,38},{7,39},{8,40},{9,... | collective-permute-start | bytes 1966088 | tf_op jit(solution)/shard_map/ppermute | solution.py:29
  60.7 21.0 %collective-permute-start.4 = (bf16[512,512]{1,0:T(8,128)(2,1)}, bf16[512,512]{1,0:T(8,128)(2,1)S(1)}, u32[]{:S(2)}, u32[]{:S(2)}) collective-permute-start(bf16[512,512]{1,0:T(8,128)(2,1)} %pad_maximum_fusion.4), channel_id=1, source_target_pairs={{0,4},{1,5},{2,6},{3,7},{4,8},{5,9},{6,10},{7,11},{8,12},{9,13},{1... | collective-permute-start | bytes 1572872 | tf_op jit(solution)/shard_map/ppermute | solution.py:29
  84.9 21.9 %collective-permute-start.9 = (bf16[4,512,512]{2,1,0:T(8,128)(2,1)S(1)}, bf16[4,512,512]{2,1,0:T(8,128)(2,1)}, u32[]{:S(2)}, u32[]{:S(2)}) collective-permute-start(bf16[4,512,512]{2,1,0:T(8,128)(2,1)S(1)} %pad_maximum_fusion.near), channel_id=1, source_target_pairs={{0,1},{1,0},{2,3},{3,2},{4,5},{5,4},{6,7},{7,6},{8,9},{9,8},{10,11... | collective-permute-start | bytes 6291464 | tf_op jit(solution)/shard_map/ppermute | solution.py:29
  92.1 27.0 %all-to-all-start.3 = ((bf16[16,64,512]{2,1,0:T(8,128)(2,1)}), bf16[16,64,512]{2,1,0:T(8,128)(2,1)}, u32[]{:S(2)}, u32[]{:S(2)}) async-start(bf16[16,64,512]{2,1,0:T(8,128)(2,1)} %bitcast.93), calls=%async_computation.3 | async-start | bytes 2097152 | tf_op jit(solution)/shard_map/all_to_all | solution.py:382
  105.3 27.1 %collective-permute-start.11 = (bf16[6,512,128]{2,1,0:T(8,128)(2,1)}, bf16[6,512,128]{2,1,0:T(8,128)(2,1)}, u32[]{:S(2)}, u32[]{:S(2)}) collective-permute-start(bf16[6,512,128]{2,1,0:T(8,128)(2,1)} %collective-permute-done.5.block_a), channel_id=1, source_target_pairs={{0,96},{1,97},{2,98},{3,99},{4,100},{5,101},{6,102},{7,103},{8,104... | collective-permute-start | bytes 2359304 | tf_op jit(solution)/shard_map/ppermute | solution.py:29
  106.8 25.6 %collective-permute-start.12 = (bf16[5,512,128]{2,1,0:T(8,128)(2,1)}, bf16[5,512,128]{2,1,0:T(8,128)(2,1)}, u32[]{:S(2)}, u32[]{:S(2)}) collective-permute-start(bf16[5,512,128]{2,1,0:T(8,128)(2,1)} %collective-permute-done.8.block_b), channel_id=1, source_target_pairs={{0,32},{1,33},{2,34},{3,35},{4,36},{5,37},{6,38},{7,39},{8,40},{9,... | collective-permute-start | bytes 1966088 | tf_op jit(solution)/shard_map/ppermute | solution.py:29
  109.1 12.2 %collective-permute-start.10 = (f32[512]{0:T(512)S(1)}, f32[512]{0:T(512)S(1)}, u32[]{:S(2)}, u32[]{:S(2)}) collective-permute-start(f32[512]{0:T(512)S(1)} %add_reduce_fusion), channel_id=1, source_target_pairs={{0,16},{1,17},{2,18},{3,19},{4,20},{5,21},{6,22},{7,23},{8,24},{9,... | collective-permute-start | bytes 6152 | tf_op jit(solution)/shard_map/ppermute | solution.py:29
  142.9 15.6 %collective-permute-start.13 = (f32[256,640]{1,0:T(8,128)}, f32[256,640]{1,0:T(8,128)}, u32[]{:S(2)}, u32[]{:S(2)}) collective-permute-start(f32[256,640]{1,0:T(8,128)} %dynamic-slice_bitcast_fusion), channel_id=1, source_target_pairs={{0,16},{1,17},{2,18},{3,19},{4,20},{5,21},{6,22},{7,23},{8,24},{9,... | collective-permute-start | bytes 1966088 | tf_op jit(solution)/shard_map/ppermute | solution.py:29
  148.1 45.8 %collective-permute-start.14 = (bf16[1024,512]{1,0:T(8,128)(2,1)S(1)}, bf16[1024,512]{1,0:T(8,128)(2,1)S(1)}, u32[]{:S(2)}, u32[]{:S(2)}) collective-permute-start(bf16[1024,512]{1,0:T(8,128)(2,1)S(1)} %fusion.1.rows_0), channel_id=1, source_target_pairs={{0,96},{1,97},{2,98},{3,99},{4,100},{5,101},{6,102},{7,103},{8,104... | collective-permute-start | bytes 3145736 | tf_op jit(solution)/shard_map/ppermute | solution.py:29
  149.0 44.8 %collective-permute-start.15 = (bf16[1024,512]{1,0:T(8,128)(2,1)S(1)}, bf16[1024,512]{1,0:T(8,128)(2,1)}, u32[]{:S(2)}, u32[]{:S(2)}) collective-permute-start(bf16[1024,512]{1,0:T(8,128)(2,1)S(1)} %fusion.1.rows_0), channel_id=1, source_target_pairs={{0,64},{1,65},{2,66},{3,67},{4,68},{5,69},{6,70},{7,71},{8,72},{9,... | collective-permute-start | bytes 3145736 | tf_op jit(solution)/shard_map/ppermute | solution.py:29
  150.2 48.0 %collective-permute-start.16 = (bf16[1024,512]{1,0:T(8,128)(2,1)S(1)}, bf16[1024,512]{1,0:T(8,128)(2,1)}, u32[]{:S(2)}, u32[]{:S(2)}) collective-permute-start(bf16[1024,512]{1,0:T(8,128)(2,1)S(1)} %fusion.1.rows_0), channel_id=1, source_target_pairs={{0,32},{1,33},{2,34},{3,35},{4,36},{5,37},{6,38},{7,39},{8,40},{9,... | collective-permute-start | bytes 3145736 | tf_op jit(solution)/shard_map/ppermute | solution.py:29
  162.5 15.8 %all-to-all-start.2 = ((bf16[16,16,640]{2,1,0:T(8,128)(2,1)}), bf16[16,16,640]{2,1,0:T(8,128)(2,1)S(1)}, u32[]{:S(2)}, u32[]{:S(2)}) async-start(bf16[16,16,640]{2,1,0:T(8,128)(2,1)} %reshape.60), calls=%async_computation.2 | async-start | bytes 655360 | tf_op jit(solution)/shard_map/all_to_all | solution.py:422
  207.1 12.8 %collective-permute-start.22 = (bf16[4,2,16,1024]{3,2,1,0:T(8,128)(2,1)S(1)}, bf16[4,2,16,1024]{3,2,1,0:T(8,128)(2,1)S(1)}, u32[]{:S(2)}, u32[]{:S(2)}) collective-permute-start(bf16[4,2,16,1024]{3,2,1,0:T(8,128)(2,1)S(1)} %get-tuple-element.77), channel_id=1, source_target_pairs={{0,4},{1,5},{2,6},{3,7},{4,8},{5,9},{6,10},{7,11},{8,12},{9,13},{1... | collective-permute-start | bytes 786440 | tf_op jit(solution)/shard_map/ppermute | solution.py:29
  207.4 16.6 %collective-permute-start.21 = (bf16[4,2,16,1024]{3,2,1,0:T(8,128)(2,1)S(1)}, bf16[4,2,16,1024]{3,2,1,0:T(8,128)(2,1)S(1)}, u32[]{:S(2)}, u32[]{:S(2)}) collective-permute-start(bf16[4,2,16,1024]{3,2,1,0:T(8,128)(2,1)S(1)} %get-tuple-element.77), channel_id=1, source_target_pairs={{0,8},{1,9},{2,10},{3,11},{4,12},{5,13},{6,14},{7,15},{8,0},{9,1},... | collective-permute-start | bytes 786440 | tf_op jit(solution)/shard_map/ppermute | solution.py:29
  211.2 12.9 %collective-permute-start.20 = (bf16[4,2,16,1024]{3,2,1,0:T(8,128)(2,1)S(1)}, bf16[4,2,16,1024]{3,2,1,0:T(8,128)(2,1)S(1)}, u32[]{:S(2)}, u32[]{:S(2)}) collective-permute-start(bf16[4,2,16,1024]{3,2,1,0:T(8,128)(2,1)S(1)} %get-tuple-element.77), channel_id=1, source_target_pairs={{0,12},{1,13},{2,14},{3,15},{4,0},{5,1},{6,2},{7,3},{8,4},{9,5},{1... | collective-permute-start | bytes 786440 | tf_op jit(solution)/shard_map/ppermute | solution.py:29
  213.1 12.9 %collective-permute-start.28 = (bf16[4,2,16,1024]{3,2,1,0:T(8,128)(2,1)S(1)}, bf16[4,2,16,1024]{3,2,1,0:T(8,128)(2,1)S(1)}, u32[]{:S(2)}, u32[]{:S(2)}) collective-permute-start(bf16[4,2,16,1024]{3,2,1,0:T(8,128)(2,1)S(1)} %get-tuple-element.73), channel_id=1, source_target_pairs={{0,18},{1,19},{2,16},{3,17},{4,22},{5,23},{6,20},{7,21},{8,26},{9,... | collective-permute-start | bytes 786440 | tf_op jit(solution)/shard_map/ppermute | solution.py:29
  213.1 12.8 %collective-permute-start.27 = (bf16[4,2,16,1024]{3,2,1,0:T(8,128)(2,1)S(1)}, bf16[4,2,16,1024]{3,2,1,0:T(8,128)(2,1)S(1)}, u32[]{:S(2)}, u32[]{:S(2)}) collective-permute-start(bf16[4,2,16,1024]{3,2,1,0:T(8,128)(2,1)S(1)} %get-tuple-element.73), channel_id=1, source_target_pairs={{0,16},{1,17},{2,18},{3,19},{4,20},{5,21},{6,22},{7,23},{8,24},{9,... | collective-permute-start | bytes 786440 | tf_op jit(solution)/shard_map/ppermute | solution.py:29
  (34 other events, 353.4 us)

commit v2 on v1

v2 whole, which is shorter than its diff:
```python
import math

import jax
import jax.numpy as jnp
from jax import lax
from jax.experimental import pallas as pl
from jax.experimental.pallas import tpu as pltpu
from jax.sharding import PartitionSpec as P

EPSILON = 1e-06
NEG_LARGE = -1e30
AXES = ("rep", "tp")


def device_index(y, zl, x, zh, c):
    return (y * 2 + zl) * 16 + x * 4 + zh * 2 + c


def permute(value, target):
    pairs = []
    for y in range(4):
        for zl in range(2):
            for x in range(4):
                for zh in range(2):
                    for c in range(2):
                        pairs.append(
                            (device_index(y, zl, x, zh, c), device_index(*target(y, zl, x, zh, c)))
                        )
    return lax.ppermute(value, AXES, pairs)


def swap_low(value):
    return permute(value, lambda y, zl, x, zh, c: (y, 1 - zl, x, zh, c))


def swap_core(value):
    return permute(value, lambda y, zl, x, zh, c: (y, zl, x, zh, 1 - c))


def from_y(value, step):
    return permute(value, lambda y, zl, x, zh, c: ((y - step) % 4, zl, x, zh, c))


def from_x(value, step):
    return permute(value, lambda y, zl, x, zh, c: (y, zl, (x - step) % 4, zh, c))


def after(value, earlier):
    return lax.optimization_barrier((value, earlier))[0]


def pick(value, index, axis=0):
    return lax.dynamic_index_in_dim(value, index, axis, keepdims=False)


def share_sums(sums):
    spread = jnp.broadcast_to(sums[None, :], (8, sums.shape[0]))
    return jnp.sum(lax.all_to_all(spread, "rep", 0, 0, tiled=True), axis=0)


def pack_columns_kernel(place, query, key_value, output, down_q, down_kv, down_o, out):
    f32 = jnp.float32
    down_q, down_kv, down_o = (d[...].astype(f32) for d in (down_q, down_kv, down_o))
    blank = jnp.zeros_like(down_o)
    down = jnp.where(
        place[0] < 8,
        jnp.concatenate([down_q, down_kv, down_o, blank], axis=0),
        jnp.concatenate([down_o, blank, down_q, down_kv], axis=0),
    )
    down = down.T.astype(jnp.bfloat16)
    for i in range(4):
        for k in range(4):
            columns = slice((i * 4 + k) * 128, (i * 4 + k + 1) * 128)
            out[i, k] = query[:, columns]
            out[i, 6 + k] = output[:, columns]
        out[i, 4] = key_value[:, i * 128 : (i + 1) * 128]
        out[i, 5] = down


def pack_columns(place, query, key_value, output, *downs):
    down = pl.BlockSpec((32, 64), lambda i, place: (0, 0))
    return pl.pallas_call(
        pack_columns_kernel,
        grid_spec=pltpu.PrefetchScalarGridSpec(
            num_scalar_prefetch=1,
            grid=(4,),
            in_specs=[
                pl.BlockSpec((64, 2048), lambda i, place: (0, i)),
                pl.BlockSpec((64, 512), lambda i, place: (0, i)),
                pl.BlockSpec((64, 2048), lambda i, place: (0, i)),
                down,
                down,
                down,
            ],
            out_specs=pl.BlockSpec((4, 10, 64, 128), lambda i, place: (i, 0, 0, 0)),
        ),
        out_shape=jax.ShapeDtypeStruct((16, 10, 64, 128), jnp.bfloat16),
        cost_estimate=pl.CostEstimate(flops=0, bytes_accessed=2**22, transcendentals=0),
    )(place, query, key_value, output, *downs)


def unpack_columns_kernel(received, ups, ups_out, block_a, block_b, rows_out, down, out):
    lanes = lax.broadcasted_iota(jnp.int32, (64, 128), 1)
    for i in range(8):
        rows = slice(i * 64, (i + 1) * 64)
        first, second = received[i, 5], received[8 + i, 5]
        down[0, rows] = first
        down[1, rows] = second
        block_a[0, rows] = jnp.where(
            lanes < 64, first.astype(jnp.float32), second.astype(jnp.float32)
        ).astype(jnp.bfloat16)
        for k in range(5):
            block_a[1 + k, rows] = received[i, k]
            block_b[k, rows] = received[8 + i, k]
        for k in range(4):
            for half in range(2):
                rows_out[half, rows, k * 128 : (k + 1) * 128] = received[half * 8 + i, 6 + k]
    total = None
    for half in range(2):
        merged = jnp.dot(block_a[0], ups[half], preferred_element_type=jnp.float32)
        sums = []
        for k in range(5):
            rows = block_a[1 + k] if half == 0 else block_b[k]
            tile = merged[:, k * 128 : (k + 1) * 128] + rows.astype(jnp.float32)
            sums.append(jnp.sum(tile * tile, axis=0, keepdims=True))
        merged = jnp.dot(down[half], ups_out[half], preferred_element_type=jnp.float32)
        merged = merged + rows_out[half].astype(jnp.float32)
        sums.append(jnp.sum(merged * merged, axis=0, keepdims=True))
        sums = jnp.concatenate(sums, axis=1)
        total = sums if total is None else total + sums
    out[...] = total


def unpack_columns(received, ups, ups_out):
    return pl.pallas_call(
        unpack_columns_kernel,
        out_shape=[
            jax.ShapeDtypeStruct((6, 512, 128), jnp.bfloat16),
            jax.ShapeDtypeStruct((5, 512, 128), jnp.bfloat16),
            jax.ShapeDtypeStruct((2, 512, 512), jnp.bfloat16),
            jax.ShapeDtypeStruct((2, 512, 128), jnp.bfloat16),
            jax.ShapeDtypeStruct((1, 1152), jnp.float32),
        ],
        compiler_params=pltpu.CompilerParams(vmem_limit_bytes=24 * 2**20),
        cost_estimate=pl.CostEstimate(flops=2**28, bytes_accessed=2**22, transcendentals=0),
    )(received, ups, ups_out)


def scale_rows_kernel(rows, down, ups, factor, out_a, out_b):
    for half, out in enumerate((out_a, out_b)):
        merged = jnp.dot(down[half], ups[half], preferred_element_type=jnp.float32)
        merged = rows[half].astype(jnp.float32) + merged
        out[...] = (merged * factor[...]).astype(jnp.bfloat16)


def scale_rows(rows, down, ups, factor):
    return pl.pallas_call(
        scale_rows_kernel,
        out_shape=[jax.ShapeDtypeStruct((512, 512), jnp.bfloat16)] * 2,
        compiler_params=pltpu.CompilerParams(vmem_limit_bytes=56 * 2**20),
        cost_estimate=pl.CostEstimate(flops=2**20, bytes_accessed=2**12, transcendentals=0),
    )(rows, down, ups, factor)


def token_sums_kernel(near, out):
    total = None
    for e in range(4):
        wide = near[e].astype(jnp.float32)
        part = jnp.sum(wide * wide, axis=1, keepdims=True)
        total = part if total is None else total + part
    out[...] = total


def token_sums(near):
    return pl.pallas_call(
        token_sums_kernel,
        out_shape=jax.ShapeDtypeStruct((512, 1), jnp.float32),
        compiler_params=pltpu.CompilerParams(vmem_limit_bytes=56 * 2**20),
        cost_estimate=pl.CostEstimate(flops=2**20, bytes_accessed=2**12, transcendentals=0),
    )(near)


def multiply_slabs_kernel(place, *refs):
    count = (place.shape[0] - 2) // 2
    slabs, refs = refs[: 3 * count], refs[3 * count :]
    inverse, ups, factor = refs[:3]
    blocks, rest = refs[3 : 3 + 2 * count], refs[3 + 2 * count :]
    value = None
    for i in range(count):
        near, far, gain = slabs[3 * i : 3 * i + 3]
        block_a, block_b = blocks[2 * i : 2 * i + 2]
        for half in range(2):
            tokens = jnp.where(place[2 * count] == half, near[0], far[0]).astype(jnp.float32)
            normed = (tokens * inverse[...] * gain[0, half]).astype(jnp.bfloat16)
            merged = jnp.dot(block_a[0], ups[half], preferred_element_type=jnp.float32)
            tiles = []
            for k in range(5):
                rows = block_a[1 + k] if half == 0 else block_b[k]
                tiles.append(merged[:, k * 128 : (k + 1) * 128] + rows.astype(jnp.float32))
            weight = (jnp.concatenate(tiles, axis=1) * factor[...]).astype(jnp.bfloat16)
            part = jnp.dot(normed, weight, preferred_element_type=jnp.float32)
            value = part if value is None else value + part
    if len(rest) == 1:
        rest[0][...] = value
    else:
        value = value + rest[0][...]
        swapped = place[2 * count + 1] == 1
        rest[1][...] = jnp.where(swapped, value[:256], value[256:])
        rest[2][...] = jnp.where(swapped, value[256:], value[:256])


def multiply_slabs(place, near, far, inverse, gains, blocks, ups, factor, total):
    count = len(blocks) // 2

    def whole(shape):
        return pl.BlockSpec(shape, lambda i, place: (0,) * len(shape))

    operands, specs = [], []
    for k in range(count):
        operands += [near, far, gains]
        specs += [pl.BlockSpec((1, 512, 512), lambda i, place, k=k: (place[k], 0, 0))] * 2
        specs.append(
            pl.BlockSpec((1, 2, 1, 512), lambda i, place, k=k: (place[count + k], 0, 0, 0))
        )
    rest = [inverse, ups, factor, *blocks] + ([] if total is None else [total])
    operands += rest
    specs += [whole(operand.shape) for operand in rest]
    rows = 512 if total is None else 256
    shape = jax.ShapeDtypeStruct((rows, 640), jnp.float32)
    return pl.pallas_call(
        multiply_slabs_kernel,
        grid_spec=pltpu.PrefetchScalarGridSpec(
            num_scalar_prefetch=1,
            grid=(1,),
            in_specs=specs,
            out_specs=whole((rows, 640)) if total is None else [whole((rows, 640))] * 2,
        ),
        out_shape=shape if total is None else [shape] * 2,
        compiler_params=pltpu.CompilerParams(vmem_limit_bytes=56 * 2**20),
        cost_estimate=pl.CostEstimate(
            flops=2**20, bytes_accessed=2**12, transcendentals=0
        ),
    )(place, *operands)


def attend_kernel(place, lengths, every, keys, values, out):
    f32, bf16 = jnp.float32, jnp.bfloat16
    inv_root = 1.0 / math.sqrt(128)
    both = every[...].astype(f32)
    fresh_keys = every[0, :, 512:]
    fresh_values = every[1, :, 512:]
    contract_last = (((1,), (1,)), ((), ()))
    fresh_column = lax.broadcasted_iota(jnp.int32, (128, 16), 1)
    fresh_row = lax.broadcasted_iota(jnp.int32, (128, 16), 0)
    slots = lax.broadcasted_iota(jnp.int32, (32, 1024), 1)
    blank = jnp.zeros((32, 128), bf16)
    queries = [
        jnp.concatenate(
            [
                both[h // 4, b * 4 : b * 4 + 4, (h % 4) * 128 : (h % 4 + 1) * 128]
                for h in range(8)
            ],
            axis=0,
        ).astype(bf16)
        for b in range(4)
    ]
    fresh = lax.dot_general(
        jnp.concatenate(queries, axis=0), fresh_keys, contract_last, preferred_element_type=f32
    )
    own = (fresh_row // 32) * 4
    order = (fresh_column >= own) & (fresh_column - own <= fresh_row % 4)
    fresh = jnp.where(order, fresh * inv_root, NEG_LARGE)
    scores = []
    for b in (0, 2):
        query = jnp.concatenate(
            [
                jnp.concatenate([queries[b], blank], axis=1),
                jnp.concatenate([blank, queries[b + 1]], axis=1),
            ],
            axis=0,
        )
        key = jnp.concatenate([keys[b, 0], keys[b + 1, 0]], axis=1)
        scores.append(
            lax.dot_general(query, key, contract_last, preferred_element_type=f32)
        )
    live = jnp.concatenate([slots < lengths[b] for b in range(4)], axis=0)
    scores = jnp.where(live, jnp.concatenate(scores, axis=0) * inv_root, NEG_LARGE)
    peak = jnp.maximum(
        jnp.max(scores, axis=1, keepdims=True), jnp.max(fresh, axis=1, keepdims=True)
    )
    probs = jnp.where(live, jnp.exp(scores - peak), 0.0)
    fresh_probs = jnp.where(order, jnp.exp(fresh - peak), 0.0)
    total = jnp.sum(probs, axis=1, keepdims=True) + jnp.sum(fresh_probs, axis=1, keepdims=True)
    rounded = probs.astype(bf16)
    contexts = []
    for b in (0, 2):
        value = jnp.concatenate([values[b, 0], values[b + 1, 0]], axis=1)
        part = jnp.dot(rounded[b * 32 : b * 32 + 64], value, preferred_element_type=f32)
        contexts += [part[:32, :128], part[32:, 128:]]
    context = jnp.concatenate(contexts, axis=0)
    context += jnp.dot(fresh_probs.astype(bf16), fresh_values, preferred_element_type=f32)
    context = context / total
    pieces = [
        jnp.concatenate(
            [context[b * 32 + h * 4 : b * 32 + h * 4 + 4] for h in range(8)], axis=1
        )
        for b in range(4)
    ]
    out[0] = jnp.concatenate(pieces, axis=0).astype(bf16)


def attend(place, lengths, every, cached_key_rows, cached_value_rows):
    def slab(g, place, lengths):
        return (((g + place[1]) % 2) * 4 + (g // 2 + 4 - place[0]) % 4, 0, 0)

    cache = pl.BlockSpec((4, 1, 1024, 128), lambda g, place, lengths: (0, g, 0, 0))
    return pl.pallas_call(
        attend_kernel,
        grid_spec=pltpu.PrefetchScalarGridSpec(
            num_scalar_prefetch=2,
            grid=(8,),
            in_specs=[
                pl.BlockSpec((2, 16, 640), lambda g, place, lengths: (g, 0, 0)),
                cache,
                cache,
            ],
            out_specs=pl.BlockSpec((1, 16, 1024), slab),
        ),
        out_shape=jax.ShapeDtypeStruct((8, 16, 1024), jnp.bfloat16),
        compiler_params=pltpu.CompilerParams(vmem_limit_bytes=56 * 2**20),
        cost_estimate=pl.CostEstimate(flops=2**20, bytes_accessed=2**12, transcendentals=0),
    )(place, lengths, every, cached_key_rows, cached_value_rows)


def output_kernel(place, near_a, near_b, far_a, far_b, *refs):
    weights, (mine, other) = refs[:8], refs[8:]
    total = None
    for j in range(4):
        parts = []
        for first, second in ((near_a, near_b), (far_a, far_b)):
            if j < 2:
                parts.append(first[:, :, j].reshape(256, 1024))
            else:
                parts.extend(second[:, e, j - 2].reshape(64, 1024) for e in range(4))
        rows = jnp.concatenate(parts, axis=0)
        for half in range(2):
            part = jnp.dot(
                rows[:, half * 512 : (half + 1) * 512],
                weights[2 * j + half][...],
                preferred_element_type=jnp.float32,
            )
            total = part if total is None else total + part
    for cr in range(2):
        for e in range(4):
            for dl in range(2):
                for dh in range(2):
                    start = cr * 256 + e * 64 + dl * 32 + dh * 16
                    target = ((place[0] + e) % 4) * 4 + (place[1] ^ dh) * 2 + (place[2] ^ cr)
                    rows = total[start : start + 16]
                    if dl == 0:
                        mine[target] = rows
                    else:
                        other[target] = rows.astype(jnp.bfloat16)


def multiply_output(place, pieces, rows_o):
    def whole(shape):
        return pl.BlockSpec(shape, lambda i, place: (0,) * len(shape))

    operands = [*pieces, *rows_o]
    return pl.pallas_call(
        output_kernel,
        grid_spec=pltpu.PrefetchScalarGridSpec(
            num_scalar_prefetch=1,
            grid=(1,),
            in_specs=[whole(operand.shape) for operand in operands],
            out_specs=[whole((16, 16, 512)), whole((16, 16, 512))],
        ),
        out_shape=[
            jax.ShapeDtypeStruct((16, 16, 512), jnp.float32),
            jax.ShapeDtypeStruct((16, 16, 512), jnp.bfloat16),
        ],
        compiler_params=pltpu.CompilerParams(vmem_limit_bytes=40 * 2**20),
        cost_estimate=pl.CostEstimate(flops=2**31, bytes_accessed=2**23, transcendentals=0),
    )(place, *operands)


def per_device(
    token_hidden_rows,
    input_norm_gain,
    frozen_query,
    frozen_key_value,
    frozen_output,
    query_down_factor,
    query_up_factor,
    key_value_down_factor,
    key_value_up_factor,
    output_down_factor,
    output_up_factor,
    query_column_scale,
    key_value_column_scale,
    output_column_scale,
    cached_key_rows,
    cached_value_rows,
    lengths,
):
    f32, bf16 = jnp.float32, jnp.bfloat16
    r, t = lax.axis_index("rep"), lax.axis_index("tp")
    y, zl = r // 2, r % 2
    x, zh, c = t // 4, (t // 2) % 2, t % 2

    local = token_hidden_rows.transpose(1, 0, 2).reshape(256, 512)
    pair = jnp.concatenate(
        [
            permute(local, lambda y, zl, x, zh, c, s=s: (y, zh, x, zl ^ s, c))
            for s in range(2)
        ]
    )

    frozen = pack_columns(
        t.astype(jnp.int32).reshape(1),
        frozen_query,
        frozen_key_value,
        frozen_output,
        query_down_factor.T,
        key_value_down_factor.T,
        output_down_factor.T,
    )
    received = lax.all_to_all(frozen, "tp", 0, 0, tiled=True)

    up_q = lax.dynamic_slice_in_dim(query_up_factor, t * 512, 512, 1)
    up_kv = lax.dynamic_slice_in_dim(key_value_up_factor, t * 128, 128, 1)
    up_o = lax.dynamic_slice_in_dim(output_up_factor, t * 512, 512, 1)
    up_qkv = jnp.concatenate(
        [
            jnp.concatenate([up_q, jnp.zeros((32, 128), bf16)], axis=1),
            jnp.concatenate([jnp.zeros((32, 512), bf16), up_kv], axis=1),
        ],
        axis=0,
    )
    blank = jnp.zeros((64, 640), bf16)
    ups = jnp.stack(
        [jnp.concatenate([up_qkv, blank], axis=0), jnp.concatenate([blank, up_qkv], axis=0)]
    )
    blank = jnp.zeros((32, 512), bf16)
    ups_out = jnp.stack(
        [
            jnp.concatenate([blank, blank, up_o, blank]),
            jnp.concatenate([up_o, blank, blank, blank]),
        ]
    )
    scale_qkv = jnp.concatenate(
        [
            lax.dynamic_slice_in_dim(query_column_scale, t * 512, 512, 0),
            lax.dynamic_slice_in_dim(key_value_column_scale, t * 128, 128, 0),
        ]
    )
    scale_out = lax.dynamic_slice_in_dim(output_column_scale, t * 512, 512, 0)

    received, ups, ups_out, scale_qkv, scale_out = lax.optimization_barrier(
        (received, ups, ups_out, scale_qkv, scale_out)
    )
    own_a, own_b, own_o, down_own, sums = unpack_columns(received, ups, ups_out)

    sums = sums.reshape(1152)
    sums = [sums] + [from_y(sums, step) for step in (1, 2, 3)]
    own_a, own_b, pair, sums = lax.optimization_barrier((own_a, own_b, pair, sums))

    next_a, last_a = from_y(own_a, 1), from_y(own_a, 3)
    tokens = [pair] + [from_x(pair, step) for step in (1, 2, 3)]
    next_a, last_a, tokens, late_b = lax.optimization_barrier((next_a, last_a, tokens, own_b))
    next_b, last_b = from_y(late_b, 1), from_y(late_b, 3)
    near = jnp.stack(tokens)
    far = swap_core(near)
    squares = token_sums(near).reshape(512)
    both = jnp.concatenate([sum(sums), squares + swap_core(squares)])
    both = both + swap_low(both)
    near, far, both, next_a, next_b, last_a, last_b = lax.optimization_barrier(
        (near, far, both, next_a, next_b, last_a, last_b)
    )
    far_a, far_b = from_y(next_a, 1), from_y(last_b, 3)
    factor_qkv = (scale_qkv / jnp.sqrt(both[:640])).reshape(1, 640)
    factor_out = (scale_out / jnp.sqrt(both[640:1152])).reshape(1, 512)
    inverse = lax.rsqrt(both[1152:] / 8192.0 + EPSILON).reshape(512, 1)
    weight_a, weight_b = scale_rows(own_o, down_own, ups_out, factor_out)

    gains = pick(input_norm_gain.reshape(4, 2, 2, 1, 512), zl, 1)

    def project(steps, blocks, total):
        place = [(y + step - x) % 4 for step in steps] + [(y + step) % 4 for step in steps]
        place = jnp.stack(place + [c, zh ^ zl]).astype(jnp.int32)
        return multiply_slabs(
            place, near, far, inverse, gains, blocks, ups, factor_qkv, total
        )

    total = project((0, 1, 3), (own_a, own_b, next_a, next_b, last_a, last_b), None)
    total, far_a, far_b, weight_a, weight_b = lax.optimization_barrier(
        (total, far_a, far_b, weight_a, weight_b)
    )
    other, mine = project((2,), (far_a, far_b), total)

    rows_o = [weight_a, weight_b, from_y(weight_a, 1), from_y(weight_b, 1)]
    rows_last = [from_y(weight_a, 3), from_y(weight_b, 3)]
    rows_o += [from_y(rows_o[2], 1), from_y(rows_last[1], 3)] + rows_last

    projected = (mine + swap_low(other)).astype(bf16).reshape(16, 16, 640)
    every = lax.all_to_all(projected, "tp", 0, 0, tiled=True)
    place = jnp.stack([y, zl]).astype(jnp.int32)
    attended = attend(place, lengths, every, cached_key_rows, cached_value_rows)

    attended, rows_o = lax.optimization_barrier((attended, rows_o))
    slabs = attended.reshape(2, 4, 16, 1024)

    def along_z(own, other):
        def flip(value, dl, dh):
            return permute(value, lambda y, zl, x, zh, c: (y, zl ^ dl, x, zh ^ dh, c))

        return jnp.stack([own, flip(own, 0, 1), flip(other, 1, 0), flip(other, 1, 1)])

    def along_x(value):
        return jnp.stack([value] + [from_x(value, step) for step in (1, 2, 3)])

    first = jnp.stack([slabs[0, :2], swap_low(slabs[1, :2])])
    flipped = permute(first, lambda y, zl, x, zh, c: (y, zl, x, 1 - zh, c))
    first = jnp.stack([first[0], flipped[0], first[1], flipped[1]])
    second = along_x(slabs[:, 2:])
    first = along_x(first)
    second = along_z(second[:, 0], second[:, 1])
    place = jnp.stack([x, zh, c]).astype(jnp.int32)
    mine, other = multiply_output(
        place, (first, second, swap_core(first), swap_core(second)), rows_o
    )
    result = (mine + swap_low(other).astype(f32)).astype(bf16)
    return result.reshape(16, 4, 4, 512).transpose(2, 0, 1, 3).reshape(4, 64, 512)


def solution(mesh):
    return jax.shard_map(
        per_device,
        mesh=mesh,
        in_specs=(
            P(None, "rep", "tp"),
            P(),
            P(("rep", "tp"), None),
            P(("rep", "tp"), None),
            P(("rep", "tp"), None),
            P(("rep", "tp"), None),
            P(),
            P(("rep", "tp"), None),
            P(),
            P(("rep", "tp"), None),
            P(),
            P(),
            P(),
            P(),
            P(("rep", "tp"), None, None, None),
            P(("rep", "tp"), None, None, None),
            P(("rep", "tp")),
        ),
        out_specs=P(None, "rep", "tp"),
        check_vma=False,
    )
```

time: 250 us -> 238 us (0.952)
  starting transfers between devices: 84.2 us -> 64.6 us
  waiting for transfers between devices: 89.9 us -> 105 us
  other arithmetic: 13.8 us -> 8.16 us
  Pallas kernels: 36.6 us -> 41.1 us
  matrix products: 3.51 us -> 0 us
  local copies, waits for them, and re-layouts: 20.3 us -> 16.9 us
    all_to_all x3 -> x0, starting transfers between devices: 17.7 us -> none  [the longest x1 9.65 us: per_device(): lax.all_to_all(frozen_o.reshape(64, 16, 512).transpose(1, 0, 2), 'tp', 0,...]
    ppermute x32 -> x38, waiting for transfers between devices: 54.9 us -> 72 us  [permute(): return lax.ppermute(value, AXES, pairs)]
    all_to_all x3 -> x0, waiting for transfers between devices: 13.8 us -> none  [the longest x1 9.03 us: per_device(): lax.all_to_all(frozen_o.reshape(64, 16, 512).transpose(1, 0, 2), 'tp', 0,...]
    all_to_all x1, waiting for transfers between devices: 12.4 us -> 24.2 us  [per_device(): received = lax.all_to_all(frozen, 'tp', 0, 0, tiled=True)]
    pallas_call x4, Pallas kernels: 13.1 us -> 19.9 us  [the longest x2 14.5 us: multiply_slabs(): pl.pallas_call(multiply_slabs_kernel, grid_spec=pltpu.PrefetchScalarGridS...]
    ppermute x32 -> x38, starting transfers between devices: 51.1 us -> 45.3 us  [permute(): return lax.ppermute(value, AXES, pairs)]
    reduce_sum x4 -> x0, other arithmetic: 4.52 us -> none  [the longest x1 2.26 us: per_device(): jnp.sum(near_wide * near_wide + far_wide * far_wide, axis=(0, 2))]
    all_to_all x1, starting transfers between devices: 6.23 us -> 10 us  [per_device(): every = lax.all_to_all(projected, 'tp', 0, 0, tiled=True)]
  transfers between devices with their start and end apart: 37 -> 40, of which waited for: 16 -> 20; matrix products, arithmetic and copies ran while one was open for 11% -> 7% of each run, Pallas kernels for 10% -> 12%
where the time goes in v2:
time: 238 us; the launch traced here: 236 us
  waiting for transfers between devices  105 us (44%)
  starting transfers between devices  64.6 us (27%)
  Pallas kernels  41.1 us (17%)
  local copies, waits for them, and re-layouts  16.9 us (7%)
  other arithmetic  8.16 us (3%)
    ppermute x38, waiting for transfers between devices, permute(): return lax.ppermute(value, AXES, pairs)  72 us
    ppermute x38, starting transfers between devices, permute(): return lax.ppermute(value, AXES, pairs)  45.3 us
    all_to_all x1, waiting for transfers between devices, per_device(): received = lax.all_to_all(frozen, 'tp', 0, 0, tiled=True)  24.2 us
    pallas_call x2, Pallas kernels, multiply_slabs(): pl.pallas_call(multiply_slabs_kernel, grid_spec=pltpu.PrefetchScalarGridS...  14.5 us
    pallas_call x1, Pallas kernels, attend(): pl.pallas_call(attend_kernel, grid_spec=pltpu.PrefetchScalarGridSpec(num_...  12.2 us
    all_to_all x1, starting transfers between devices, per_device(): every = lax.all_to_all(projected, 'tp', 0, 0, tiled=True)  10 us
    all_to_all x1, starting transfers between devices, per_device(): received = lax.all_to_all(frozen, 'tp', 0, 0, tiled=True)  9.26 us
    all_to_all x1, waiting for transfers between devices, per_device(): every = lax.all_to_all(projected, 'tp', 0, 0, tiled=True)  9.11 us
  transfers between devices with their start and end apart: 40, of which 20 were waited for; matrix products, arithmetic and copies ran while one was open for 7% of the time, Pallas kernels for 12%

profile of v2, /device:TPU:1, one launch (start us, length us, event | category | flops | bytes accessed | tf_op | source)
XLA Modules:
  0.0 236.4 jit_solution(6907936386618936665)
XLA Ops:
  0.0 4.1 %shard_map.163 = bf16[16,10,64,128]{3,2,1,0:T(8,128)(2,1)} custom-call(s32[1]{0:T(128)} %bitcast.8.place, bf16[64,8192]{1,0:T(8,128)(2,1)} %query.1, bf16[64,2048]{1,0:T(8,128)(2,1)} %key_value.1, bf16[64,8192]{1,0:T(8,128)(2,1)} %output.1, bf16[32,64]{1,0:T(8,128)(2,1)} %bitcast.89, bf16[32,64]{1,0:T(8,128)(2,1)} %bitcast.90, bf16[32,64]{1,0:T(8,128)(2,1)} %bitcast.91), custom_call_target="tpu_custom_call" | custom-call | bytes 4194304 | tf_op jit(solution)/shard_map/pallas_call | solution.py:82
  4.2 9.3 %all-to-all-start = ((bf16[16,10,64,128]{3,2,1,0:T(8,128)(2,1)}), bf16[16,10,64,128]{3,2,1,0:T(8,128)(2,1)S(1)}, u32[]{:S(2)}, u32[]{:S(2)}) async-start(bf16[16,10,64,128]{3,2,1,0:T(8,128)(2,1)} %shard_map.163), calls=%async_computation | async-start | bytes 5242880 | tf_op jit(solution)/shard_map/all_to_all | solution.py:429
  14.4 3.6 %collective-permute-start = (bf16[256,512]{1,0:T(8,128)(2,1)}, bf16[256,512]{1,0:T(8,128)(2,1)}, u32[]{:S(2)}, u32[]{:S(2)}) collective-permute-start(bf16[256,512]{1,0:T(8,128)(2,1)} %reshape.37), channel_id=1, source_target_pairs={{0,0},{1,1},{2,16},{3,17},{4,4},{5,5},{6,20},{7,21},{8,8},{9,9},{1... | collective-permute-start | bytes 786440 | tf_op jit(solution)/shard_map/ppermute | solution.py:29
  23.3 24.2 %all-to-all-done.received = bf16[16,10,64,128]{3,2,1,0:T(8,128)(2,1)S(1)} async-done(((bf16[16,10,64,128]{3,2,1,0:T(8,128)(2,1)}), bf16[16,10,64,128]{3,2,1,0:T(8,128)(2,1)S(1)}, u32[]{:S(2)}, u32[]{:S(2)}) %all-to-all-start) | async-done | bytes 2621472 | tf_op jit(solution)/shard_map/all_to_all | solution.py:429
  51.9 2.8 %collective-permute-start.2 = (f32[1152]{0:T(1024)S(1)}, f32[1152]{0:T(1024)S(1)}, u32[]{:S(2)}, u32[]{:S(2)}) collective-permute-start(f32[1152]{0:T(1024)S(1)} %reduce), channel_id=1, source_target_pairs={{0,96},{1,97},{2,98},{3,99},{4,100},{5,101},{6,102},{7,103},{8,104... | collective-permute-start | bytes 13832 | tf_op jit(solution)/shard_map/ppermute | solution.py:29
  62.7 7.7 %collective-permute-done.7 = bf16[512,512]{1,0:T(8,128)(2,1)S(1)} collective-permute-done((bf16[512,512]{1,0:T(8,128)(2,1)S(1)}, bf16[512,512]{1,0:T(8,128)(2,1)S(1)}, u32[]{:S(2)}, u32[]{:S(2)}) %collective-permute-start.7) | collective-permute-done | bytes 524320 | tf_op jit(solution)/shard_map/ppermute | solution.py:29
  70.4 2.9 %collective-permute-done.8 = bf16[512,512]{1,0:T(8,128)(2,1)S(1)} collective-permute-done((bf16[512,512]{1,0:T(8,128)(2,1)S(1)}, bf16[512,512]{1,0:T(8,128)(2,1)S(1)}, u32[]{:S(2)}, u32[]{:S(2)}) %collective-permute-start.8) | collective-permute-done | bytes 524320 | tf_op jit(solution)/shard_map/ppermute | solution.py:29
  73.3 15.0 %collective-permute-done.9 = bf16[512,512]{1,0:T(8,128)(2,1)S(1)} collective-permute-done((bf16[512,512]{1,0:T(8,128)(2,1)S(1)}, bf16[512,512]{1,0:T(8,128)(2,1)S(1)}, u32[]{:S(2)}, u32[]{:S(2)}) %collective-permute-start.9) | collective-permute-done | bytes 524320 | tf_op jit(solution)/shard_map/ppermute | solution.py:29
  92.3 2.8 %shard_map.165 = f32[512,1]{1,0:T(8,128)} custom-call(bf16[4,512,512]{2,1,0:T(8,128)(2,1)} %copy-done.10), custom_call_target="tpu_custom_call" | custom-call | flops 1048576 | bytes 4096 | tf_op jit(solution)/shard_map/pallas_call | solution.py:175
  97.9 3.5 %collective-permute-start.12 = (f32[1664]{0:T(1024)S(1)}, f32[1664]{0:T(1024)S(1)}, u32[]{:S(2)}, u32[]{:S(2)}) collective-permute-start(f32[1664]{0:T(1024)S(1)} %pad_maximum_fusion.9), channel_id=1, source_target_pairs={{0,16},{1,17},{2,18},{3,19},{4,20},{5,21},{6,22},{7,23},{8,24},{9,... | collective-permute-start | bytes 19976 | tf_op jit(solution)/shard_map/ppermute | solution.py:29
  102.9 3.7 %collective-permute-done.13.refs_15_ = bf16[5,512,128]{2,1,0:T(8,128)(2,1)S(1)} collective-permute-done((bf16[5,512,128]{2,1,0:T(8,128)(2,1)S(1)}, bf16[5,512,128]{2,1,0:T(8,128)(2,1)S(1)}, u32[]{:S(2)}, u32[]{:S(2)}) %collective-permute-start.13) | collective-permute-done | bytes 655392 | tf_op jit(solution)/shard_map/ppermute | solution.py:29
  118.3 9.0 %shard_map.166.refs_8_ = f32[512,640]{1,0:T(8,128)} custom-call(s32[8]{0:T(128)} %stack.169.place, bf16[4,512,512]{2,1,0:T(8,128)(2,1)} %copy-done.10, bf16[4,512,512]{2,1,0:T(8,128)(2,1)} %collective-permute-done.10.refs_1_.refs_4_.refs_7_, f32[4,2,1,512]{3,2,1,0:T(1,128)} %dynamic-slice_bitcast_fusion.refs_2_.refs_5_.refs_8_, ...), custom_call_target="tpu_custom_call" | custom-call | flops 1048576 | bytes 4096 | tf_op jit(solution)/shard_map/pallas_call | solution.py:230
  128.4 5.6 %shard_map.168 = (f32[256,640]{1,0:T(8,128)}, f32[256,640]{1,0:T(8,128)}) custom-call(s32[4]{0:T(128)} %pad_add_fusion.2.place, bf16[4,512,512]{2,1,0:T(8,128)(2,1)} %copy-done.10, bf16[4,512,512]{2,1,0:T(8,128)(2,1)} %collective-permute-done.10.refs_1_.refs_4_.refs_7_, f32[4,2,1,512]{3,2,1,0:T(1,128)} %dynamic-slice_bitcast_fusion.refs_2_.refs_5_.refs_8_, ...), custom_call_target="tpu_custom_call" | custom-call | flops 1048576 | bytes 4096 | tf_op jit(solution)/shard_map/pallas_call | solution.py:230
  134.0 3.5 %collective-permute-start.17 = (f32[256,640]{1,0:T(8,128)}, f32[256,640]{1,0:T(8,128)S(1)}, u32[]{:S(2)}, u32[]{:S(2)}) collective-permute-start(f32[256,640]{1,0:T(8,128)} %get-tuple-element.93), channel_id=1, source_target_pairs={{0,16},{1,17},{2,18},{3,19},{4,20},{5,21},{6,22},{7,23},{8,24},{9,... | collective-permute-start | bytes 1966088 | tf_op jit(solution)/shard_map/ppermute | solution.py:29
  141.7 6.7 %collective-permute-done.18.refs_2_ = bf16[512,512]{1,0:T(8,128)(2,1)S(1)} collective-permute-done((bf16[512,512]{1,0:T(8,128)(2,1)S(1)}, bf16[512,512]{1,0:T(8,128)(2,1)S(1)}, u32[]{:S(2)}, u32[]{:S(2)}) %collective-permute-start.18) | collective-permute-done | bytes 524320 | tf_op jit(solution)/shard_map/ppermute | solution.py:29
  148.4 3.0 %collective-permute-start.20 = (bf16[512,512]{1,0:T(8,128)(2,1)S(1)}, bf16[512,512]{1,0:T(8,128)(2,1)}, u32[]{:S(2)}, u32[]{:S(2)}) collective-permute-start(bf16[512,512]{1,0:T(8,128)(2,1)S(1)} %collective-permute-done.18.refs_2_), channel_id=1, source_target_pairs={{0,96},{1,97},{2,98},{3,99},{4,100},{5,101},{6,102},{7,103},{8,104... | collective-permute-start | bytes 1572872 | tf_op jit(solution)/shard_map/ppermute | solution.py:29
  153.4 10.0 %all-to-all-start.1 = ((bf16[16,16,640]{2,1,0:T(8,128)(2,1)}), bf16[16,16,640]{2,1,0:T(8,128)(2,1)}, u32[]{:S(2)}, u32[]{:S(2)}) async-start(bf16[16,16,640]{2,1,0:T(8,128)(2,1)} %bitcast.70), calls=%async_computation.1 | async-start | bytes 655360 | tf_op jit(solution)/shard_map/all_to_all | solution.py:507
  163.9 9.1 %all-to-all-done.1.every = bf16[16,16,640]{2,1,0:T(8,128)(2,1)} async-done(((bf16[16,16,640]{2,1,0:T(8,128)(2,1)}), bf16[16,16,640]{2,1,0:T(8,128)(2,1)}, u32[]{:S(2)}, u32[]{:S(2)}) %all-to-all-start.1) | async-done | bytes 327712 | tf_op jit(solution)/shard_map/all_to_all | solution.py:507
  173.1 12.2 %shard_map.169 = bf16[8,16,1024]{2,1,0:T(8,128)(2,1)} custom-call(s32[2]{0:T(128)} %pad_add_fusion.1.place, s32[4]{0:T(128)} %lengths.1, bf16[16,16,640]{2,1,0:T(8,128)(2,1)} %all-to-all-done.1.every, bf16[4,8,1024,128]{3,2,1,0:T(8,128)(2,1)} %keys.1, bf16[4,8,1024,128]{3,2,1,0:T(8,128)(2,1)} %values.1), custom_call_target="tpu_custom_call" | custom-call | flops 1048576 | bytes 4096 | tf_op jit(solution)/shard_map/pallas_call | solution.py:317
  193.1 4.0 %collective-permute-done.31 = bf16[2,2,16,1024]{3,2,1,0:T(8,128)(2,1)S(1)} collective-permute-done((bf16[2,2,16,1024]{3,2,1,0:T(8,128)(2,1)S(1)}, bf16[2,2,16,1024]{3,2,1,0:T(8,128)(2,1)S(1)}, u32[]{:S(2)}, u32[]{:S(2)}) %collective-permute-start.31) | collective-permute-done | bytes 131104 | tf_op jit(solution)/shard_map/ppermute | solution.py:29
  202.6 8.8 %collective-permute-done.32 = bf16[4,2,16,1024]{3,2,1,0:T(8,128)(2,1)S(1)} collective-permute-done((bf16[4,2,16,1024]{3,2,1,0:T(8,128)(2,1)S(1)}, bf16[4,2,16,1024]{3,2,1,0:T(8,128)(2,1)S(1)}, u32[]{:S(2)}, u32[]{:S(2)}) %collective-permute-start.32) | collective-permute-done | bytes 262176 | tf_op jit(solution)/shard_map/ppermute | solution.py:29
  214.3 4.8 %collective-permute-done.28 = bf16[4,2,16,1024]{3,2,1,0:T(8,128)(2,1)S(1)} collective-permute-done((bf16[4,2,16,1024]{3,2,1,0:T(8,128)(2,1)S(1)}, bf16[4,2,16,1024]{3,2,1,0:T(8,128)(2,1)S(1)}, u32[]{:S(2)}, u32[]{:S(2)}) %collective-permute-start.28) | collective-permute-done | bytes 262176 | tf_op jit(solution)/shard_map/ppermute | solution.py:29
  223.9 4.1 %shard_map.170 = (f32[16,16,512]{2,1,0:T(8,128)S(1)}, bf16[16,16,512]{2,1,0:T(8,128)(2,1)S(1)}) custom-call(s32[3]{0:T(128)S(1)} %pad_add_fusion.place, bf16[4,4,2,16,1024]{4,3,2,1,0:T(8,128)(2,1)S(1)} %pad_maximum_fusion.1.near_a, bf16[4,4,2,16,1024]{4,3,2,1,0:T(8,128)(2,1)S(1)} %pad_maximum_fusion.2.near_b, ...), custom_call_target="tpu_custom_call" | custom-call | flops 2147483648 | bytes 8388608 | tf_op jit(solution)/shard_map/pallas_call | solution.py:371
  228.0 7.5 %collective-permute-done.37 = bf16[16,16,512]{2,1,0:T(8,128)(2,1)S(1)} collective-permute-done((bf16[16,16,512]{2,1,0:T(8,128)(2,1)S(1)}, bf16[16,16,512]{2,1,0:T(8,128)(2,1)S(1)}, u32[]{:S(2)}, u32[]{:S(2)}) %collective-permute-start.37) | collective-permute-done | bytes 262176 | tf_op jit(solution)/shard_map/ppermute | solution.py:29
  (153 shorter events, 68.2 us)
Async XLA Ops:
  4.2 43.3 %all-to-all-start = ((bf16[16,10,64,128]{3,2,1,0:T(8,128)(2,1)}), bf16[16,10,64,128]{3,2,1,0:T(8,128)(2,1)S(1)}, u32[]{:S(2)}, u32[]{:S(2)}) async-start(bf16[16,10,64,128]{3,2,1,0:T(8,128)(2,1)} %shard_map.163), calls=%async_computation | async-start | bytes 5242880 | tf_op jit(solution)/shard_map/all_to_all | solution.py:429
  14.4 41.3 %collective-permute-start = (bf16[256,512]{1,0:T(8,128)(2,1)}, bf16[256,512]{1,0:T(8,128)(2,1)}, u32[]{:S(2)}, u32[]{:S(2)}) collective-permute-start(bf16[256,512]{1,0:T(8,128)(2,1)} %reshape.37), channel_id=1, source_target_pairs={{0,0},{1,1},{2,16},{3,17},{4,4},{5,5},{6,20},{7,21},{8,8},{9,9},{1... | collective-permute-start | bytes 786440 | tf_op jit(solution)/shard_map/ppermute | solution.py:29
  18.0 37.7 %collective-permute-start.1 = (bf16[256,512]{1,0:T(8,128)(2,1)}, bf16[256,512]{1,0:T(8,128)(2,1)}, u32[]{:S(2)}, u32[]{:S(2)}) collective-permute-start(bf16[256,512]{1,0:T(8,128)(2,1)} %reshape.37), channel_id=1, source_target_pairs={{0,2},{1,3},{2,18},{3,19},{4,6},{5,7},{6,22},{7,23},{8,10},{9,11},... | collective-permute-start | bytes 786440 | tf_op jit(solution)/shard_map/ppermute | solution.py:29
  58.8 29.5 %collective-permute-start.5 = (bf16[6,512,128]{2,1,0:T(8,128)(2,1)}, bf16[6,512,128]{2,1,0:T(8,128)(2,1)S(1)}, u32[]{:S(2)}, u32[]{:S(2)}) collective-permute-start(bf16[6,512,128]{2,1,0:T(8,128)(2,1)} %copy-done.4), channel_id=1, source_target_pairs={{0,96},{1,97},{2,98},{3,99},{4,100},{5,101},{6,102},{7,103},{8,104... | collective-permute-start | bytes 2359304 | tf_op jit(solution)/shard_map/ppermute | solution.py:29
  59.2 29.1 %collective-permute-start.6 = (bf16[6,512,128]{2,1,0:T(8,128)(2,1)}, bf16[6,512,128]{2,1,0:T(8,128)(2,1)S(1)}, u32[]{:S(2)}, u32[]{:S(2)}) collective-permute-start(bf16[6,512,128]{2,1,0:T(8,128)(2,1)} %copy-done.4), channel_id=1, source_target_pairs={{0,32},{1,33},{2,34},{3,35},{4,36},{5,37},{6,38},{7,39},{8,40},{9,... | collective-permute-start | bytes 2359304 | tf_op jit(solution)/shard_map/ppermute | solution.py:29
  61.7 11.6 %collective-permute-start.8 = (bf16[512,512]{1,0:T(8,128)(2,1)S(1)}, bf16[512,512]{1,0:T(8,128)(2,1)S(1)}, u32[]{:S(2)}, u32[]{:S(2)}) collective-permute-start(bf16[512,512]{1,0:T(8,128)(2,1)S(1)} %pad_maximum_fusion.3), channel_id=1, source_target_pairs={{0,8},{1,9},{2,10},{3,11},{4,12},{5,13},{6,14},{7,15},{8,0},{9,1},... | collective-permute-start | bytes 1572872 | tf_op jit(solution)/shard_map/ppermute | solution.py:29
  62.1 26.2 %collective-permute-start.9 = (bf16[512,512]{1,0:T(8,128)(2,1)S(1)}, bf16[512,512]{1,0:T(8,128)(2,1)S(1)}, u32[]{:S(2)}, u32[]{:S(2)}) collective-permute-start(bf16[512,512]{1,0:T(8,128)(2,1)S(1)} %pad_maximum_fusion.3), channel_id=1, source_target_pairs={{0,4},{1,5},{2,6},{3,7},{4,8},{5,9},{6,10},{7,11},{8,12},{9,13},{1... | collective-permute-start | bytes 1572872 | tf_op jit(solution)/shard_map/ppermute | solution.py:29
  89.9 19.2 %collective-permute-start.10 = (bf16[4,512,512]{2,1,0:T(8,128)(2,1)S(1)}, bf16[4,512,512]{2,1,0:T(8,128)(2,1)}, u32[]{:S(2)}, u32[]{:S(2)}) collective-permute-start(bf16[4,512,512]{2,1,0:T(8,128)(2,1)S(1)} %pad_maximum_fusion.near.refs_0_.refs_3_.refs_6_), channel_id=1, source_target_pairs={{0,1},{1,0},{2,3},{3,2},{4,5},{5,4},{6,7},{7,6},{8,9},{9,8},{10,11... | collective-permute-start | bytes 6291464 | tf_op jit(solution)/shard_map/ppermute | solution.py:29
  90.6 15.9 %collective-permute-start.13 = (bf16[5,512,128]{2,1,0:T(8,128)(2,1)S(1)}, bf16[5,512,128]{2,1,0:T(8,128)(2,1)S(1)}, u32[]{:S(2)}, u32[]{:S(2)}) collective-permute-start(bf16[5,512,128]{2,1,0:T(8,128)(2,1)S(1)} %copy-done.6), channel_id=1, source_target_pairs={{0,96},{1,97},{2,98},{3,99},{4,100},{5,101},{6,102},{7,103},{8,104... | collective-permute-start | bytes 1966088 | tf_op jit(solution)/shard_map/ppermute | solution.py:29
  92.3 16.8 %collective-permute-start.14 = (bf16[5,512,128]{2,1,0:T(8,128)(2,1)S(1)}, bf16[5,512,128]{2,1,0:T(8,128)(2,1)}, u32[]{:S(2)}, u32[]{:S(2)}) collective-permute-start(bf16[5,512,128]{2,1,0:T(8,128)(2,1)S(1)} %copy-done.6), channel_id=1, source_target_pairs={{0,32},{1,33},{2,34},{3,35},{4,36},{5,37},{6,38},{7,39},{8,40},{9,... | collective-permute-start | bytes 1966088 | tf_op jit(solution)/shard_map/ppermute | solution.py:29
  109.1 18.2 %collective-permute-start.15 = (bf16[6,512,128]{2,1,0:T(8,128)(2,1)}, bf16[6,512,128]{2,1,0:T(8,128)(2,1)S(1)}, u32[]{:S(2)}, u32[]{:S(2)}) collective-permute-start(bf16[6,512,128]{2,1,0:T(8,128)(2,1)} %copy-done.11), channel_id=1, source_target_pairs={{0,96},{1,97},{2,98},{3,99},{4,100},{5,101},{6,102},{7,103},{8,104... | collective-permute-start | bytes 2359304 | tf_op jit(solution)/shard_map/ppermute | solution.py:29
  110.0 17.3 %collective-permute-start.16 = (bf16[5,512,128]{2,1,0:T(8,128)(2,1)}, bf16[5,512,128]{2,1,0:T(8,128)(2,1)S(1)}, u32[]{:S(2)}, u32[]{:S(2)}) collective-permute-start(bf16[5,512,128]{2,1,0:T(8,128)(2,1)} %collective-permute-done.14.refs_17_), channel_id=1, source_target_pairs={{0,32},{1,33},{2,34},{3,35},{4,36},{5,37},{6,38},{7,39},{8,40},{9,... | collective-permute-start | bytes 1966088 | tf_op jit(solution)/shard_map/ppermute | solution.py:29
  134.0 17.5 %collective-permute-start.17 = (f32[256,640]{1,0:T(8,128)}, f32[256,640]{1,0:T(8,128)S(1)}, u32[]{:S(2)}, u32[]{:S(2)}) collective-permute-start(f32[256,640]{1,0:T(8,128)} %get-tuple-element.93), channel_id=1, source_target_pairs={{0,16},{1,17},{2,18},{3,19},{4,20},{5,21},{6,22},{7,23},{8,24},{9,... | collective-permute-start | bytes 1966088 | tf_op jit(solution)/shard_map/ppermute | solution.py:29
  139.0 12.5 %collective-permute-start.21 = (bf16[512,512]{1,0:T(8,128)(2,1)S(1)}, bf16[512,512]{1,0:T(8,128)(2,1)S(1)}, u32[]{:S(2)}, u32[]{:S(2)}) collective-permute-start(bf16[512,512]{1,0:T(8,128)(2,1)S(1)} %copy-done.8), channel_id=1, source_target_pairs={{0,32},{1,33},{2,34},{3,35},{4,36},{5,37},{6,38},{7,39},{8,40},{9,... | collective-permute-start | bytes 1572872 | tf_op jit(solution)/shard_map/ppermute | solution.py:29
  139.0 46.2 %collective-permute-start.19 = (bf16[512,512]{1,0:T(8,128)(2,1)S(1)}, bf16[512,512]{1,0:T(8,128)(2,1)S(1)}, u32[]{:S(2)}, u32[]{:S(2)}) collective-permute-start(bf16[512,512]{1,0:T(8,128)(2,1)S(1)} %copy-done.8), channel_id=1, source_target_pairs={{0,96},{1,97},{2,98},{3,99},{4,100},{5,101},{6,102},{7,103},{8,104... | collective-permute-start | bytes 1572872 | tf_op jit(solution)/shard_map/ppermute | solution.py:29
  141.7 43.5 %collective-permute-start.23 = (bf16[512,512]{1,0:T(8,128)(2,1)S(1)}, bf16[512,512]{1,0:T(8,128)(2,1)S(1)}, u32[]{:S(2)}, u32[]{:S(2)}) collective-permute-start(bf16[512,512]{1,0:T(8,128)(2,1)S(1)} %copy-done.7), channel_id=1, source_target_pairs={{0,32},{1,33},{2,34},{3,35},{4,36},{5,37},{6,38},{7,39},{8,40},{9,... | collective-permute-start | bytes 1572872 | tf_op jit(solution)/shard_map/ppermute | solution.py:29
  148.4 36.8 %collective-permute-start.20 = (bf16[512,512]{1,0:T(8,128)(2,1)S(1)}, bf16[512,512]{1,0:T(8,128)(2,1)}, u32[]{:S(2)}, u32[]{:S(2)}) collective-permute-start(bf16[512,512]{1,0:T(8,128)(2,1)S(1)} %collective-permute-done.18.refs_2_), channel_id=1, source_target_pairs={{0,96},{1,97},{2,98},{3,99},{4,100},{5,101},{6,102},{7,103},{8,104... | collective-permute-start | bytes 1572872 | tf_op jit(solution)/shard_map/ppermute | solution.py:29
  151.5 33.8 %collective-permute-start.22 = (bf16[512,512]{1,0:T(8,128)(2,1)S(1)}, bf16[512,512]{1,0:T(8,128)(2,1)}, u32[]{:S(2)}, u32[]{:S(2)}) collective-permute-start(bf16[512,512]{1,0:T(8,128)(2,1)S(1)} %collective-permute-done.21.refs_7_), channel_id=1, source_target_pairs={{0,32},{1,33},{2,34},{3,35},{4,36},{5,37},{6,38},{7,39},{8,40},{9,... | collective-permute-start | bytes 1572872 | tf_op jit(solution)/shard_map/ppermute | solution.py:29
  153.4 19.7 %all-to-all-start.1 = ((bf16[16,16,640]{2,1,0:T(8,128)(2,1)}), bf16[16,16,640]{2,1,0:T(8,128)(2,1)}, u32[]{:S(2)}, u32[]{:S(2)}) async-start(bf16[16,16,640]{2,1,0:T(8,128)(2,1)} %bitcast.70), calls=%async_computation.1 | async-start | bytes 655360 | tf_op jit(solution)/shard_map/all_to_all | solution.py:507
  197.2 14.2 %collective-permute-start.33 = (bf16[4,2,16,1024]{3,2,1,0:T(8,128)(2,1)S(1)}, bf16[4,2,16,1024]{3,2,1,0:T(8,128)(2,1)S(1)}, u32[]{:S(2)}, u32[]{:S(2)}) collective-permute-start(bf16[4,2,16,1024]{3,2,1,0:T(8,128)(2,1)S(1)} %get-tuple-element.109), channel_id=1, source_target_pairs={{0,16},{1,17},{2,18},{3,19},{4,20},{5,21},{6,22},{7,23},{8,24},{9,... | collective-permute-start | bytes 786440 | tf_op jit(solution)/shard_map/ppermute | solution.py:29
  198.5 12.9 %collective-permute-start.34 = (bf16[4,2,16,1024]{3,2,1,0:T(8,128)(2,1)S(1)}, bf16[4,2,16,1024]{3,2,1,0:T(8,128)(2,1)S(1)}, u32[]{:S(2)}, u32[]{:S(2)}) collective-permute-start(bf16[4,2,16,1024]{3,2,1,0:T(8,128)(2,1)S(1)} %get-tuple-element.109), channel_id=1, source_target_pairs={{0,18},{1,19},{2,16},{3,17},{4,22},{5,23},{6,20},{7,21},{8,26},{9,... | collective-permute-start | bytes 786440 | tf_op jit(solution)/shard_map/ppermute | solution.py:29
  199.1 12.4 %collective-permute-start.32 = (bf16[4,2,16,1024]{3,2,1,0:T(8,128)(2,1)S(1)}, bf16[4,2,16,1024]{3,2,1,0:T(8,128)(2,1)S(1)}, u32[]{:S(2)}, u32[]{:S(2)}) collective-permute-start(bf16[4,2,16,1024]{3,2,1,0:T(8,128)(2,1)S(1)} %get-tuple-element.108), channel_id=1, source_target_pairs={{0,2},{1,3},{2,0},{3,1},{4,6},{5,7},{6,4},{7,5},{8,10},{9,11},{10,... | collective-permute-start | bytes 786440 | tf_op jit(solution)/shard_map/ppermute | solution.py:29
  200.6 13.7 %collective-permute-start.26 = (bf16[4,2,16,1024]{3,2,1,0:T(8,128)(2,1)S(1)}, bf16[4,2,16,1024]{3,2,1,0:T(8,128)(2,1)S(1)}, u32[]{:S(2)}, u32[]{:S(2)}) collective-permute-start(bf16[4,2,16,1024]{3,2,1,0:T(8,128)(2,1)S(1)} %get-tuple-element.113), channel_id=1, source_target_pairs={{0,12},{1,13},{2,14},{3,15},{4,0},{5,1},{6,2},{7,3},{8,4},{9,5},{1... | collective-permute-start | bytes 786440 | tf_op jit(solution)/shard_map/ppermute | solution.py:29
  200.9 13.4 %collective-permute-start.27 = (bf16[4,2,16,1024]{3,2,1,0:T(8,128)(2,1)S(1)}, bf16[4,2,16,1024]{3,2,1,0:T(8,128)(2,1)S(1)}, u32[]{:S(2)}, u32[]{:S(2)}) collective-permute-start(bf16[4,2,16,1024]{3,2,1,0:T(8,128)(2,1)S(1)} %get-tuple-element.113), channel_id=1, source_target_pairs={{0,8},{1,9},{2,10},{3,11},{4,12},{5,13},{6,14},{7,15},{8,0},{9,1},... | collective-permute-start | bytes 786440 | tf_op jit(solution)/shard_map/ppermute | solution.py:29
  (36 other events, 337.2 us)

commit v3 on v2

--- a/solution.py
+++ b/solution.py
@@ -205,8 +205,8 @@
     else:
         value = value + rest[0][...]
         swapped = place[2 * count + 1] == 1
-        rest[1][...] = jnp.where(swapped, value[:256], value[256:])
-        rest[2][...] = jnp.where(swapped, value[256:], value[:256])
+        rest[1][:256] = jnp.where(swapped, value[256:], value[:256])
+        rest[1][256:] = jnp.where(swapped, value[:256], value[256:])
 
 
 def multiply_slabs(place, near, far, inverse, gains, blocks, ups, factor, total):
@@ -225,17 +225,15 @@
     rest = [inverse, ups, factor, *blocks] + ([] if total is None else [total])
     operands += rest
     specs += [whole(operand.shape) for operand in rest]
-    rows = 512 if total is None else 256
-    shape = jax.ShapeDtypeStruct((rows, 640), jnp.float32)
     return pl.pallas_call(
         multiply_slabs_kernel,
         grid_spec=pltpu.PrefetchScalarGridSpec(
             num_scalar_prefetch=1,
             grid=(1,),
             in_specs=specs,
-            out_specs=whole((rows, 640)) if total is None else [whole((rows, 640))] * 2,
+            out_specs=whole((512, 640)),
         ),
-        out_shape=shape if total is None else [shape] * 2,
+        out_shape=jax.ShapeDtypeStruct((512, 640), jnp.float32),
         compiler_params=pltpu.CompilerParams(vmem_limit_bytes=56 * 2**20),
         cost_estimate=pl.CostEstimate(
             flops=2**20, bytes_accessed=2**12, transcendentals=0
@@ -466,19 +464,18 @@
     sums = [sums] + [from_y(sums, step) for step in (1, 2, 3)]
     own_a, own_b, pair, sums = lax.optimization_barrier((own_a, own_b, pair, sums))
 
-    next_a, last_a = from_y(own_a, 1), from_y(own_a, 3)
+    next_a, last_b = from_y(own_a, 1), from_y(own_b, 3)
+    next_b, last_a = from_y(own_b, 1), from_y(own_a, 3)
     tokens = [pair] + [from_x(pair, step) for step in (1, 2, 3)]
-    next_a, last_a, tokens, late_b = lax.optimization_barrier((next_a, last_a, tokens, own_b))
-    next_b, last_b = from_y(late_b, 1), from_y(late_b, 3)
+    next_a, next_b, last_a, last_b, tokens = lax.optimization_barrier(
+        (next_a, next_b, last_a, last_b, tokens)
+    )
+    far_a, far_b = from_y(next_a, 1), from_y(last_b, 3)
     near = jnp.stack(tokens)
     far = swap_core(near)
     squares = token_sums(near).reshape(512)
     both = jnp.concatenate([sum(sums), squares + swap_core(squares)])
     both = both + swap_low(both)
-    near, far, both, next_a, next_b, last_a, last_b = lax.optimization_barrier(
-        (near, far, both, next_a, next_b, last_a, last_b)
-    )
-    far_a, far_b = from_y(next_a, 1), from_y(last_b, 3)
     factor_qkv = (scale_qkv / jnp.sqrt(both[:640])).reshape(1, 640)
     factor_out = (scale_out / jnp.sqrt(both[640:1152])).reshape(1, 512)
     inverse = lax.rsqrt(both[1152:] / 8192.0 + EPSILON).reshape(512, 1)
@@ -488,7 +485,7 @@
 
     def project(steps, blocks, total):
         place = [(y + step - x) % 4 for step in steps] + [(y + step) % 4 for step in steps]
-        place = jnp.stack(place + [c, zh ^ zl]).astype(jnp.int32)
+        place = jnp.stack(place + [c, zh]).astype(jnp.int32)
         return multiply_slabs(
             place, near, far, inverse, gains, blocks, ups, factor_qkv, total
         )
@@ -497,14 +494,19 @@
     total, far_a, far_b, weight_a, weight_b = lax.optimization_barrier(
         (total, far_a, far_b, weight_a, weight_b)
     )
-    other, mine = project((2,), (far_a, far_b), total)
+    total = project((2,), (far_a, far_b), total)
 
     rows_o = [weight_a, weight_b, from_y(weight_a, 1), from_y(weight_b, 1)]
     rows_last = [from_y(weight_a, 3), from_y(weight_b, 3)]
-    rows_o += [from_y(rows_o[2], 1), from_y(rows_last[1], 3)] + rows_last
-
-    projected = (mine + swap_low(other)).astype(bf16).reshape(16, 16, 640)
-    every = lax.all_to_all(projected, "tp", 0, 0, tiled=True)
+
+    groups = [[32 * k + i for i in range(32)] for k in range(4)]
+    halves = lax.all_to_all(
+        total.reshape(32, 16, 640), AXES, 0, 0, axis_index_groups=groups, tiled=True
+    )
+    every = jnp.sum(halves.reshape(2, 16, 16, 640), axis=0).astype(bf16)
+    rows_next, rows_before, every = lax.optimization_barrier((rows_o[2], rows_last[1], every))
+    rows_o += [from_y(rows_next, 1), from_y(rows_before, 3)] + rows_last
+
     place = jnp.stack([y, zl]).astype(jnp.int32)
     attended = attend(place, lengths, every, cached_key_rows, cached_value_rows)
 

time: 238 us -> 230 us (0.966)
  waiting for transfers between devices: 105 us -> 102 us
  local copies, waits for them, and re-layouts: 16.9 us -> 14.3 us
    ppermute x38 -> x37, waiting for transfers between devices: 72 us -> 61.5 us  [permute(): return lax.ppermute(value, AXES, pairs)]
    all_to_all x1, waiting for transfers between devices: 9.11 us -> 15.5 us  [per_device(): lax.all_to_all(total.reshape(32, 16, 640), AXES, 0, 0, axis_index_groups=...]
    ppermute x38 -> x37, starting transfers between devices: 45.3 us -> 47.5 us  [permute(): return lax.ppermute(value, AXES, pairs)]
    unnamed x40 -> x32, local copies, waits for them, and re-layouts: 6.11 us -> 4.8 us
  transfers between devices with their start and end apart: 40 -> 39, of which waited for: 20 -> 16; matrix products, arithmetic and copies ran while one was open for 7% -> 6% of each run, Pallas kernels for 12% -> 12%
where the time goes in v3:
time: 230 us; the launch traced here: 229 us
  waiting for transfers between devices  102 us (44%)
  starting transfers between devices  65.7 us (29%)
  Pallas kernels  39.8 us (17%)
  local copies, waits for them, and re-layouts  14.3 us (6%)
  other arithmetic  7.27 us (3%)
    ppermute x37, waiting for transfers between devices, permute(): return lax.ppermute(value, AXES, pairs)  61.5 us
    ppermute x37, starting transfers between devices, permute(): return lax.ppermute(value, AXES, pairs)  47.5 us
    all_to_all x1, waiting for transfers between devices, per_device(): received = lax.all_to_all(frozen, 'tp', 0, 0, tiled=True)  24.7 us
    all_to_all x1, waiting for transfers between devices, per_device(): lax.all_to_all(total.reshape(32, 16, 640), AXES, 0, 0, axis_index_groups=...  15.5 us
    pallas_call x2, Pallas kernels, multiply_slabs(): pl.pallas_call(multiply_slabs_kernel, grid_spec=pltpu.PrefetchScalarGridS...  14.3 us
    pallas_call x1, Pallas kernels, attend(): pl.pallas_call(attend_kernel, grid_spec=pltpu.PrefetchScalarGridSpec(num_...  12.2 us
    all_to_all x1, starting transfers between devices, per_device(): received = lax.all_to_all(frozen, 'tp', 0, 0, tiled=True)  9.26 us
    all_to_all x1, starting transfers between devices, per_device(): lax.all_to_all(total.reshape(32, 16, 640), AXES, 0, 0, axis_index_groups=...  8.95 us
  transfers between devices with their start and end apart: 39, of which 16 were waited for; matrix products, arithmetic and copies ran while one was open for 6% of the time, Pallas kernels for 12%

profile of v3, /device:TPU:1, one launch (start us, length us, event | category | flops | bytes accessed | tf_op | source)
XLA Modules:
  0.0 229.1 jit_solution(16958909382558677717)
XLA Ops:
  0.0 4.1 %shard_map.163 = bf16[16,10,64,128]{3,2,1,0:T(8,128)(2,1)} custom-call(s32[1]{0:T(128)} %bitcast.11.place, bf16[64,8192]{1,0:T(8,128)(2,1)} %query.1, bf16[64,2048]{1,0:T(8,128)(2,1)} %key_value.1, bf16[64,8192]{1,0:T(8,128)(2,1)} %output.1, bf16[32,64]{1,0:T(8,128)(2,1)} %bitcast.89, bf16[32,64]{1,0:T(8,128)(2,1)} %bitcast.90, bf16[32,64]{1,0:T(8,128)(2,1)} %bitcast.91), custom_call_target="tpu_custom_call" | custom-call | bytes 4194304 | tf_op jit(solution)/shard_map/pallas_call | solution.py:82
  4.1 9.3 %all-to-all-start = ((bf16[16,10,64,128]{3,2,1,0:T(8,128)(2,1)}), bf16[16,10,64,128]{3,2,1,0:T(8,128)(2,1)S(1)}, u32[]{:S(2)}, u32[]{:S(2)}) async-start(bf16[16,10,64,128]{3,2,1,0:T(8,128)(2,1)} %shard_map.163), calls=%async_computation | async-start | bytes 5242880 | tf_op jit(solution)/shard_map/all_to_all | solution.py:427
  14.4 3.6 %collective-permute-start = (bf16[256,512]{1,0:T(8,128)(2,1)}, bf16[256,512]{1,0:T(8,128)(2,1)}, u32[]{:S(2)}, u32[]{:S(2)}) collective-permute-start(bf16[256,512]{1,0:T(8,128)(2,1)} %reshape.40), channel_id=1, source_target_pairs={{0,0},{1,1},{2,16},{3,17},{4,4},{5,5},{6,20},{7,21},{8,8},{9,9},{1... | collective-permute-start | bytes 786440 | tf_op jit(solution)/shard_map/ppermute | solution.py:29
  22.7 24.7 %all-to-all-done.received = bf16[16,10,64,128]{3,2,1,0:T(8,128)(2,1)S(1)} async-done(((bf16[16,10,64,128]{3,2,1,0:T(8,128)(2,1)}), bf16[16,10,64,128]{3,2,1,0:T(8,128)(2,1)S(1)}, u32[]{:S(2)}, u32[]{:S(2)}) %all-to-all-start) | async-done | bytes 2621472 | tf_op jit(solution)/shard_map/all_to_all | solution.py:427
  51.8 2.8 %collective-permute-start.2 = (f32[1152]{0:T(1024)S(1)}, f32[1152]{0:T(1024)S(1)}, u32[]{:S(2)}, u32[]{:S(2)}) collective-permute-start(f32[1152]{0:T(1024)S(1)} %reduce), channel_id=1, source_target_pairs={{0,96},{1,97},{2,98},{3,99},{4,100},{5,101},{6,102},{7,103},{8,104... | collective-permute-start | bytes 13832 | tf_op jit(solution)/shard_map/ppermute | solution.py:29
  63.8 7.2 %collective-permute-done.10 = bf16[512,512]{1,0:T(8,128)(2,1)S(1)} collective-permute-done((bf16[512,512]{1,0:T(8,128)(2,1)S(1)}, bf16[512,512]{1,0:T(8,128)(2,1)S(1)}, u32[]{:S(2)}, u32[]{:S(2)}) %collective-permute-start.10) | collective-permute-done | bytes 524320 | tf_op jit(solution)/shard_map/ppermute | solution.py:29
  71.0 14.2 %collective-permute-done.11 = bf16[512,512]{1,0:T(8,128)(2,1)S(1)} collective-permute-done((bf16[512,512]{1,0:T(8,128)(2,1)S(1)}, bf16[512,512]{1,0:T(8,128)(2,1)S(1)}, u32[]{:S(2)}, u32[]{:S(2)}) %collective-permute-start.11) | collective-permute-done | bytes 524320 | tf_op jit(solution)/shard_map/ppermute | solution.py:29
  85.3 13.0 %collective-permute-done.9 = bf16[512,512]{1,0:T(8,128)(2,1)S(1)} collective-permute-done((bf16[512,512]{1,0:T(8,128)(2,1)S(1)}, bf16[512,512]{1,0:T(8,128)(2,1)S(1)}, u32[]{:S(2)}, u32[]{:S(2)}) %collective-permute-start.9) | collective-permute-done | bytes 524320 | tf_op jit(solution)/shard_map/ppermute | solution.py:29
  101.9 2.8 %shard_map.165 = f32[512,1]{1,0:T(8,128)} custom-call(bf16[4,512,512]{2,1,0:T(8,128)(2,1)} %copy-done.9), custom_call_target="tpu_custom_call" | custom-call | flops 1048576 | bytes 4096 | tf_op jit(solution)/shard_map/pallas_call | solution.py:175
  113.5 2.7 %shard_map.167 = (bf16[512,512]{1,0:T(8,128)(2,1)}, bf16[512,512]{1,0:T(8,128)(2,1)}) custom-call(bf16[2,512,512]{2,1,0:T(8,128)(2,1)} %copy-done.3, bf16[2,512,128]{2,1,0:T(8,128)(2,1)} %copy-done.8, bf16[2,128,512]{2,1,0:T(8,128)(2,1)} %copy-done.2, f32[1,512]{1,0:T(1,128)} %bitcast.92), custom_call_target="tpu_custom_call" | custom-call | flops 1048576 | bytes 4096 | tf_op jit(solution)/shard_map/pallas_call | solution.py:157
  116.1 9.0 %shard_map.166.refs_8_ = f32[512,640]{1,0:T(8,128)} custom-call(s32[8]{0:T(128)} %stack.152.place, bf16[4,512,512]{2,1,0:T(8,128)(2,1)} %copy-done.9, bf16[4,512,512]{2,1,0:T(8,128)(2,1)} %collective-permute-done.12.refs_1_.refs_4_.refs_7_, f32[4,2,1,512]{3,2,1,0:T(1,128)} %dynamic-slice_bitcast_fusion.refs_2_.refs_5_.refs_8_, ...), custom_call_target="tpu_custom_call" | custom-call | flops 1048576 | bytes 4096 | tf_op jit(solution)/shard_map/pallas_call | solution.py:228
  125.7 5.4 %shard_map.168 = f32[512,640]{1,0:T(8,128)} custom-call(s32[4]{0:T(128)} %pad_add_fusion.2.place, bf16[4,512,512]{2,1,0:T(8,128)(2,1)} %copy-done.9, bf16[4,512,512]{2,1,0:T(8,128)(2,1)} %collective-permute-done.12.refs_1_.refs_4_.refs_7_, f32[4,2,1,512]{3,2,1,0:T(1,128)} %dynamic-slice_bitcast_fusion.refs_2_.refs_5_.refs_8_, ...), custom_call_target="tpu_custom_call" | custom-call | flops 1048576 | bytes 4096 | tf_op jit(solution)/shard_map/pallas_call | solution.py:228
  131.1 9.0 %all-to-all-start.1 = ((f32[32,16,640]{2,1,0:T(8,128)}), f32[32,16,640]{2,1,0:T(8,128)}, u32[]{:S(2)}, u32[]{:S(2)}) async-start(f32[32,16,640]{2,1,0:T(8,128)} %bitcast.69), calls=%async_computation.1 | async-start | bytes 2621440 | tf_op jit(solution)/shard_map/all_to_all | solution.py:503
  142.0 2.7 %collective-permute-start.19 = (bf16[512,512]{1,0:T(8,128)(2,1)S(1)}, bf16[512,512]{1,0:T(8,128)(2,1)S(1)}, u32[]{:S(2)}, u32[]{:S(2)}) collective-permute-start(bf16[512,512]{1,0:T(8,128)(2,1)S(1)} %copy-done.7), channel_id=1, source_target_pairs={{0,96},{1,97},{2,98},{3,99},{4,100},{5,101},{6,102},{7,103},{8,104... | collective-permute-start | bytes 1572872 | tf_op jit(solution)/shard_map/ppermute | solution.py:29
  144.6 15.5 %all-to-all-done.1 = f32[32,16,640]{2,1,0:T(8,128)} async-done(((f32[32,16,640]{2,1,0:T(8,128)}), f32[32,16,640]{2,1,0:T(8,128)}, u32[]{:S(2)}, u32[]{:S(2)}) %all-to-all-start.1) | async-done | bytes 1310752 | tf_op jit(solution)/shard_map/all_to_all | solution.py:503
  164.7 12.2 %shard_map.169 = bf16[8,16,1024]{2,1,0:T(8,128)(2,1)} custom-call(s32[2]{0:T(128)} %pad_add_fusion.1.place, s32[4]{0:T(128)} %lengths.1, bf16[16,16,640]{2,1,0:T(8,128)(2,1)} %reduce_sum.9.every, bf16[4,8,1024,128]{3,2,1,0:T(8,128)(2,1)} %keys.1, bf16[4,8,1024,128]{3,2,1,0:T(8,128)(2,1)} %values.1), custom_call_target="tpu_custom_call" | custom-call | flops 1048576 | bytes 4096 | tf_op jit(solution)/shard_map/pallas_call | solution.py:315
  181.8 2.5 %collective-permute-start.28 = (bf16[2,2,16,1024]{3,2,1,0:T(8,128)(2,1)S(1)}, bf16[2,2,16,1024]{3,2,1,0:T(8,128)(2,1)S(1)}, u32[]{:S(2)}, u32[]{:S(2)}) collective-permute-start(bf16[2,2,16,1024]{3,2,1,0:T(8,128)(2,1)S(1)} %get-tuple-element.101), channel_id=1, source_target_pairs={{0,12},{1,13},{2,14},{3,15},{4,0},{5,1},{6,2},{7,3},{8,4},{9,5},{1... | collective-permute-start | bytes 393224 | tf_op jit(solution)/shard_map/ppermute | solution.py:29
  185.4 2.5 %collective-permute-start.24 = (bf16[2,2,16,1024]{3,2,1,0:T(8,128)(2,1)S(1)}, bf16[2,2,16,1024]{3,2,1,0:T(8,128)(2,1)S(1)}, u32[]{:S(2)}, u32[]{:S(2)}) collective-permute-start(bf16[2,2,16,1024]{3,2,1,0:T(8,128)(2,1)S(1)} %pad_maximum_fusion.8), channel_id=1, source_target_pairs={{0,2},{1,3},{2,0},{3,1},{4,6},{5,7},{6,4},{7,5},{8,10},{9,11},{10,... | collective-permute-start | bytes 393224 | tf_op jit(solution)/shard_map/ppermute | solution.py:29
  192.0 2.5 %collective-permute-start.33 = (bf16[4,2,16,1024]{3,2,1,0:T(8,128)(2,1)S(1)}, bf16[4,2,16,1024]{3,2,1,0:T(8,128)(2,1)S(1)}, u32[]{:S(2)}, u32[]{:S(2)}) collective-permute-start(bf16[4,2,16,1024]{3,2,1,0:T(8,128)(2,1)S(1)} %get-tuple-element.99), channel_id=1, source_target_pairs={{0,18},{1,19},{2,16},{3,17},{4,22},{5,23},{6,20},{7,21},{8,26},{9,... | collective-permute-start | bytes 786440 | tf_op jit(solution)/shard_map/ppermute | solution.py:29
  196.2 7.2 %collective-permute-done.31 = bf16[4,2,16,1024]{3,2,1,0:T(8,128)(2,1)S(1)} collective-permute-done((bf16[4,2,16,1024]{3,2,1,0:T(8,128)(2,1)S(1)}, bf16[4,2,16,1024]{3,2,1,0:T(8,128)(2,1)S(1)}, u32[]{:S(2)}, u32[]{:S(2)}) %collective-permute-start.31) | collective-permute-done | bytes 262176 | tf_op jit(solution)/shard_map/ppermute | solution.py:29
  204.4 3.6 %collective-permute-start.35 = (bf16[4,4,2,16,1024]{4,3,2,1,0:T(8,128)(2,1)S(1)}, bf16[4,4,2,16,1024]{4,3,2,1,0:T(8,128)(2,1)S(1)}, u32[]{:S(2)}, u32[]{:S(2)}) collective-permute-start(bf16[4,4,2,16,1024]{4,3,2,1,0:T(8,128)(2,1)S(1)} %pad_maximum_fusion.2.near_b), channel_id=1, source_target_pairs={{0,1},{1,0},{2,3},{3,2},{4,5},{5,4},{6,7},{7,6},{8,9},{9,8},{10,11... | collective-permute-start | bytes 3145736 | tf_op jit(solution)/shard_map/ppermute | solution.py:29
  210.4 5.1 %collective-permute-start.34 = (bf16[4,4,2,16,1024]{4,3,2,1,0:T(8,128)(2,1)S(1)}, bf16[4,4,2,16,1024]{4,3,2,1,0:T(8,128)(2,1)S(1)}, u32[]{:S(2)}, u32[]{:S(2)}) collective-permute-start(bf16[4,4,2,16,1024]{4,3,2,1,0:T(8,128)(2,1)S(1)} %pad_maximum_fusion.1.near_a), channel_id=1, source_target_pairs={{0,1},{1,0},{2,3},{3,2},{4,5},{5,4},{6,7},{7,6},{8,9},{9,8},{10,11... | collective-permute-start | bytes 3145736 | tf_op jit(solution)/shard_map/ppermute | solution.py:29
  217.7 2.9 %shard_map.170 = (f32[16,16,512]{2,1,0:T(8,128)S(1)}, bf16[16,16,512]{2,1,0:T(8,128)(2,1)S(1)}) custom-call(s32[3]{0:T(128)S(1)} %pad_add_fusion.place, bf16[4,4,2,16,1024]{4,3,2,1,0:T(8,128)(2,1)S(1)} %pad_maximum_fusion.1.near_a, bf16[4,4,2,16,1024]{4,3,2,1,0:T(8,128)(2,1)S(1)} %pad_maximum_fusion.2.near_b, ...), custom_call_target="tpu_custom_call" | custom-call | flops 2147483648 | bytes 8388608 | tf_op jit(solution)/shard_map/pallas_call | solution.py:369
  220.9 7.3 %collective-permute-done.36 = bf16[16,16,512]{2,1,0:T(8,128)(2,1)S(1)} collective-permute-done((bf16[16,16,512]{2,1,0:T(8,128)(2,1)S(1)}, bf16[16,16,512]{2,1,0:T(8,128)(2,1)S(1)}, u32[]{:S(2)}, u32[]{:S(2)}) %collective-permute-start.36) | collective-permute-done | bytes 262176 | tf_op jit(solution)/shard_map/ppermute | solution.py:29
  (143 shorter events, 57.3 us)
Async XLA Ops:
  4.1 43.3 %all-to-all-start = ((bf16[16,10,64,128]{3,2,1,0:T(8,128)(2,1)}), bf16[16,10,64,128]{3,2,1,0:T(8,128)(2,1)S(1)}, u32[]{:S(2)}, u32[]{:S(2)}) async-start(bf16[16,10,64,128]{3,2,1,0:T(8,128)(2,1)} %shard_map.163), calls=%async_computation | async-start | bytes 5242880 | tf_op jit(solution)/shard_map/all_to_all | solution.py:427
  14.4 41.2 %collective-permute-start = (bf16[256,512]{1,0:T(8,128)(2,1)}, bf16[256,512]{1,0:T(8,128)(2,1)}, u32[]{:S(2)}, u32[]{:S(2)}) collective-permute-start(bf16[256,512]{1,0:T(8,128)(2,1)} %reshape.40), channel_id=1, source_target_pairs={{0,0},{1,1},{2,16},{3,17},{4,4},{5,5},{6,20},{7,21},{8,8},{9,9},{1... | collective-permute-start | bytes 786440 | tf_op jit(solution)/shard_map/ppermute | solution.py:29
  18.0 37.7 %collective-permute-start.1 = (bf16[256,512]{1,0:T(8,128)(2,1)}, bf16[256,512]{1,0:T(8,128)(2,1)}, u32[]{:S(2)}, u32[]{:S(2)}) collective-permute-start(bf16[256,512]{1,0:T(8,128)(2,1)} %reshape.40), channel_id=1, source_target_pairs={{0,2},{1,3},{2,18},{3,19},{4,6},{5,7},{6,22},{7,23},{8,10},{9,11},... | collective-permute-start | bytes 786440 | tf_op jit(solution)/shard_map/ppermute | solution.py:29
  58.7 12.3 %collective-permute-start.10 = (bf16[512,512]{1,0:T(8,128)(2,1)S(1)}, bf16[512,512]{1,0:T(8,128)(2,1)S(1)}, u32[]{:S(2)}, u32[]{:S(2)}) collective-permute-start(bf16[512,512]{1,0:T(8,128)(2,1)S(1)} %pad_maximum_fusion.3), channel_id=1, source_target_pairs={{0,8},{1,9},{2,10},{3,11},{4,12},{5,13},{6,14},{7,15},{8,0},{9,1},... | collective-permute-start | bytes 1572872 | tf_op jit(solution)/shard_map/ppermute | solution.py:29
  60.3 25.0 %collective-permute-start.11 = (bf16[512,512]{1,0:T(8,128)(2,1)S(1)}, bf16[512,512]{1,0:T(8,128)(2,1)S(1)}, u32[]{:S(2)}, u32[]{:S(2)}) collective-permute-start(bf16[512,512]{1,0:T(8,128)(2,1)S(1)} %pad_maximum_fusion.3), channel_id=1, source_target_pairs={{0,4},{1,5},{2,6},{3,7},{4,8},{5,9},{6,10},{7,11},{8,12},{9,13},{1... | collective-permute-start | bytes 1572872 | tf_op jit(solution)/shard_map/ppermute | solution.py:29
  60.7 37.5 %collective-permute-start.5 = (bf16[6,512,128]{2,1,0:T(8,128)(2,1)}, bf16[6,512,128]{2,1,0:T(8,128)(2,1)S(1)}, u32[]{:S(2)}, u32[]{:S(2)}) collective-permute-start(bf16[6,512,128]{2,1,0:T(8,128)(2,1)} %copy-done.4), channel_id=1, source_target_pairs={{0,96},{1,97},{2,98},{3,99},{4,100},{5,101},{6,102},{7,103},{8,104... | collective-permute-start | bytes 2359304 | tf_op jit(solution)/shard_map/ppermute | solution.py:29
  61.1 37.2 %collective-permute-start.7 = (bf16[6,512,128]{2,1,0:T(8,128)(2,1)}, bf16[6,512,128]{2,1,0:T(8,128)(2,1)S(1)}, u32[]{:S(2)}, u32[]{:S(2)}) collective-permute-start(bf16[6,512,128]{2,1,0:T(8,128)(2,1)} %copy-done.4), channel_id=1, source_target_pairs={{0,32},{1,33},{2,34},{3,35},{4,36},{5,37},{6,38},{7,39},{8,40},{9,... | collective-permute-start | bytes 2359304 | tf_op jit(solution)/shard_map/ppermute | solution.py:29
  62.2 36.1 %collective-permute-start.6 = (bf16[5,512,128]{2,1,0:T(8,128)(2,1)}, bf16[5,512,128]{2,1,0:T(8,128)(2,1)S(1)}, u32[]{:S(2)}, u32[]{:S(2)}) collective-permute-start(bf16[5,512,128]{2,1,0:T(8,128)(2,1)} %copy-done.5), channel_id=1, source_target_pairs={{0,96},{1,97},{2,98},{3,99},{4,100},{5,101},{6,102},{7,103},{8,104... | collective-permute-start | bytes 1966088 | tf_op jit(solution)/shard_map/ppermute | solution.py:29
  71.0 27.2 %collective-permute-start.8 = (bf16[5,512,128]{2,1,0:T(8,128)(2,1)}, bf16[5,512,128]{2,1,0:T(8,128)(2,1)S(1)}, u32[]{:S(2)}, u32[]{:S(2)}) collective-permute-start(bf16[5,512,128]{2,1,0:T(8,128)(2,1)} %copy-done.5), channel_id=1, source_target_pairs={{0,32},{1,33},{2,34},{3,35},{4,36},{5,37},{6,38},{7,39},{8,40},{9,... | collective-permute-start | bytes 1966088 | tf_op jit(solution)/shard_map/ppermute | solution.py:29
  85.3 13.0 %collective-permute-start.9 = (bf16[512,512]{1,0:T(8,128)(2,1)S(1)}, bf16[512,512]{1,0:T(8,128)(2,1)S(1)}, u32[]{:S(2)}, u32[]{:S(2)}) collective-permute-start(bf16[512,512]{1,0:T(8,128)(2,1)S(1)} %pad_maximum_fusion.3), channel_id=1, source_target_pairs={{0,12},{1,13},{2,14},{3,15},{4,0},{5,1},{6,2},{7,3},{8,4},{9,5},{1... | collective-permute-start | bytes 1572872 | tf_op jit(solution)/shard_map/ppermute | solution.py:29
  99.9 16.2 %collective-permute-start.12 = (bf16[4,512,512]{2,1,0:T(8,128)(2,1)S(1)}, bf16[4,512,512]{2,1,0:T(8,128)(2,1)}, u32[]{:S(2)}, u32[]{:S(2)}) collective-permute-start(bf16[4,512,512]{2,1,0:T(8,128)(2,1)S(1)} %pad_maximum_fusion.near.refs_0_.refs_3_.refs_6_), channel_id=1, source_target_pairs={{0,1},{1,0},{2,3},{3,2},{4,5},{5,4},{6,7},{7,6},{8,9},{9,8},{10,11... | collective-permute-start | bytes 6291464 | tf_op jit(solution)/shard_map/ppermute | solution.py:29
  106.5 19.2 %collective-permute-start.15 = (bf16[6,512,128]{2,1,0:T(8,128)(2,1)S(1)}, bf16[6,512,128]{2,1,0:T(8,128)(2,1)}, u32[]{:S(2)}, u32[]{:S(2)}) collective-permute-start(bf16[6,512,128]{2,1,0:T(8,128)(2,1)S(1)} %collective-permute-done.5.refs_14_), channel_id=1, source_target_pairs={{0,96},{1,97},{2,98},{3,99},{4,100},{5,101},{6,102},{7,103},{8,104... | collective-permute-start | bytes 2359304 | tf_op jit(solution)/shard_map/ppermute | solution.py:29
  106.9 18.2 %collective-permute-start.16 = (bf16[5,512,128]{2,1,0:T(8,128)(2,1)}, bf16[5,512,128]{2,1,0:T(8,128)(2,1)}, u32[]{:S(2)}, u32[]{:S(2)}) collective-permute-start(bf16[5,512,128]{2,1,0:T(8,128)(2,1)} %copy-done.13), channel_id=1, source_target_pairs={{0,32},{1,33},{2,34},{3,35},{4,36},{5,37},{6,38},{7,39},{8,40},{9,... | collective-permute-start | bytes 1966088 | tf_op jit(solution)/shard_map/ppermute | solution.py:29
  131.1 29.0 %all-to-all-start.1 = ((f32[32,16,640]{2,1,0:T(8,128)}), f32[32,16,640]{2,1,0:T(8,128)}, u32[]{:S(2)}, u32[]{:S(2)}) async-start(f32[32,16,640]{2,1,0:T(8,128)} %bitcast.69), calls=%async_computation.1 | async-start | bytes 2621440 | tf_op jit(solution)/shard_map/all_to_all | solution.py:503
  140.1 22.2 %collective-permute-start.17 = (bf16[512,512]{1,0:T(8,128)(2,1)S(1)}, bf16[512,512]{1,0:T(8,128)(2,1)S(1)}, u32[]{:S(2)}, u32[]{:S(2)}) collective-permute-start(bf16[512,512]{1,0:T(8,128)(2,1)S(1)} %copy-done.6), channel_id=1, source_target_pairs={{0,96},{1,97},{2,98},{3,99},{4,100},{5,101},{6,102},{7,103},{8,104... | collective-permute-start | bytes 1572872 | tf_op jit(solution)/shard_map/ppermute | solution.py:29
  142.0 20.4 %collective-permute-start.18 = (bf16[512,512]{1,0:T(8,128)(2,1)S(1)}, bf16[512,512]{1,0:T(8,128)(2,1)S(1)}, u32[]{:S(2)}, u32[]{:S(2)}) collective-permute-start(bf16[512,512]{1,0:T(8,128)(2,1)S(1)} %copy-done.7), channel_id=1, source_target_pairs={{0,32},{1,33},{2,34},{3,35},{4,36},{5,37},{6,38},{7,39},{8,40},{9,... | collective-permute-start | bytes 1572872 | tf_op jit(solution)/shard_map/ppermute | solution.py:29
  142.0 34.9 %collective-permute-start.19 = (bf16[512,512]{1,0:T(8,128)(2,1)S(1)}, bf16[512,512]{1,0:T(8,128)(2,1)S(1)}, u32[]{:S(2)}, u32[]{:S(2)}) collective-permute-start(bf16[512,512]{1,0:T(8,128)(2,1)S(1)} %copy-done.7), channel_id=1, source_target_pairs={{0,96},{1,97},{2,98},{3,99},{4,100},{5,101},{6,102},{7,103},{8,104... | collective-permute-start | bytes 1572872 | tf_op jit(solution)/shard_map/ppermute | solution.py:29
  144.6 32.3 %collective-permute-start.22 = (bf16[512,512]{1,0:T(8,128)(2,1)S(1)}, bf16[512,512]{1,0:T(8,128)(2,1)S(1)}, u32[]{:S(2)}, u32[]{:S(2)}) collective-permute-start(bf16[512,512]{1,0:T(8,128)(2,1)S(1)} %copy-done.6), channel_id=1, source_target_pairs={{0,32},{1,33},{2,34},{3,35},{4,36},{5,37},{6,38},{7,39},{8,40},{9,... | collective-permute-start | bytes 1572872 | tf_op jit(solution)/shard_map/ppermute | solution.py:29
  162.4 14.6 %collective-permute-start.20 = (bf16[512,512]{1,0:T(8,128)(2,1)S(1)}, bf16[512,512]{1,0:T(8,128)(2,1)S(1)}, u32[]{:S(2)}, u32[]{:S(2)}) collective-permute-start(bf16[512,512]{1,0:T(8,128)(2,1)S(1)} %collective-permute-done.17.refs_2_), channel_id=1, source_target_pairs={{0,96},{1,97},{2,98},{3,99},{4,100},{5,101},{6,102},{7,103},{8,104... | collective-permute-start | bytes 1572872 | tf_op jit(solution)/shard_map/ppermute | solution.py:29
  164.1 14.5 %collective-permute-start.21 = (bf16[512,512]{1,0:T(8,128)(2,1)S(1)}, bf16[512,512]{1,0:T(8,128)(2,1)S(1)}, u32[]{:S(2)}, u32[]{:S(2)}) collective-permute-start(bf16[512,512]{1,0:T(8,128)(2,1)S(1)} %collective-permute-done.18.refs_7_), channel_id=1, source_target_pairs={{0,32},{1,33},{2,34},{3,35},{4,36},{5,37},{6,38},{7,39},{8,40},{9,... | collective-permute-start | bytes 1572872 | tf_op jit(solution)/shard_map/ppermute | solution.py:29
  191.7 12.5 %collective-permute-start.32 = (bf16[4,2,16,1024]{3,2,1,0:T(8,128)(2,1)S(1)}, bf16[4,2,16,1024]{3,2,1,0:T(8,128)(2,1)S(1)}, u32[]{:S(2)}, u32[]{:S(2)}) collective-permute-start(bf16[4,2,16,1024]{3,2,1,0:T(8,128)(2,1)S(1)} %get-tuple-element.99), channel_id=1, source_target_pairs={{0,16},{1,17},{2,18},{3,19},{4,20},{5,21},{6,22},{7,23},{8,24},{9,... | collective-permute-start | bytes 786440 | tf_op jit(solution)/shard_map/ppermute | solution.py:29
  192.0 12.2 %collective-permute-start.33 = (bf16[4,2,16,1024]{3,2,1,0:T(8,128)(2,1)S(1)}, bf16[4,2,16,1024]{3,2,1,0:T(8,128)(2,1)S(1)}, u32[]{:S(2)}, u32[]{:S(2)}) collective-permute-start(bf16[4,2,16,1024]{3,2,1,0:T(8,128)(2,1)S(1)} %get-tuple-element.99), channel_id=1, source_target_pairs={{0,18},{1,19},{2,16},{3,17},{4,22},{5,23},{6,20},{7,21},{8,26},{9,... | collective-permute-start | bytes 786440 | tf_op jit(solution)/shard_map/ppermute | solution.py:29
  195.1 12.9 %collective-permute-start.25 = (bf16[4,2,16,1024]{3,2,1,0:T(8,128)(2,1)S(1)}, bf16[4,2,16,1024]{3,2,1,0:T(8,128)(2,1)S(1)}, u32[]{:S(2)}, u32[]{:S(2)}) collective-permute-start(bf16[4,2,16,1024]{3,2,1,0:T(8,128)(2,1)S(1)} %get-tuple-element.103), channel_id=1, source_target_pairs={{0,12},{1,13},{2,14},{3,15},{4,0},{5,1},{6,2},{7,3},{8,4},{9,5},{1... | collective-permute-start | bytes 786440 | tf_op jit(solution)/shard_map/ppermute | solution.py:29
  195.7 12.3 %collective-permute-start.26 = (bf16[4,2,16,1024]{3,2,1,0:T(8,128)(2,1)S(1)}, bf16[4,2,16,1024]{3,2,1,0:T(8,128)(2,1)S(1)}, u32[]{:S(2)}, u32[]{:S(2)}) collective-permute-start(bf16[4,2,16,1024]{3,2,1,0:T(8,128)(2,1)S(1)} %get-tuple-element.103), channel_id=1, source_target_pairs={{0,8},{1,9},{2,10},{3,11},{4,12},{5,13},{6,14},{7,15},{8,0},{9,1},... | collective-permute-start | bytes 786440 | tf_op jit(solution)/shard_map/ppermute | solution.py:29
  (31 other events, 230.3 us)

commit v4 on v3

--- a/solution.py
+++ b/solution.py
@@ -467,11 +467,11 @@
     next_a, last_b = from_y(own_a, 1), from_y(own_b, 3)
     next_b, last_a = from_y(own_b, 1), from_y(own_a, 3)
     tokens = [pair] + [from_x(pair, step) for step in (1, 2, 3)]
-    next_a, next_b, last_a, last_b, tokens = lax.optimization_barrier(
-        (next_a, next_b, last_a, last_b, tokens)
+    near = jnp.stack(tokens)
+    next_a, next_b, last_a, last_b, near = lax.optimization_barrier(
+        (next_a, next_b, last_a, last_b, near)
     )
     far_a, far_b = from_y(next_a, 1), from_y(last_b, 3)
-    near = jnp.stack(tokens)
     far = swap_core(near)
     squares = token_sums(near).reshape(512)
     both = jnp.concatenate([sum(sums), squares + swap_core(squares)])
@@ -491,9 +491,8 @@
         )
 
     total = project((0, 1, 3), (own_a, own_b, next_a, next_b, last_a, last_b), None)
-    total, far_a, far_b, weight_a, weight_b = lax.optimization_barrier(
-        (total, far_a, far_b, weight_a, weight_b)
-    )
+    total, far_a, far_b = lax.optimization_barrier((total, far_a, far_b))
+    weight_a, weight_b = lax.optimization_barrier((weight_a, weight_b, far_a))[:2]
     total = project((2,), (far_a, far_b), total)
 
     rows_o = [weight_a, weight_b, from_y(weight_a, 1), from_y(weight_b, 1)]

time: 230 us -> 228 us (level)
  waiting for transfers between devices: 102 us -> 92.8 us
  starting transfers between devices: 65.7 us -> 74.3 us
    ppermute x37, starting transfers between devices: 47.5 us -> 55.7 us  [permute(): return lax.ppermute(value, AXES, pairs)]
    ppermute x37, waiting for transfers between devices: 61.5 us -> 56.3 us  [permute(): return lax.ppermute(value, AXES, pairs)]
    unnamed x32 -> x30, local copies, waits for them, and re-layouts: 4.8 us -> 4.35 us
  transfers between devices with their start and end apart: 39 -> 39, of which waited for: 16 -> 19; matrix products, arithmetic and copies ran while one was open for 6% -> 6% of each run, Pallas kernels for 12% -> 12%
where the time goes in v4:
time: 228 us; the launch traced here: 227 us
  waiting for transfers between devices  92.8 us (41%)
  starting transfers between devices  74.3 us (33%)
  Pallas kernels  39.8 us (17%)
  local copies, waits for them, and re-layouts  13.9 us (6%)
  other arithmetic  5.86 us (3%)
    ppermute x37, waiting for transfers between devices, permute(): return lax.ppermute(value, AXES, pairs)  56.3 us
    ppermute x37, starting transfers between devices, permute(): return lax.ppermute(value, AXES, pairs)  55.7 us
    all_to_all x1, waiting for transfers between devices, per_device(): received = lax.all_to_all(frozen, 'tp', 0, 0, tiled=True)  23.1 us
    pallas_call x2, Pallas kernels, multiply_slabs(): pl.pallas_call(multiply_slabs_kernel, grid_spec=pltpu.PrefetchScalarGridS...  14.4 us
    all_to_all x1, waiting for transfers between devices, per_device(): lax.all_to_all(total.reshape(32, 16, 640), AXES, 0, 0, axis_index_groups=...  13.4 us
    pallas_call x1, Pallas kernels, attend(): pl.pallas_call(attend_kernel, grid_spec=pltpu.PrefetchScalarGridSpec(num_...  12.2 us
    all_to_all x1, starting transfers between devices, per_device(): lax.all_to_all(total.reshape(32, 16, 640), AXES, 0, 0, axis_index_groups=...  9.34 us
    all_to_all x1, starting transfers between devices, per_device(): received = lax.all_to_all(frozen, 'tp', 0, 0, tiled=True)  9.26 us
  transfers between devices with their start and end apart: 39, of which 19 were waited for; matrix products, arithmetic and copies ran while one was open for 6% of the time, Pallas kernels for 12%

profile of v4, /device:TPU:1, one launch (start us, length us, event | category | flops | bytes accessed | tf_op | source)
XLA Modules:
  0.0 227.1 jit_solution(9292370724397231844)
XLA Ops:
  0.0 4.2 %shard_map.163 = bf16[16,10,64,128]{3,2,1,0:T(8,128)(2,1)} custom-call(s32[1]{0:T(128)} %bitcast.5.place, bf16[64,8192]{1,0:T(8,128)(2,1)} %query.1, bf16[64,2048]{1,0:T(8,128)(2,1)} %key_value.1, bf16[64,8192]{1,0:T(8,128)(2,1)} %output.1, bf16[32,64]{1,0:T(8,128)(2,1)} %bitcast.90, bf16[32,64]{1,0:T(8,128)(2,1)} %bitcast.91, bf16[32,64]{1,0:T(8,128)(2,1)} %bitcast.92), custom_call_target="tpu_custom_call" | custom-call | bytes 4194304 | tf_op jit(solution)/shard_map/pallas_call | solution.py:82
  4.2 9.3 %all-to-all-start = ((bf16[16,10,64,128]{3,2,1,0:T(8,128)(2,1)}), bf16[16,10,64,128]{3,2,1,0:T(8,128)(2,1)S(1)}, u32[]{:S(2)}, u32[]{:S(2)}) async-start(bf16[16,10,64,128]{3,2,1,0:T(8,128)(2,1)} %shard_map.163), calls=%async_computation | async-start | bytes 5242880 | tf_op jit(solution)/shard_map/all_to_all | solution.py:427
  14.4 2.9 %collective-permute-start.1 = (bf16[256,512]{1,0:T(8,128)(2,1)}, bf16[256,512]{1,0:T(8,128)(2,1)}, u32[]{:S(2)}, u32[]{:S(2)}) collective-permute-start(bf16[256,512]{1,0:T(8,128)(2,1)} %reshape.40), channel_id=1, source_target_pairs={{0,2},{1,3},{2,18},{3,19},{4,6},{5,7},{6,22},{7,23},{8,10},{9,11},... | collective-permute-start | bytes 786440 | tf_op jit(solution)/shard_map/ppermute | solution.py:29
  17.3 3.6 %collective-permute-start = (bf16[256,512]{1,0:T(8,128)(2,1)}, bf16[256,512]{1,0:T(8,128)(2,1)}, u32[]{:S(2)}, u32[]{:S(2)}) collective-permute-start(bf16[256,512]{1,0:T(8,128)(2,1)} %reshape.40), channel_id=1, source_target_pairs={{0,0},{1,1},{2,16},{3,17},{4,4},{5,5},{6,20},{7,21},{8,8},{9,9},{1... | collective-permute-start | bytes 786440 | tf_op jit(solution)/shard_map/ppermute | solution.py:29
  24.4 23.1 %all-to-all-done.received = bf16[16,10,64,128]{3,2,1,0:T(8,128)(2,1)S(1)} async-done(((bf16[16,10,64,128]{3,2,1,0:T(8,128)(2,1)}), bf16[16,10,64,128]{3,2,1,0:T(8,128)(2,1)S(1)}, u32[]{:S(2)}, u32[]{:S(2)}) %all-to-all-start) | async-done | bytes 2621472 | tf_op jit(solution)/shard_map/all_to_all | solution.py:427
  51.8 2.8 %collective-permute-start.2 = (f32[1152]{0:T(1024)S(1)}, f32[1152]{0:T(1024)S(1)}, u32[]{:S(2)}, u32[]{:S(2)}) collective-permute-start(f32[1152]{0:T(1024)S(1)} %reduce), channel_id=1, source_target_pairs={{0,96},{1,97},{2,98},{3,99},{4,100},{5,101},{6,102},{7,103},{8,104... | collective-permute-start | bytes 13832 | tf_op jit(solution)/shard_map/ppermute | solution.py:29
  63.9 6.9 %collective-permute-done.11 = bf16[512,512]{1,0:T(8,128)(2,1)S(1)} collective-permute-done((bf16[512,512]{1,0:T(8,128)(2,1)S(1)}, bf16[512,512]{1,0:T(8,128)(2,1)S(1)}, u32[]{:S(2)}, u32[]{:S(2)}) %collective-permute-start.11) | collective-permute-done | bytes 524320 | tf_op jit(solution)/shard_map/ppermute | solution.py:29
  71.3 10.7 %collective-permute-done.10 = bf16[512,512]{1,0:T(8,128)(2,1)S(1)} collective-permute-done((bf16[512,512]{1,0:T(8,128)(2,1)S(1)}, bf16[512,512]{1,0:T(8,128)(2,1)S(1)}, u32[]{:S(2)}, u32[]{:S(2)}) %collective-permute-start.10) | collective-permute-done | bytes 524320 | tf_op jit(solution)/shard_map/ppermute | solution.py:29
  84.8 6.6 %collective-permute-done.6.refs_15_ = bf16[5,512,128]{2,1,0:T(8,128)(2,1)S(1)} collective-permute-done((bf16[5,512,128]{2,1,0:T(8,128)(2,1)}, bf16[5,512,128]{2,1,0:T(8,128)(2,1)S(1)}, u32[]{:S(2)}, u32[]{:S(2)}) %collective-permute-start.6) | collective-permute-done | bytes 655392 | tf_op jit(solution)/shard_map/ppermute | solution.py:29
  91.5 4.6 %collective-permute-done.8.refs_17_ = bf16[5,512,128]{2,1,0:T(8,128)(2,1)S(1)} collective-permute-done((bf16[5,512,128]{2,1,0:T(8,128)(2,1)}, bf16[5,512,128]{2,1,0:T(8,128)(2,1)S(1)}, u32[]{:S(2)}, u32[]{:S(2)}) %collective-permute-start.8) | collective-permute-done | bytes 655392 | tf_op jit(solution)/shard_map/ppermute | solution.py:29
  97.0 4.4 %collective-permute-start.14 = (bf16[4,512,512]{2,1,0:T(8,128)(2,1)S(1)}, bf16[4,512,512]{2,1,0:T(8,128)(2,1)}, u32[]{:S(2)}, u32[]{:S(2)}) collective-permute-start(bf16[4,512,512]{2,1,0:T(8,128)(2,1)S(1)} %pad_maximum_fusion.near.refs_0_.refs_3_.refs_6_), channel_id=1, source_target_pairs={{0,1},{1,0},{2,3},{3,2},{4,5},{5,4},{6,7},{7,6},{8,9},{9,8},{10,11... | collective-permute-start | bytes 6291464 | tf_op jit(solution)/shard_map/ppermute | solution.py:29
  107.5 3.8 %collective-permute-start.13 = (f32[1664]{0:T(1024)S(1)}, f32[1664]{0:T(1024)S(1)}, u32[]{:S(2)}, u32[]{:S(2)}) collective-permute-start(f32[1664]{0:T(1024)S(1)} %pad_maximum_fusion.9), channel_id=1, source_target_pairs={{0,16},{1,17},{2,18},{3,19},{4,20},{5,21},{6,22},{7,23},{8,24},{9,... | collective-permute-start | bytes 19976 | tf_op jit(solution)/shard_map/ppermute | solution.py:29
  114.8 9.0 %shard_map.167.refs_8_ = f32[512,640]{1,0:T(8,128)} custom-call(s32[8]{0:T(128)} %stack.163.place, bf16[4,512,512]{2,1,0:T(8,128)(2,1)} %copy-done.9, bf16[4,512,512]{2,1,0:T(8,128)(2,1)} %collective-permute-done.14.refs_1_.refs_4_.refs_7_, f32[4,2,1,512]{3,2,1,0:T(1,128)} %dynamic-slice_bitcast_fusion.refs_2_.refs_5_.refs_8_, ...), custom_call_target="tpu_custom_call" | custom-call | flops 1048576 | bytes 4096 | tf_op jit(solution)/shard_map/pallas_call | solution.py:228
  124.8 5.4 %shard_map.168 = f32[512,640]{1,0:T(8,128)} custom-call(s32[4]{0:T(128)} %pad_add_fusion.2.place, bf16[4,512,512]{2,1,0:T(8,128)(2,1)} %copy-done.9, bf16[4,512,512]{2,1,0:T(8,128)(2,1)} %collective-permute-done.14.refs_1_.refs_4_.refs_7_, f32[4,2,1,512]{3,2,1,0:T(1,128)} %dynamic-slice_bitcast_fusion.refs_2_.refs_5_.refs_8_, ...), custom_call_target="tpu_custom_call" | custom-call | flops 1048576 | bytes 4096 | tf_op jit(solution)/shard_map/pallas_call | solution.py:228
  130.3 9.3 %all-to-all-start.1 = ((f32[32,16,640]{2,1,0:T(8,128)}), f32[32,16,640]{2,1,0:T(8,128)S(1)}, u32[]{:S(2)}, u32[]{:S(2)}) async-start(f32[32,16,640]{2,1,0:T(8,128)} %bitcast.69), calls=%async_computation.1 | async-start | bytes 2621440 | tf_op jit(solution)/shard_map/all_to_all | solution.py:502
  146.2 13.4 %all-to-all-done.1 = f32[32,16,640]{2,1,0:T(8,128)S(1)} async-done(((f32[32,16,640]{2,1,0:T(8,128)}), f32[32,16,640]{2,1,0:T(8,128)S(1)}, u32[]{:S(2)}, u32[]{:S(2)}) %all-to-all-start.1) | async-done | bytes 1310752 | tf_op jit(solution)/shard_map/all_to_all | solution.py:502
  162.5 12.2 %shard_map.169 = bf16[8,16,1024]{2,1,0:T(8,128)(2,1)} custom-call(s32[2]{0:T(128)} %pad_add_fusion.1.place, s32[4]{0:T(128)} %lengths.1, bf16[16,16,640]{2,1,0:T(8,128)(2,1)} %reduce_sum.9.every, bf16[4,8,1024,128]{3,2,1,0:T(8,128)(2,1)} %keys.1, bf16[4,8,1024,128]{3,2,1,0:T(8,128)(2,1)} %values.1), custom_call_target="tpu_custom_call" | custom-call | flops 1048576 | bytes 4096 | tf_op jit(solution)/shard_map/pallas_call | solution.py:315
  174.7 3.5 %collective-permute-done.20.refs_4_ = bf16[512,512]{1,0:T(8,128)(2,1)S(1)} collective-permute-done((bf16[512,512]{1,0:T(8,128)(2,1)S(1)}, bf16[512,512]{1,0:T(8,128)(2,1)S(1)}, u32[]{:S(2)}, u32[]{:S(2)}) %collective-permute-start.20) | collective-permute-done | bytes 524320 | tf_op jit(solution)/shard_map/ppermute | solution.py:29
  196.8 3.3 %collective-permute-start.26 = (bf16[4,2,16,1024]{3,2,1,0:T(8,128)(2,1)S(1)}, bf16[4,2,16,1024]{3,2,1,0:T(8,128)(2,1)S(1)}, u32[]{:S(2)}, u32[]{:S(2)}) collective-permute-start(bf16[4,2,16,1024]{3,2,1,0:T(8,128)(2,1)S(1)} %get-tuple-element.97), channel_id=1, source_target_pairs={{0,8},{1,9},{2,10},{3,11},{4,12},{5,13},{6,14},{7,15},{8,0},{9,1},... | collective-permute-start | bytes 786440 | tf_op jit(solution)/shard_map/ppermute | solution.py:29
  201.7 3.5 %collective-permute-done.31 = bf16[4,2,16,1024]{3,2,1,0:T(8,128)(2,1)S(1)} collective-permute-done((bf16[4,2,16,1024]{3,2,1,0:T(8,128)(2,1)S(1)}, bf16[4,2,16,1024]{3,2,1,0:T(8,128)(2,1)S(1)}, u32[]{:S(2)}, u32[]{:S(2)}) %collective-permute-start.31) | collective-permute-done | bytes 262176 | tf_op jit(solution)/shard_map/ppermute | solution.py:29
  205.3 4.0 %collective-permute-start.35 = (bf16[4,4,2,16,1024]{4,3,2,1,0:T(8,128)(2,1)S(1)}, bf16[4,4,2,16,1024]{4,3,2,1,0:T(8,128)(2,1)S(1)}, u32[]{:S(2)}, u32[]{:S(2)}) collective-permute-start(bf16[4,4,2,16,1024]{4,3,2,1,0:T(8,128)(2,1)S(1)} %pad_maximum_fusion.2.near_b), channel_id=1, source_target_pairs={{0,1},{1,0},{2,3},{3,2},{4,5},{5,4},{6,7},{7,6},{8,9},{9,8},{10,11... | collective-permute-start | bytes 3145736 | tf_op jit(solution)/shard_map/ppermute | solution.py:29
  209.5 3.9 %collective-permute-start.34 = (bf16[4,4,2,16,1024]{4,3,2,1,0:T(8,128)(2,1)S(1)}, bf16[4,4,2,16,1024]{4,3,2,1,0:T(8,128)(2,1)S(1)}, u32[]{:S(2)}, u32[]{:S(2)}) collective-permute-start(bf16[4,4,2,16,1024]{4,3,2,1,0:T(8,128)(2,1)S(1)} %pad_maximum_fusion.1.near_a), channel_id=1, source_target_pairs={{0,1},{1,0},{2,3},{3,2},{4,5},{5,4},{6,7},{7,6},{8,9},{9,8},{10,11... | collective-permute-start | bytes 3145736 | tf_op jit(solution)/shard_map/ppermute | solution.py:29
  215.7 2.9 %shard_map.170 = (f32[16,16,512]{2,1,0:T(8,128)S(1)}, bf16[16,16,512]{2,1,0:T(8,128)(2,1)S(1)}) custom-call(s32[3]{0:T(128)S(1)} %pad_add_fusion.place, bf16[4,4,2,16,1024]{4,3,2,1,0:T(8,128)(2,1)S(1)} %pad_maximum_fusion.1.near_a, bf16[4,4,2,16,1024]{4,3,2,1,0:T(8,128)(2,1)S(1)} %pad_maximum_fusion.2.near_b, ...), custom_call_target="tpu_custom_call" | custom-call | flops 2147483648 | bytes 8388608 | tf_op jit(solution)/shard_map/pallas_call | solution.py:369
  218.7 7.5 %collective-permute-done.36 = bf16[16,16,512]{2,1,0:T(8,128)(2,1)S(1)} collective-permute-done((bf16[16,16,512]{2,1,0:T(8,128)(2,1)S(1)}, bf16[16,16,512]{2,1,0:T(8,128)(2,1)S(1)}, u32[]{:S(2)}, u32[]{:S(2)}) %collective-permute-start.36) | collective-permute-done | bytes 262176 | tf_op jit(solution)/shard_map/ppermute | solution.py:29
  (141 shorter events, 66.0 us)
Async XLA Ops:
  4.2 43.3 %all-to-all-start = ((bf16[16,10,64,128]{3,2,1,0:T(8,128)(2,1)}), bf16[16,10,64,128]{3,2,1,0:T(8,128)(2,1)S(1)}, u32[]{:S(2)}, u32[]{:S(2)}) async-start(bf16[16,10,64,128]{3,2,1,0:T(8,128)(2,1)} %shard_map.163), calls=%async_computation | async-start | bytes 5242880 | tf_op jit(solution)/shard_map/all_to_all | solution.py:427
  14.4 41.3 %collective-permute-start.1 = (bf16[256,512]{1,0:T(8,128)(2,1)}, bf16[256,512]{1,0:T(8,128)(2,1)}, u32[]{:S(2)}, u32[]{:S(2)}) collective-permute-start(bf16[256,512]{1,0:T(8,128)(2,1)} %reshape.40), channel_id=1, source_target_pairs={{0,2},{1,3},{2,18},{3,19},{4,6},{5,7},{6,22},{7,23},{8,10},{9,11},... | collective-permute-start | bytes 786440 | tf_op jit(solution)/shard_map/ppermute | solution.py:29
  17.3 38.4 %collective-permute-start = (bf16[256,512]{1,0:T(8,128)(2,1)}, bf16[256,512]{1,0:T(8,128)(2,1)}, u32[]{:S(2)}, u32[]{:S(2)}) collective-permute-start(bf16[256,512]{1,0:T(8,128)(2,1)} %reshape.40), channel_id=1, source_target_pairs={{0,0},{1,1},{2,16},{3,17},{4,4},{5,5},{6,20},{7,21},{8,8},{9,9},{1... | collective-permute-start | bytes 786440 | tf_op jit(solution)/shard_map/ppermute | solution.py:29
  58.7 12.1 %collective-permute-start.11 = (bf16[512,512]{1,0:T(8,128)(2,1)S(1)}, bf16[512,512]{1,0:T(8,128)(2,1)S(1)}, u32[]{:S(2)}, u32[]{:S(2)}) collective-permute-start(bf16[512,512]{1,0:T(8,128)(2,1)S(1)} %pad_maximum_fusion.3), channel_id=1, source_target_pairs={{0,4},{1,5},{2,6},{3,7},{4,8},{5,9},{6,10},{7,11},{8,12},{9,13},{1... | collective-permute-start | bytes 1572872 | tf_op jit(solution)/shard_map/ppermute | solution.py:29
  58.8 23.2 %collective-permute-start.10 = (bf16[512,512]{1,0:T(8,128)(2,1)S(1)}, bf16[512,512]{1,0:T(8,128)(2,1)S(1)}, u32[]{:S(2)}, u32[]{:S(2)}) collective-permute-start(bf16[512,512]{1,0:T(8,128)(2,1)S(1)} %pad_maximum_fusion.3), channel_id=1, source_target_pairs={{0,8},{1,9},{2,10},{3,11},{4,12},{5,13},{6,14},{7,15},{8,0},{9,1},... | collective-permute-start | bytes 1572872 | tf_op jit(solution)/shard_map/ppermute | solution.py:29
  61.3 34.8 %collective-permute-start.5 = (bf16[6,512,128]{2,1,0:T(8,128)(2,1)}, bf16[6,512,128]{2,1,0:T(8,128)(2,1)S(1)}, u32[]{:S(2)}, u32[]{:S(2)}) collective-permute-start(bf16[6,512,128]{2,1,0:T(8,128)(2,1)} %copy-done.4), channel_id=1, source_target_pairs={{0,96},{1,97},{2,98},{3,99},{4,100},{5,101},{6,102},{7,103},{8,104... | collective-permute-start | bytes 2359304 | tf_op jit(solution)/shard_map/ppermute | solution.py:29
  61.7 34.4 %collective-permute-start.7 = (bf16[6,512,128]{2,1,0:T(8,128)(2,1)}, bf16[6,512,128]{2,1,0:T(8,128)(2,1)}, u32[]{:S(2)}, u32[]{:S(2)}) collective-permute-start(bf16[6,512,128]{2,1,0:T(8,128)(2,1)} %copy-done.4), channel_id=1, source_target_pairs={{0,32},{1,33},{2,34},{3,35},{4,36},{5,37},{6,38},{7,39},{8,40},{9,... | collective-permute-start | bytes 2359304 | tf_op jit(solution)/shard_map/ppermute | solution.py:29
  62.8 21.8 %collective-permute-start.9 = (bf16[512,512]{1,0:T(8,128)(2,1)S(1)}, bf16[512,512]{1,0:T(8,128)(2,1)S(1)}, u32[]{:S(2)}, u32[]{:S(2)}) collective-permute-start(bf16[512,512]{1,0:T(8,128)(2,1)S(1)} %pad_maximum_fusion.3), channel_id=1, source_target_pairs={{0,12},{1,13},{2,14},{3,15},{4,0},{5,1},{6,2},{7,3},{8,4},{9,5},{1... | collective-permute-start | bytes 1572872 | tf_op jit(solution)/shard_map/ppermute | solution.py:29
  70.8 20.7 %collective-permute-start.6 = (bf16[5,512,128]{2,1,0:T(8,128)(2,1)}, bf16[5,512,128]{2,1,0:T(8,128)(2,1)S(1)}, u32[]{:S(2)}, u32[]{:S(2)}) collective-permute-start(bf16[5,512,128]{2,1,0:T(8,128)(2,1)} %copy-done.5), channel_id=1, source_target_pairs={{0,96},{1,97},{2,98},{3,99},{4,100},{5,101},{6,102},{7,103},{8,104... | collective-permute-start | bytes 1966088 | tf_op jit(solution)/shard_map/ppermute | solution.py:29
  82.0 14.1 %collective-permute-start.8 = (bf16[5,512,128]{2,1,0:T(8,128)(2,1)}, bf16[5,512,128]{2,1,0:T(8,128)(2,1)S(1)}, u32[]{:S(2)}, u32[]{:S(2)}) collective-permute-start(bf16[5,512,128]{2,1,0:T(8,128)(2,1)} %copy-done.5), channel_id=1, source_target_pairs={{0,32},{1,33},{2,34},{3,35},{4,36},{5,37},{6,38},{7,39},{8,40},{9,... | collective-permute-start | bytes 1966088 | tf_op jit(solution)/shard_map/ppermute | solution.py:29
  97.0 17.8 %collective-permute-start.14 = (bf16[4,512,512]{2,1,0:T(8,128)(2,1)S(1)}, bf16[4,512,512]{2,1,0:T(8,128)(2,1)}, u32[]{:S(2)}, u32[]{:S(2)}) collective-permute-start(bf16[4,512,512]{2,1,0:T(8,128)(2,1)S(1)} %pad_maximum_fusion.near.refs_0_.refs_3_.refs_6_), channel_id=1, source_target_pairs={{0,1},{1,0},{2,3},{3,2},{4,5},{5,4},{6,7},{7,6},{8,9},{9,8},{10,11... | collective-permute-start | bytes 6291464 | tf_op jit(solution)/shard_map/ppermute | solution.py:29
  106.0 18.9 %collective-permute-start.15 = (bf16[6,512,128]{2,1,0:T(8,128)(2,1)S(1)}, bf16[6,512,128]{2,1,0:T(8,128)(2,1)}, u32[]{:S(2)}, u32[]{:S(2)}) collective-permute-start(bf16[6,512,128]{2,1,0:T(8,128)(2,1)S(1)} %collective-permute-done.5.refs_14_), channel_id=1, source_target_pairs={{0,96},{1,97},{2,98},{3,99},{4,100},{5,101},{6,102},{7,103},{8,104... | collective-permute-start | bytes 2359304 | tf_op jit(solution)/shard_map/ppermute | solution.py:29
  106.1 17.6 %collective-permute-start.16 = (bf16[5,512,128]{2,1,0:T(8,128)(2,1)}, bf16[5,512,128]{2,1,0:T(8,128)(2,1)}, u32[]{:S(2)}, u32[]{:S(2)}) collective-permute-start(bf16[5,512,128]{2,1,0:T(8,128)(2,1)} %copy-done.12), channel_id=1, source_target_pairs={{0,32},{1,33},{2,34},{3,35},{4,36},{5,37},{6,38},{7,39},{8,40},{9,... | collective-permute-start | bytes 1966088 | tf_op jit(solution)/shard_map/ppermute | solution.py:29
  130.3 29.3 %all-to-all-start.1 = ((f32[32,16,640]{2,1,0:T(8,128)}), f32[32,16,640]{2,1,0:T(8,128)S(1)}, u32[]{:S(2)}, u32[]{:S(2)}) async-start(f32[32,16,640]{2,1,0:T(8,128)} %bitcast.69), calls=%async_computation.1 | async-start | bytes 2621440 | tf_op jit(solution)/shard_map/all_to_all | solution.py:502
  142.3 18.2 %collective-permute-start.17 = (bf16[512,512]{1,0:T(8,128)(2,1)}, bf16[512,512]{1,0:T(8,128)(2,1)S(1)}, u32[]{:S(2)}, u32[]{:S(2)}) collective-permute-start(bf16[512,512]{1,0:T(8,128)(2,1)} %get-tuple-element.81.refs_0_), channel_id=1, source_target_pairs={{0,96},{1,97},{2,98},{3,99},{4,100},{5,101},{6,102},{7,103},{8,104... | collective-permute-start | bytes 1572872 | tf_op jit(solution)/shard_map/ppermute | solution.py:29
  143.5 16.9 %collective-permute-start.18 = (bf16[512,512]{1,0:T(8,128)(2,1)}, bf16[512,512]{1,0:T(8,128)(2,1)S(1)}, u32[]{:S(2)}, u32[]{:S(2)}) collective-permute-start(bf16[512,512]{1,0:T(8,128)(2,1)} %get-tuple-element.82.refs_1_), channel_id=1, source_target_pairs={{0,32},{1,33},{2,34},{3,35},{4,36},{5,37},{6,38},{7,39},{8,40},{9,... | collective-permute-start | bytes 1572872 | tf_op jit(solution)/shard_map/ppermute | solution.py:29
  143.7 31.0 %collective-permute-start.19 = (bf16[512,512]{1,0:T(8,128)(2,1)}, bf16[512,512]{1,0:T(8,128)(2,1)S(1)}, u32[]{:S(2)}, u32[]{:S(2)}) collective-permute-start(bf16[512,512]{1,0:T(8,128)(2,1)} %get-tuple-element.82.refs_1_), channel_id=1, source_target_pairs={{0,96},{1,97},{2,98},{3,99},{4,100},{5,101},{6,102},{7,103},{8,104... | collective-permute-start | bytes 1572872 | tf_op jit(solution)/shard_map/ppermute | solution.py:29
  146.2 28.6 %collective-permute-start.22 = (bf16[512,512]{1,0:T(8,128)(2,1)}, bf16[512,512]{1,0:T(8,128)(2,1)S(1)}, u32[]{:S(2)}, u32[]{:S(2)}) collective-permute-start(bf16[512,512]{1,0:T(8,128)(2,1)} %get-tuple-element.81.refs_0_), channel_id=1, source_target_pairs={{0,32},{1,33},{2,34},{3,35},{4,36},{5,37},{6,38},{7,39},{8,40},{9,... | collective-permute-start | bytes 1572872 | tf_op jit(solution)/shard_map/ppermute | solution.py:29
  160.5 17.8 %collective-permute-start.20 = (bf16[512,512]{1,0:T(8,128)(2,1)S(1)}, bf16[512,512]{1,0:T(8,128)(2,1)S(1)}, u32[]{:S(2)}, u32[]{:S(2)}) collective-permute-start(bf16[512,512]{1,0:T(8,128)(2,1)S(1)} %collective-permute-done.17.refs_2_), channel_id=1, source_target_pairs={{0,96},{1,97},{2,98},{3,99},{4,100},{5,101},{6,102},{7,103},{8,104... | collective-permute-start | bytes 1572872 | tf_op jit(solution)/shard_map/ppermute | solution.py:29
  161.7 18.7 %collective-permute-start.21 = (bf16[512,512]{1,0:T(8,128)(2,1)S(1)}, bf16[512,512]{1,0:T(8,128)(2,1)S(1)}, u32[]{:S(2)}, u32[]{:S(2)}) collective-permute-start(bf16[512,512]{1,0:T(8,128)(2,1)S(1)} %collective-permute-done.18.refs_7_), channel_id=1, source_target_pairs={{0,32},{1,33},{2,34},{3,35},{4,36},{5,37},{6,38},{7,39},{8,40},{9,... | collective-permute-start | bytes 1572872 | tf_op jit(solution)/shard_map/ppermute | solution.py:29
  192.3 9.4 %collective-permute-start.33 = (bf16[4,2,16,1024]{3,2,1,0:T(8,128)(2,1)S(1)}, bf16[4,2,16,1024]{3,2,1,0:T(8,128)(2,1)S(1)}, u32[]{:S(2)}, u32[]{:S(2)}) collective-permute-start(bf16[4,2,16,1024]{3,2,1,0:T(8,128)(2,1)S(1)} %get-tuple-element.93), channel_id=1, source_target_pairs={{0,18},{1,19},{2,16},{3,17},{4,22},{5,23},{6,20},{7,21},{8,26},{9,... | collective-permute-start | bytes 786440 | tf_op jit(solution)/shard_map/ppermute | solution.py:29
  194.5 10.7 %collective-permute-start.31 = (bf16[4,2,16,1024]{3,2,1,0:T(8,128)(2,1)S(1)}, bf16[4,2,16,1024]{3,2,1,0:T(8,128)(2,1)S(1)}, u32[]{:S(2)}, u32[]{:S(2)}) collective-permute-start(bf16[4,2,16,1024]{3,2,1,0:T(8,128)(2,1)S(1)} %get-tuple-element.92), channel_id=1, source_target_pairs={{0,2},{1,3},{2,0},{3,1},{4,6},{5,7},{6,4},{7,5},{8,10},{9,11},{10,... | collective-permute-start | bytes 786440 | tf_op jit(solution)/shard_map/ppermute | solution.py:29
  196.3 13.0 %collective-permute-start.27 = (bf16[4,2,16,1024]{3,2,1,0:T(8,128)(2,1)S(1)}, bf16[4,2,16,1024]{3,2,1,0:T(8,128)(2,1)S(1)}, u32[]{:S(2)}, u32[]{:S(2)}) collective-permute-start(bf16[4,2,16,1024]{3,2,1,0:T(8,128)(2,1)S(1)} %get-tuple-element.97), channel_id=1, source_target_pairs={{0,4},{1,5},{2,6},{3,7},{4,8},{5,9},{6,10},{7,11},{8,12},{9,13},{1... | collective-permute-start | bytes 786440 | tf_op jit(solution)/shard_map/ppermute | solution.py:29
  196.8 12.5 %collective-permute-start.26 = (bf16[4,2,16,1024]{3,2,1,0:T(8,128)(2,1)S(1)}, bf16[4,2,16,1024]{3,2,1,0:T(8,128)(2,1)S(1)}, u32[]{:S(2)}, u32[]{:S(2)}) collective-permute-start(bf16[4,2,16,1024]{3,2,1,0:T(8,128)(2,1)S(1)} %get-tuple-element.97), channel_id=1, source_target_pairs={{0,8},{1,9},{2,10},{3,11},{4,12},{5,13},{6,14},{7,15},{8,0},{9,1},... | collective-permute-start | bytes 786440 | tf_op jit(solution)/shard_map/ppermute | solution.py:29
  (30 other events, 268.6 us)

commit v5 on v4

--- a/solution.py
+++ b/solution.py
@@ -468,18 +468,22 @@
     next_b, last_a = from_y(own_b, 1), from_y(own_a, 3)
     tokens = [pair] + [from_x(pair, step) for step in (1, 2, 3)]
     near = jnp.stack(tokens)
-    next_a, next_b, last_a, last_b, near = lax.optimization_barrier(
-        (next_a, next_b, last_a, last_b, near)
+    sums = sum(sums)
+    sums = sums + swap_low(sums)
+    factor_qkv = (scale_qkv / jnp.sqrt(sums[:640])).reshape(1, 640)
+    factor_out = (scale_out / jnp.sqrt(sums[640:])).reshape(1, 512)
+    weight_a, weight_b = scale_rows(own_o, down_own, ups_out, factor_out)
+    next_a, next_b, last_a, last_b, near, factor_qkv, weight_a, weight_b = (
+        lax.optimization_barrier(
+            (next_a, next_b, last_a, last_b, near, factor_qkv, weight_a, weight_b)
+        )
     )
     far_a, far_b = from_y(next_a, 1), from_y(last_b, 3)
     far = swap_core(near)
     squares = token_sums(near).reshape(512)
-    both = jnp.concatenate([sum(sums), squares + swap_core(squares)])
-    both = both + swap_low(both)
-    factor_qkv = (scale_qkv / jnp.sqrt(both[:640])).reshape(1, 640)
-    factor_out = (scale_out / jnp.sqrt(both[640:1152])).reshape(1, 512)
-    inverse = lax.rsqrt(both[1152:] / 8192.0 + EPSILON).reshape(512, 1)
-    weight_a, weight_b = scale_rows(own_o, down_own, ups_out, factor_out)
+    squares = squares + swap_core(squares)
+    squares = squares + swap_low(squares)
+    inverse = lax.rsqrt(squares / 8192.0 + EPSILON).reshape(512, 1)
 
     gains = pick(input_norm_gain.reshape(4, 2, 2, 1, 512), zl, 1)
 
@@ -492,19 +496,18 @@
 
     total = project((0, 1, 3), (own_a, own_b, next_a, next_b, last_a, last_b), None)
     total, far_a, far_b = lax.optimization_barrier((total, far_a, far_b))
-    weight_a, weight_b = lax.optimization_barrier((weight_a, weight_b, far_a))[:2]
     total = project((2,), (far_a, far_b), total)
 
-    rows_o = [weight_a, weight_b, from_y(weight_a, 1), from_y(weight_b, 1)]
-    rows_last = [from_y(weight_a, 3), from_y(weight_b, 3)]
+    first_rows, last_rows = from_y(weight_a, 1), from_y(weight_b, 3)
+    total, first_rows, last_rows = lax.optimization_barrier((total, first_rows, last_rows))
+    rows_o = [weight_a, weight_b, first_rows, from_y(weight_b, 1)]
+    rows_o += [from_y(first_rows, 1), from_y(last_rows, 3), from_y(weight_a, 3), last_rows]
 
     groups = [[32 * k + i for i in range(32)] for k in range(4)]
     halves = lax.all_to_all(
         total.reshape(32, 16, 640), AXES, 0, 0, axis_index_groups=groups, tiled=True
     )
     every = jnp.sum(halves.reshape(2, 16, 16, 640), axis=0).astype(bf16)
-    rows_next, rows_before, every = lax.optimization_barrier((rows_o[2], rows_last[1], every))
-    rows_o += [from_y(rows_next, 1), from_y(rows_before, 3)] + rows_last
 
     place = jnp.stack([y, zl]).astype(jnp.int32)
     attended = attend(place, lengths, every, cached_key_rows, cached_value_rows)

time: 228 us -> 223 us (0.978)
  waiting for transfers between devices: 92.8 us -> 80.9 us
  starting transfers between devices: 74.3 us -> 77.7 us
  other arithmetic: 5.86 us -> 8.71 us
    ppermute x37 -> x38, waiting for transfers between devices: 56.3 us -> 42.4 us  [permute(): return lax.ppermute(value, AXES, pairs)]
    ppermute x37 -> x38, starting transfers between devices: 55.7 us -> 59.7 us  [permute(): return lax.ppermute(value, AXES, pairs)]
  transfers between devices with their start and end apart: 39 -> 40, of which waited for: 19 -> 15; matrix products, arithmetic and copies ran while one was open for 6% -> 7% of each run, Pallas kernels for 12% -> 15%
where the time goes in v5:
time: 223 us; the launch traced here: 222 us
  waiting for transfers between devices  80.9 us (36%)
  starting transfers between devices  77.7 us (35%)
  Pallas kernels  41 us (18%)
  local copies, waits for them, and re-layouts  13 us (6%)
  other arithmetic  8.71 us (4%)
    ppermute x38, starting transfers between devices, permute(): return lax.ppermute(value, AXES, pairs)  59.7 us
    ppermute x38, waiting for transfers between devices, permute(): return lax.ppermute(value, AXES, pairs)  42.4 us
    all_to_all x1, waiting for transfers between devices, per_device(): received = lax.all_to_all(frozen, 'tp', 0, 0, tiled=True)  23.1 us
    all_to_all x1, waiting for transfers between devices, per_device(): lax.all_to_all(total.reshape(32, 16, 640), AXES, 0, 0, axis_index_groups=...  15.4 us
    pallas_call x2, Pallas kernels, multiply_slabs(): pl.pallas_call(multiply_slabs_kernel, grid_spec=pltpu.PrefetchScalarGridS...  14.4 us
    pallas_call x1, Pallas kernels, attend(): pl.pallas_call(attend_kernel, grid_spec=pltpu.PrefetchScalarGridSpec(num_...  12.2 us
    all_to_all x1, starting transfers between devices, per_device(): received = lax.all_to_all(frozen, 'tp', 0, 0, tiled=True)  9.26 us
    all_to_all x1, starting transfers between devices, per_device(): lax.all_to_all(total.reshape(32, 16, 640), AXES, 0, 0, axis_index_groups=...  8.71 us
  transfers between devices with their start and end apart: 40, of which 15 were waited for; matrix products, arithmetic and copies ran while one was open for 7% of the time, Pallas kernels for 15%

profile of v5, /device:TPU:1, one launch (start us, length us, event | category | flops | bytes accessed | tf_op | source)
XLA Modules:
  0.0 221.8 jit_solution(10055013483527266442)
XLA Ops:
  0.0 4.1 %shard_map.163 = bf16[16,10,64,128]{3,2,1,0:T(8,128)(2,1)} custom-call(s32[1]{0:T(128)} %bitcast.7.place, bf16[64,8192]{1,0:T(8,128)(2,1)} %query.1, bf16[64,2048]{1,0:T(8,128)(2,1)} %key_value.1, bf16[64,8192]{1,0:T(8,128)(2,1)} %output.1, bf16[32,64]{1,0:T(8,128)(2,1)} %bitcast.89, bf16[32,64]{1,0:T(8,128)(2,1)} %bitcast.90, bf16[32,64]{1,0:T(8,128)(2,1)} %bitcast.91), custom_call_target="tpu_custom_call" | custom-call | bytes 4194304 | tf_op jit(solution)/shard_map/pallas_call | solution.py:82
  4.1 9.3 %all-to-all-start = ((bf16[16,10,64,128]{3,2,1,0:T(8,128)(2,1)}), bf16[16,10,64,128]{3,2,1,0:T(8,128)(2,1)S(1)}, u32[]{:S(2)}, u32[]{:S(2)}) async-start(bf16[16,10,64,128]{3,2,1,0:T(8,128)(2,1)} %shard_map.163), calls=%async_computation | async-start | bytes 5242880 | tf_op jit(solution)/shard_map/all_to_all | solution.py:427
  14.4 2.9 %collective-permute-start.1 = (bf16[256,512]{1,0:T(8,128)(2,1)}, bf16[256,512]{1,0:T(8,128)(2,1)}, u32[]{:S(2)}, u32[]{:S(2)}) collective-permute-start(bf16[256,512]{1,0:T(8,128)(2,1)} %reshape.40), channel_id=1, source_target_pairs={{0,2},{1,3},{2,18},{3,19},{4,6},{5,7},{6,22},{7,23},{8,10},{9,11},... | collective-permute-start | bytes 786440 | tf_op jit(solution)/shard_map/ppermute | solution.py:29
  17.3 3.6 %collective-permute-start = (bf16[256,512]{1,0:T(8,128)(2,1)}, bf16[256,512]{1,0:T(8,128)(2,1)}, u32[]{:S(2)}, u32[]{:S(2)}) collective-permute-start(bf16[256,512]{1,0:T(8,128)(2,1)} %reshape.40), channel_id=1, source_target_pairs={{0,0},{1,1},{2,16},{3,17},{4,4},{5,5},{6,20},{7,21},{8,8},{9,9},{1... | collective-permute-start | bytes 786440 | tf_op jit(solution)/shard_map/ppermute | solution.py:29
  24.3 23.1 %all-to-all-done.received = bf16[16,10,64,128]{3,2,1,0:T(8,128)(2,1)S(1)} async-done(((bf16[16,10,64,128]{3,2,1,0:T(8,128)(2,1)}), bf16[16,10,64,128]{3,2,1,0:T(8,128)(2,1)S(1)}, u32[]{:S(2)}, u32[]{:S(2)}) %all-to-all-start) | async-done | bytes 2621472 | tf_op jit(solution)/shard_map/all_to_all | solution.py:427
  51.7 2.8 %collective-permute-start.2 = (f32[1152]{0:T(1024)S(1)}, f32[1152]{0:T(1024)S(1)}, u32[]{:S(2)}, u32[]{:S(2)}) collective-permute-start(f32[1152]{0:T(1024)S(1)} %reduce), channel_id=1, source_target_pairs={{0,96},{1,97},{2,98},{3,99},{4,100},{5,101},{6,102},{7,103},{8,104... | collective-permute-start | bytes 13832 | tf_op jit(solution)/shard_map/ppermute | solution.py:29
  71.2 10.7 %collective-permute-done.10 = bf16[512,512]{1,0:T(8,128)(2,1)S(1)} collective-permute-done((bf16[512,512]{1,0:T(8,128)(2,1)S(1)}, bf16[512,512]{1,0:T(8,128)(2,1)S(1)}, u32[]{:S(2)}, u32[]{:S(2)}) %collective-permute-start.10) | collective-permute-done | bytes 524320 | tf_op jit(solution)/shard_map/ppermute | solution.py:29
  87.3 4.2 %collective-permute-done.6.refs_15_ = bf16[5,512,128]{2,1,0:T(8,128)(2,1)S(1)} collective-permute-done((bf16[5,512,128]{2,1,0:T(8,128)(2,1)}, bf16[5,512,128]{2,1,0:T(8,128)(2,1)S(1)}, u32[]{:S(2)}, u32[]{:S(2)}) %collective-permute-start.6) | collective-permute-done | bytes 655392 | tf_op jit(solution)/shard_map/ppermute | solution.py:29
  91.5 4.6 %collective-permute-done.8.refs_17_ = bf16[5,512,128]{2,1,0:T(8,128)(2,1)} collective-permute-done((bf16[5,512,128]{2,1,0:T(8,128)(2,1)}, bf16[5,512,128]{2,1,0:T(8,128)(2,1)}, u32[]{:S(2)}, u32[]{:S(2)}) %collective-permute-start.8) | collective-permute-done | bytes 655392 | tf_op jit(solution)/shard_map/ppermute | solution.py:29
  96.1 4.5 %collective-permute-start.13 = (bf16[4,512,512]{2,1,0:T(8,128)(2,1)}, bf16[4,512,512]{2,1,0:T(8,128)(2,1)}, u32[]{:S(2)}, u32[]{:S(2)}) collective-permute-start(bf16[4,512,512]{2,1,0:T(8,128)(2,1)} %pad_maximum_fusion.near.refs_0_.refs_3_.refs_6_), channel_id=1, source_target_pairs={{0,1},{1,0},{2,3},{3,2},{4,5},{5,4},{6,7},{7,6},{8,9},{9,8},{10,11... | collective-permute-start | bytes 6291464 | tf_op jit(solution)/shard_map/ppermute | solution.py:29
  102.1 2.8 %shard_map.166 = f32[512,1]{1,0:T(8,128)} custom-call(bf16[4,512,512]{2,1,0:T(8,128)(2,1)} %pad_maximum_fusion.near.refs_0_.refs_3_.refs_6_), custom_call_target="tpu_custom_call" | custom-call | flops 1048576 | bytes 4096 | tf_op jit(solution)/shard_map/pallas_call | solution.py:175
  107.5 3.5 %collective-permute-start.15 = (f32[512]{0:T(512)S(1)}, f32[512]{0:T(512)S(1)}, u32[]{:S(2)}, u32[]{:S(2)}) collective-permute-start(f32[512]{0:T(512)S(1)} %add.109), channel_id=1, source_target_pairs={{0,16},{1,17},{2,18},{3,19},{4,20},{5,21},{6,22},{7,23},{8,24},{9,... | collective-permute-start | bytes 6152 | tf_op jit(solution)/shard_map/ppermute | solution.py:29
  116.8 8.9 %shard_map.167.refs_8_ = f32[512,640]{1,0:T(8,128)} custom-call(s32[8]{0:T(128)} %stack.166.place, bf16[4,512,512]{2,1,0:T(8,128)(2,1)} %pad_maximum_fusion.near.refs_0_.refs_3_.refs_6_, bf16[4,512,512]{2,1,0:T(8,128)(2,1)} %collective-permute-done.13.refs_1_.refs_4_.refs_7_, f32[4,2,1,512]{3,2,1,0:T(1,128)} %dynamic-slice_bitcast_fusion.refs_2_.refs_5_.refs_8_, ...), custom_call_target="tpu_custom_call" | custom-call | flops 1048576 | bytes 4096 | tf_op jit(solution)/shard_map/pallas_call | solution.py:228
  125.8 5.4 %shard_map.168 = f32[512,640]{1,0:T(8,128)} custom-call(s32[4]{0:T(128)} %pad_add_fusion.2.place, bf16[4,512,512]{2,1,0:T(8,128)(2,1)} %pad_maximum_fusion.near.refs_0_.refs_3_.refs_6_, bf16[4,512,512]{2,1,0:T(8,128)(2,1)} %collective-permute-done.13.refs_1_.refs_4_.refs_7_, f32[4,2,1,512]{3,2,1,0:T(1,128)} %dynamic-slice_bitcast_fusion.refs_2_.refs_5_.refs_8_, ...), custom_call_target="tpu_custom_call" | custom-call | flops 1048576 | bytes 4096 | tf_op jit(solution)/shard_map/pallas_call | solution.py:228
  131.2 8.7 %all-to-all-start.1 = ((f32[32,16,640]{2,1,0:T(8,128)}), f32[32,16,640]{2,1,0:T(8,128)}, u32[]{:S(2)}, u32[]{:S(2)}) async-start(f32[32,16,640]{2,1,0:T(8,128)} %bitcast.69), calls=%async_computation.1 | async-start | bytes 2621440 | tf_op jit(solution)/shard_map/all_to_all | solution.py:507
  144.5 15.4 %all-to-all-done.1 = f32[32,16,640]{2,1,0:T(8,128)} async-done(((f32[32,16,640]{2,1,0:T(8,128)}), f32[32,16,640]{2,1,0:T(8,128)}, u32[]{:S(2)}, u32[]{:S(2)}) %all-to-all-start.1) | async-done | bytes 1310752 | tf_op jit(solution)/shard_map/all_to_all | solution.py:507
  162.2 12.2 %shard_map.169 = bf16[8,16,1024]{2,1,0:T(8,128)(2,1)} custom-call(s32[2]{0:T(128)} %pad_add_fusion.1.place, s32[4]{0:T(128)} %lengths.1, bf16[16,16,640]{2,1,0:T(8,128)(2,1)} %reduce_sum.9.every, bf16[4,8,1024,128]{3,2,1,0:T(8,128)(2,1)} %keys.1, bf16[4,8,1024,128]{3,2,1,0:T(8,128)(2,1)} %values.1), custom_call_target="tpu_custom_call" | custom-call | flops 1048576 | bytes 4096 | tf_op jit(solution)/shard_map/pallas_call | solution.py:315
  181.6 3.4 %collective-permute-done.30 = bf16[2,2,16,1024]{3,2,1,0:T(8,128)(2,1)S(1)} collective-permute-done((bf16[2,2,16,1024]{3,2,1,0:T(8,128)(2,1)S(1)}, bf16[2,2,16,1024]{3,2,1,0:T(8,128)(2,1)S(1)}, u32[]{:S(2)}, u32[]{:S(2)}) %collective-permute-start.30) | collective-permute-done | bytes 131104 | tf_op jit(solution)/shard_map/ppermute | solution.py:29
  190.5 3.4 %collective-permute-start.27 = (bf16[4,2,16,1024]{3,2,1,0:T(8,128)(2,1)S(1)}, bf16[4,2,16,1024]{3,2,1,0:T(8,128)(2,1)S(1)}, u32[]{:S(2)}, u32[]{:S(2)}) collective-permute-start(bf16[4,2,16,1024]{3,2,1,0:T(8,128)(2,1)S(1)} %get-tuple-element.99), channel_id=1, source_target_pairs={{0,8},{1,9},{2,10},{3,11},{4,12},{5,13},{6,14},{7,15},{8,0},{9,1},... | collective-permute-start | bytes 786440 | tf_op jit(solution)/shard_map/ppermute | solution.py:29
  193.8 2.8 %collective-permute-start.26 = (bf16[4,2,16,1024]{3,2,1,0:T(8,128)(2,1)S(1)}, bf16[4,2,16,1024]{3,2,1,0:T(8,128)(2,1)S(1)}, u32[]{:S(2)}, u32[]{:S(2)}) collective-permute-start(bf16[4,2,16,1024]{3,2,1,0:T(8,128)(2,1)S(1)} %get-tuple-element.99), channel_id=1, source_target_pairs={{0,12},{1,13},{2,14},{3,15},{4,0},{5,1},{6,2},{7,3},{8,4},{9,5},{1... | collective-permute-start | bytes 786440 | tf_op jit(solution)/shard_map/ppermute | solution.py:29
  198.5 3.9 %collective-permute-start.36 = (bf16[4,4,2,16,1024]{4,3,2,1,0:T(8,128)(2,1)S(1)}, bf16[4,4,2,16,1024]{4,3,2,1,0:T(8,128)(2,1)S(1)}, u32[]{:S(2)}, u32[]{:S(2)}) collective-permute-start(bf16[4,4,2,16,1024]{4,3,2,1,0:T(8,128)(2,1)S(1)} %pad_maximum_fusion.2.near_b), channel_id=1, source_target_pairs={{0,1},{1,0},{2,3},{3,2},{4,5},{5,4},{6,7},{7,6},{8,9},{9,8},{10,11... | collective-permute-start | bytes 3145736 | tf_op jit(solution)/shard_map/ppermute | solution.py:29
  204.1 2.9 %collective-permute-start.35 = (bf16[4,4,2,16,1024]{4,3,2,1,0:T(8,128)(2,1)S(1)}, bf16[4,4,2,16,1024]{4,3,2,1,0:T(8,128)(2,1)S(1)}, u32[]{:S(2)}, u32[]{:S(2)}) collective-permute-start(bf16[4,4,2,16,1024]{4,3,2,1,0:T(8,128)(2,1)S(1)} %pad_maximum_fusion.1.near_a), channel_id=1, source_target_pairs={{0,1},{1,0},{2,3},{3,2},{4,5},{5,4},{6,7},{7,6},{8,9},{9,8},{10,11... | collective-permute-start | bytes 3145736 | tf_op jit(solution)/shard_map/ppermute | solution.py:29
  209.2 4.1 %shard_map.170 = (f32[16,16,512]{2,1,0:T(8,128)S(1)}, bf16[16,16,512]{2,1,0:T(8,128)(2,1)S(1)}) custom-call(s32[3]{0:T(128)S(1)} %pad_add_fusion.place, bf16[4,4,2,16,1024]{4,3,2,1,0:T(8,128)(2,1)S(1)} %pad_maximum_fusion.1.near_a, bf16[4,4,2,16,1024]{4,3,2,1,0:T(8,128)(2,1)S(1)} %pad_maximum_fusion.2.near_b, ...), custom_call_target="tpu_custom_call" | custom-call | flops 2147483648 | bytes 8388608 | tf_op jit(solution)/shard_map/pallas_call | solution.py:369
  213.7 7.2 %collective-permute-done.37 = bf16[16,16,512]{2,1,0:T(8,128)(2,1)S(1)} collective-permute-done((bf16[16,16,512]{2,1,0:T(8,128)(2,1)S(1)}, bf16[16,16,512]{2,1,0:T(8,128)(2,1)S(1)}, u32[]{:S(2)}, u32[]{:S(2)}) %collective-permute-start.37) | collective-permute-done | bytes 262176 | tf_op jit(solution)/shard_map/ppermute | solution.py:29
  (141 shorter events, 66.9 us)
Async XLA Ops:
  4.1 43.3 %all-to-all-start = ((bf16[16,10,64,128]{3,2,1,0:T(8,128)(2,1)}), bf16[16,10,64,128]{3,2,1,0:T(8,128)(2,1)S(1)}, u32[]{:S(2)}, u32[]{:S(2)}) async-start(bf16[16,10,64,128]{3,2,1,0:T(8,128)(2,1)} %shard_map.163), calls=%async_computation | async-start | bytes 5242880 | tf_op jit(solution)/shard_map/all_to_all | solution.py:427
  14.4 41.2 %collective-permute-start.1 = (bf16[256,512]{1,0:T(8,128)(2,1)}, bf16[256,512]{1,0:T(8,128)(2,1)}, u32[]{:S(2)}, u32[]{:S(2)}) collective-permute-start(bf16[256,512]{1,0:T(8,128)(2,1)} %reshape.40), channel_id=1, source_target_pairs={{0,2},{1,3},{2,18},{3,19},{4,6},{5,7},{6,22},{7,23},{8,10},{9,11},... | collective-permute-start | bytes 786440 | tf_op jit(solution)/shard_map/ppermute | solution.py:29
  17.3 38.3 %collective-permute-start = (bf16[256,512]{1,0:T(8,128)(2,1)}, bf16[256,512]{1,0:T(8,128)(2,1)}, u32[]{:S(2)}, u32[]{:S(2)}) collective-permute-start(bf16[256,512]{1,0:T(8,128)(2,1)} %reshape.40), channel_id=1, source_target_pairs={{0,0},{1,1},{2,16},{3,17},{4,4},{5,5},{6,20},{7,21},{8,8},{9,9},{1... | collective-permute-start | bytes 786440 | tf_op jit(solution)/shard_map/ppermute | solution.py:29
  58.6 12.0 %collective-permute-start.11 = (bf16[512,512]{1,0:T(8,128)(2,1)S(1)}, bf16[512,512]{1,0:T(8,128)(2,1)S(1)}, u32[]{:S(2)}, u32[]{:S(2)}) collective-permute-start(bf16[512,512]{1,0:T(8,128)(2,1)S(1)} %pad_maximum_fusion.3), channel_id=1, source_target_pairs={{0,4},{1,5},{2,6},{3,7},{4,8},{5,9},{6,10},{7,11},{8,12},{9,13},{1... | collective-permute-start | bytes 1572872 | tf_op jit(solution)/shard_map/ppermute | solution.py:29
  58.7 23.2 %collective-permute-start.10 = (bf16[512,512]{1,0:T(8,128)(2,1)S(1)}, bf16[512,512]{1,0:T(8,128)(2,1)S(1)}, u32[]{:S(2)}, u32[]{:S(2)}) collective-permute-start(bf16[512,512]{1,0:T(8,128)(2,1)S(1)} %pad_maximum_fusion.3), channel_id=1, source_target_pairs={{0,8},{1,9},{2,10},{3,11},{4,12},{5,13},{6,14},{7,15},{8,0},{9,1},... | collective-permute-start | bytes 1572872 | tf_op jit(solution)/shard_map/ppermute | solution.py:29
  61.2 34.9 %collective-permute-start.5 = (bf16[6,512,128]{2,1,0:T(8,128)(2,1)}, bf16[6,512,128]{2,1,0:T(8,128)(2,1)S(1)}, u32[]{:S(2)}, u32[]{:S(2)}) collective-permute-start(bf16[6,512,128]{2,1,0:T(8,128)(2,1)} %copy-done.4), channel_id=1, source_target_pairs={{0,96},{1,97},{2,98},{3,99},{4,100},{5,101},{6,102},{7,103},{8,104... | collective-permute-start | bytes 2359304 | tf_op jit(solution)/shard_map/ppermute | solution.py:29
  61.6 34.5 %collective-permute-start.7 = (bf16[6,512,128]{2,1,0:T(8,128)(2,1)}, bf16[6,512,128]{2,1,0:T(8,128)(2,1)S(1)}, u32[]{:S(2)}, u32[]{:S(2)}) collective-permute-start(bf16[6,512,128]{2,1,0:T(8,128)(2,1)} %copy-done.4), channel_id=1, source_target_pairs={{0,32},{1,33},{2,34},{3,35},{4,36},{5,37},{6,38},{7,39},{8,40},{9,... | collective-permute-start | bytes 2359304 | tf_op jit(solution)/shard_map/ppermute | solution.py:29
  66.7 19.0 %collective-permute-start.9 = (bf16[512,512]{1,0:T(8,128)(2,1)S(1)}, bf16[512,512]{1,0:T(8,128)(2,1)S(1)}, u32[]{:S(2)}, u32[]{:S(2)}) collective-permute-start(bf16[512,512]{1,0:T(8,128)(2,1)S(1)} %pad_maximum_fusion.3), channel_id=1, source_target_pairs={{0,12},{1,13},{2,14},{3,15},{4,0},{5,1},{6,2},{7,3},{8,4},{9,5},{1... | collective-permute-start | bytes 1572872 | tf_op jit(solution)/shard_map/ppermute | solution.py:29
  70.6 20.9 %collective-permute-start.6 = (bf16[5,512,128]{2,1,0:T(8,128)(2,1)}, bf16[5,512,128]{2,1,0:T(8,128)(2,1)S(1)}, u32[]{:S(2)}, u32[]{:S(2)}) collective-permute-start(bf16[5,512,128]{2,1,0:T(8,128)(2,1)} %copy-done.5), channel_id=1, source_target_pairs={{0,96},{1,97},{2,98},{3,99},{4,100},{5,101},{6,102},{7,103},{8,104... | collective-permute-start | bytes 1966088 | tf_op jit(solution)/shard_map/ppermute | solution.py:29
  81.9 14.2 %collective-permute-start.8 = (bf16[5,512,128]{2,1,0:T(8,128)(2,1)}, bf16[5,512,128]{2,1,0:T(8,128)(2,1)}, u32[]{:S(2)}, u32[]{:S(2)}) collective-permute-start(bf16[5,512,128]{2,1,0:T(8,128)(2,1)} %copy-done.5), channel_id=1, source_target_pairs={{0,32},{1,33},{2,34},{3,35},{4,36},{5,37},{6,38},{7,39},{8,40},{9,... | collective-permute-start | bytes 1966088 | tf_op jit(solution)/shard_map/ppermute | solution.py:29
  96.1 20.7 %collective-permute-start.13 = (bf16[4,512,512]{2,1,0:T(8,128)(2,1)}, bf16[4,512,512]{2,1,0:T(8,128)(2,1)}, u32[]{:S(2)}, u32[]{:S(2)}) collective-permute-start(bf16[4,512,512]{2,1,0:T(8,128)(2,1)} %pad_maximum_fusion.near.refs_0_.refs_3_.refs_6_), channel_id=1, source_target_pairs={{0,1},{1,0},{2,3},{3,2},{4,5},{5,4},{6,7},{7,6},{8,9},{9,8},{10,11... | collective-permute-start | bytes 6291464 | tf_op jit(solution)/shard_map/ppermute | solution.py:29
  100.7 25.1 %collective-permute-start.16 = (bf16[6,512,128]{2,1,0:T(8,128)(2,1)S(1)}, bf16[6,512,128]{2,1,0:T(8,128)(2,1)}, u32[]{:S(2)}, u32[]{:S(2)}) collective-permute-start(bf16[6,512,128]{2,1,0:T(8,128)(2,1)S(1)} %collective-permute-done.5.refs_14_), channel_id=1, source_target_pairs={{0,96},{1,97},{2,98},{3,99},{4,100},{5,101},{6,102},{7,103},{8,104... | collective-permute-start | bytes 2359304 | tf_op jit(solution)/shard_map/ppermute | solution.py:29
  100.7 25.1 %collective-permute-start.17 = (bf16[5,512,128]{2,1,0:T(8,128)(2,1)}, bf16[5,512,128]{2,1,0:T(8,128)(2,1)}, u32[]{:S(2)}, u32[]{:S(2)}) collective-permute-start(bf16[5,512,128]{2,1,0:T(8,128)(2,1)} %collective-permute-done.8.refs_17_), channel_id=1, source_target_pairs={{0,32},{1,33},{2,34},{3,35},{4,36},{5,37},{6,38},{7,39},{8,40},{9,... | collective-permute-start | bytes 1966088 | tf_op jit(solution)/shard_map/ppermute | solution.py:29
  111.1 20.1 %collective-permute-start.18 = (bf16[512,512]{1,0:T(8,128)(2,1)S(1)}, bf16[512,512]{1,0:T(8,128)(2,1)S(1)}, u32[]{:S(2)}, u32[]{:S(2)}) collective-permute-start(bf16[512,512]{1,0:T(8,128)(2,1)S(1)} %copy-done.6), channel_id=1, source_target_pairs={{0,96},{1,97},{2,98},{3,99},{4,100},{5,101},{6,102},{7,103},{8,104... | collective-permute-start | bytes 1572872 | tf_op jit(solution)/shard_map/ppermute | solution.py:29
  113.8 17.4 %collective-permute-start.19 = (bf16[512,512]{1,0:T(8,128)(2,1)S(1)}, bf16[512,512]{1,0:T(8,128)(2,1)S(1)}, u32[]{:S(2)}, u32[]{:S(2)}) collective-permute-start(bf16[512,512]{1,0:T(8,128)(2,1)S(1)} %copy-done.7), channel_id=1, source_target_pairs={{0,32},{1,33},{2,34},{3,35},{4,36},{5,37},{6,38},{7,39},{8,40},{9,... | collective-permute-start | bytes 1572872 | tf_op jit(solution)/shard_map/ppermute | solution.py:29
  131.2 28.7 %all-to-all-start.1 = ((f32[32,16,640]{2,1,0:T(8,128)}), f32[32,16,640]{2,1,0:T(8,128)}, u32[]{:S(2)}, u32[]{:S(2)}) async-start(f32[32,16,640]{2,1,0:T(8,128)} %bitcast.69), calls=%async_computation.1 | async-start | bytes 2621440 | tf_op jit(solution)/shard_map/all_to_all | solution.py:507
  139.9 34.5 %collective-permute-start.20 = (bf16[512,512]{1,0:T(8,128)(2,1)S(1)}, bf16[512,512]{1,0:T(8,128)(2,1)S(1)}, u32[]{:S(2)}, u32[]{:S(2)}) collective-permute-start(bf16[512,512]{1,0:T(8,128)(2,1)S(1)} %copy-done.7), channel_id=1, source_target_pairs={{0,96},{1,97},{2,98},{3,99},{4,100},{5,101},{6,102},{7,103},{8,104... | collective-permute-start | bytes 1572872 | tf_op jit(solution)/shard_map/ppermute | solution.py:29
  141.2 33.2 %collective-permute-start.23 = (bf16[512,512]{1,0:T(8,128)(2,1)S(1)}, bf16[512,512]{1,0:T(8,128)(2,1)S(1)}, u32[]{:S(2)}, u32[]{:S(2)}) collective-permute-start(bf16[512,512]{1,0:T(8,128)(2,1)S(1)} %copy-done.6), channel_id=1, source_target_pairs={{0,32},{1,33},{2,34},{3,35},{4,36},{5,37},{6,38},{7,39},{8,40},{9,... | collective-permute-start | bytes 1572872 | tf_op jit(solution)/shard_map/ppermute | solution.py:29
  141.5 32.9 %collective-permute-start.21 = (bf16[512,512]{1,0:T(8,128)(2,1)S(1)}, bf16[512,512]{1,0:T(8,128)(2,1)}, u32[]{:S(2)}, u32[]{:S(2)}) collective-permute-start(bf16[512,512]{1,0:T(8,128)(2,1)S(1)} %collective-permute-done.18.refs_2_), channel_id=1, source_target_pairs={{0,96},{1,97},{2,98},{3,99},{4,100},{5,101},{6,102},{7,103},{8,104... | collective-permute-start | bytes 1572872 | tf_op jit(solution)/shard_map/ppermute | solution.py:29
  143.9 30.5 %collective-permute-start.22 = (bf16[512,512]{1,0:T(8,128)(2,1)S(1)}, bf16[512,512]{1,0:T(8,128)(2,1)}, u32[]{:S(2)}, u32[]{:S(2)}) collective-permute-start(bf16[512,512]{1,0:T(8,128)(2,1)S(1)} %collective-permute-done.19.refs_7_), channel_id=1, source_target_pairs={{0,32},{1,33},{2,34},{3,35},{4,36},{5,37},{6,38},{7,39},{8,40},{9,... | collective-permute-start | bytes 1572872 | tf_op jit(solution)/shard_map/ppermute | solution.py:29
  185.2 11.4 %collective-permute-start.33 = (bf16[4,2,16,1024]{3,2,1,0:T(8,128)(2,1)S(1)}, bf16[4,2,16,1024]{3,2,1,0:T(8,128)(2,1)S(1)}, u32[]{:S(2)}, u32[]{:S(2)}) collective-permute-start(bf16[4,2,16,1024]{3,2,1,0:T(8,128)(2,1)S(1)} %get-tuple-element.95), channel_id=1, source_target_pairs={{0,16},{1,17},{2,18},{3,19},{4,20},{5,21},{6,22},{7,23},{8,24},{9,... | collective-permute-start | bytes 786440 | tf_op jit(solution)/shard_map/ppermute | solution.py:29
  186.7 11.6 %collective-permute-start.32 = (bf16[4,2,16,1024]{3,2,1,0:T(8,128)(2,1)S(1)}, bf16[4,2,16,1024]{3,2,1,0:T(8,128)(2,1)S(1)}, u32[]{:S(2)}, u32[]{:S(2)}) collective-permute-start(bf16[4,2,16,1024]{3,2,1,0:T(8,128)(2,1)S(1)} %get-tuple-element.94), channel_id=1, source_target_pairs={{0,2},{1,3},{2,0},{3,1},{4,6},{5,7},{6,4},{7,5},{8,10},{9,11},{10,... | collective-permute-start | bytes 786440 | tf_op jit(solution)/shard_map/ppermute | solution.py:29
  189.1 13.2 %collective-permute-start.28 = (bf16[4,2,16,1024]{3,2,1,0:T(8,128)(2,1)S(1)}, bf16[4,2,16,1024]{3,2,1,0:T(8,128)(2,1)S(1)}, u32[]{:S(2)}, u32[]{:S(2)}) collective-permute-start(bf16[4,2,16,1024]{3,2,1,0:T(8,128)(2,1)S(1)} %get-tuple-element.99), channel_id=1, source_target_pairs={{0,4},{1,5},{2,6},{3,7},{4,8},{5,9},{6,10},{7,11},{8,12},{9,13},{1... | collective-permute-start | bytes 786440 | tf_op jit(solution)/shard_map/ppermute | solution.py:29
  190.5 13.5 %collective-permute-start.27 = (bf16[4,2,16,1024]{3,2,1,0:T(8,128)(2,1)S(1)}, bf16[4,2,16,1024]{3,2,1,0:T(8,128)(2,1)S(1)}, u32[]{:S(2)}, u32[]{:S(2)}) collective-permute-start(bf16[4,2,16,1024]{3,2,1,0:T(8,128)(2,1)S(1)} %get-tuple-element.99), channel_id=1, source_target_pairs={{0,8},{1,9},{2,10},{3,11},{4,12},{5,13},{6,14},{7,15},{8,0},{9,1},... | collective-permute-start | bytes 786440 | tf_op jit(solution)/shard_map/ppermute | solution.py:29
  (30 other events, 310.7 us)
